TPU v7x, 32 devices: a whole 2x2x4 slice. The times are simulated.
32 devices in a mesh: wide: 4 (over y, core), narrow: 8 (over z, x).
Axes of the slice: x: 2, y: 2, z: 4, core: 2. Of those that a mesh axis runs over, the one named last changes fastest.
Arguments:
- variables: bfloat16 [8, 2048, 768], P(None, 'wide'), may hold values from -6 to 6
- valid_slots: int32 [8, 48], replicated, may hold values from 0 to 1, as said below
- out_grad: bfloat16 [8, 2048, 1024], P(None, 'wide'), may hold values from -6 to 6
- patch_embed: bfloat16 [768, 1024], replicated, may hold values from -1.5 to 1.5
- variable_embed: bfloat16 [48, 1024], replicated, may hold values from -6 to 6
- pool_query: float32 [1024], P('narrow'), may hold values from -6 to 6
- pool_key: bfloat16 [1024, 1024], P(None, 'narrow'), may hold values from -0.1875 to 0.1875
- pool_value: bfloat16 [1024, 1024], P(None, 'narrow'), may hold values from -0.1875 to 0.1875
- value_shift: float32 [1024], P('narrow'), may hold values from -1.5 to 1.5
- pool_output: bfloat16 [1024, 1024], P('narrow'), may hold values from -0.1875 to 0.1875
- pool_bias: float32 [1024], replicated, may hold values from -1.5 to 1.5
- first_gain: float32 [1024], replicated, may hold values from 0.3 to 2
- first_shift: float32 [1024], replicated, may hold values from -2 to 2
- self_weights: bfloat16 [1024, 3, 1024], P(None, None, 'narrow'), may hold values from -0.1875 to 0.1875
- query_bias: float32 [1024], P('narrow'), may hold values from -3 to 3
- value_bias: float32 [1024], P('narrow'), may hold values from -0.3 to 0.3
- self_output: bfloat16 [1024, 1024], P('narrow'), may hold values from -0.1875 to 0.1875
- output_bias: float32 [1024], replicated, may hold values from -1.5 to 1.5
- second_gain: float32 [1024], replicated, may hold values from 0.3 to 2
- second_shift: float32 [1024], replicated, may hold values from -2 to 2
- feed_up: bfloat16 [1024, 4096], P(None, 'narrow'), may hold values from -0.1875 to 0.1875
- up_bias: float32 [4096], P('narrow'), may hold values from -3 to 3
- feed_down: bfloat16 [4096, 1024], P('narrow'), may hold values from -0.09375 to 0.09375
- down_bias: float32 [1024], replicated, may hold values from -3 to 3
Outputs:
- block_out: bfloat16 [8, 2048, 1024], P(None, 'wide')
- grad_variables: float32 [8, 2048, 768], P(None, 'wide')
- grad_patch_embed: float32 [768, 1024], replicated
- grad_variable_embed: float32 [48, 1024], replicated
- grad_pool_query: float32 [1024], P('narrow')
- grad_pool_key: float32 [1024, 1024], P(None, 'narrow')
- grad_pool_value: float32 [1024, 1024], P(None, 'narrow')
- grad_value_shift: float32 [1024], P('narrow')
- grad_pool_output: float32 [1024, 1024], P('narrow')
- grad_pool_bias: float32 [1024], replicated
- grad_first_gain: float32 [1024], replicated
- grad_first_shift: float32 [1024], replicated
- grad_self_weights: float32 [1024, 3, 1024], P(None, None, 'narrow')
- grad_query_bias: float32 [1024], P('narrow')
- grad_value_bias: float32 [1024], P('narrow')
- grad_self_output: float32 [1024, 1024], P('narrow')
- grad_output_bias: float32 [1024], replicated
- grad_second_gain: float32 [1024], replicated
- grad_second_shift: float32 [1024], replicated
- grad_feed_up: float32 [1024, 4096], P(None, 'narrow')
- grad_up_bias: float32 [4096], P('narrow')
- grad_feed_down: float32 [4096, 1024], P('narrow')
- grad_down_bias: float32 [1024], replicated
Inputs may be any that keep to these rules, and one draw needn't show every extreme that they name: `valid_slots`: every row holds exactly 30 ones.
All inputs are finite; a program needn't handle non-finite values.
Results may differ from a plain program's by a relative error of at most 0.025.
Values may be sent and summed in bfloat16 or wider, within the bound.
No kernel may reach another device: no remote copies, remote signals or barrier semaphores. Data moves between devices by JAX's collectives and lax.ppermute only.
A program may use at most 576 MiB of HBM per device.

v0:
```python
import jax
import jax.numpy as jnp
from jax import lax
from jax.sharding import PartitionSpec as P

HEAD_DIM = 64
VARS = 48
PIX = 16


highest = lax.Precision.HIGHEST


def layer_norm(stream, norm_gain, norm_shift):
    centered = stream - jnp.mean(stream, -1, keepdims=True)
    variance = jnp.mean(centered * centered, -1, keepdims=True)
    return centered * lax.rsqrt(variance + 1e-05) * norm_gain + norm_shift


def gelu_exact(tensor):
    return jax.nn.gelu(tensor, approximate=False)


def round_low(tensor):
    return tensor.astype(jnp.bfloat16)


def matmul(left, right):
    return jnp.dot(left, right, preferred_element_type=jnp.float32)


def contract_rows(left, right):
    return lax.dot_general(
        left, right, (((0,), (0,)), ((), ())), preferred_element_type=jnp.float32
    )


def contract_cols(left, right):
    return lax.dot_general(
        left, right, (((1,), (1,)), ((), ())), preferred_element_type=jnp.float32
    )


def column_sums(tensor):
    return jnp.sum(tensor, 0, dtype=jnp.float32)


def reduce_to(partial_value):
    return lax.psum(partial_value, "narrow")


def on_device(
    variables,
    valid_slots,
    out_grad,
    patch_embed,
    variable_embed,
    pool_query,
    pool_key,
    pool_value,
    value_shift,
    pool_output,
    pool_bias,
    first_gain,
    first_shift,
    self_weights,
    query_bias,
    value_bias,
    self_output,
    output_bias,
    second_gain,
    second_shift,
    feed_up,
    up_bias,
    feed_down,
    down_bias,
):
    sample_count, token_count, input_width = variables.shape
    row_count = sample_count * token_count
    model_width = patch_embed.shape[1]
    local_dim = pool_query.shape[0]
    head_count = local_dim // HEAD_DIM
    score_scale = HEAD_DIM ** (-0.5)
    embed_table = jnp.concatenate([patch_embed, variable_embed], 0)
    table_wide = embed_table.astype(jnp.float32)
    key_heads = pool_key.astype(jnp.float32).reshape(model_width, head_count, HEAD_DIM)
    query_heads = pool_query.reshape(head_count, HEAD_DIM)
    folded = jnp.einsum("dhe,he->hd", key_heads, query_heads, precision=highest)
    slot_proj = jnp.einsum("rd,hd->rh", table_wide, folded, precision=highest) * score_scale
    patch_terms = slot_proj[:input_width].reshape(VARS, PIX, head_count)
    slot_terms = slot_proj[input_width:]
    pixels = variables.astype(jnp.float32).reshape(row_count, VARS, PIX)
    slot_valid = jnp.repeat(valid_slots, token_count, axis=0)
    scores = jnp.einsum("nvc,vch->nhv", pixels, patch_terms, precision=highest) + slot_terms.T[None]
    scores = jnp.where(slot_valid[:, None, :] > 0, scores, -1e30)
    weights = jnp.exp(scores - jnp.max(scores, -1, keepdims=True))
    weights = weights / jnp.sum(weights, -1, keepdims=True)
    mixed_low = round_low(
        jnp.concatenate(
            [
                (weights[..., None] * pixels[:, None]).reshape(row_count, head_count, input_width),
                weights,
            ],
            -1,
        )
    )
    embedded_low = round_low(
        jnp.einsum("nhr,rd->nhd", mixed_low, embed_table, preferred_element_type=jnp.float32)
    )
    value_heads = pool_value.reshape(model_width, head_count, HEAD_DIM)
    pooled = jnp.einsum(
        "nhd,dhe->nhe", embedded_low, value_heads, preferred_element_type=jnp.float32
    )
    pooled = pooled + value_shift.reshape(head_count, HEAD_DIM)
    pooled_low = round_low(pooled.reshape(row_count, local_dim))
    stream_zero = reduce_to(matmul(pooled_low, pool_output)) + pool_bias
    normed_one = round_low(layer_norm(stream_zero, first_gain, first_shift))
    weights_flat = self_weights.reshape(model_width, 3 * local_dim)
    triple = matmul(normed_one, weights_flat).reshape(row_count, 3, local_dim)
    query_low = round_low(triple[:, 0] + query_bias)
    pair_low = jnp.concatenate([round_low(triple[:, 1]), round_low(triple[:, 2] + value_bias)], -1)
    pair_local = pair_low.reshape(sample_count, token_count, 2 * local_dim)
    pair_all = lax.all_gather(pair_local, "wide", axis=1, tiled=True)
    length = pair_all.shape[1]
    query_view = query_low.reshape(sample_count, token_count, head_count, HEAD_DIM)
    key_view = pair_all[..., :local_dim].reshape(sample_count, length, head_count, HEAD_DIM)
    value_view = pair_all[..., local_dim:].reshape(sample_count, length, head_count, HEAD_DIM)
    logits = (
        jnp.einsum("bqhe,bkhe->bhqk", query_view, key_view, preferred_element_type=jnp.float32)
        * score_scale
    )
    row_peak = jnp.max(logits, -1, keepdims=True)
    log_total = row_peak + jnp.log(jnp.sum(jnp.exp(logits - row_peak), -1, keepdims=True))
    probs_low = round_low(jnp.exp(logits - log_total))
    attended = jnp.einsum(
        "bhqk,bkhe->bqhe", probs_low, value_view, preferred_element_type=jnp.float32
    )
    attended_low = round_low(attended.reshape(row_count, local_dim))
    stream_one = stream_zero + reduce_to(matmul(attended_low, self_output)) + output_bias
    normed_two = round_low(layer_norm(stream_one, second_gain, second_shift))
    hidden_pre = matmul(normed_two, feed_up) + up_bias
    active_low = round_low(gelu_exact(hidden_pre))
    stream_out = stream_one + reduce_to(matmul(active_low, feed_down)) + down_bias
    block_out = round_low(stream_out).reshape(sample_count, token_count, model_width)
    grad_rows = out_grad.reshape(row_count, model_width)
    grad_feed_down = contract_rows(active_low, grad_rows)
    grad_active = contract_cols(grad_rows, feed_down)
    unused_out, gelu_back = jax.vjp(gelu_exact, hidden_pre)
    grad_hidden_low = round_low(gelu_back(grad_active)[0])
    grad_up_bias = column_sums(grad_hidden_low)
    grad_feed_up = contract_rows(normed_two, grad_hidden_low)
    grad_normed_two = reduce_to(contract_cols(grad_hidden_low, feed_up))
    unused_two, norm_back_two = jax.vjp(layer_norm, stream_one, second_gain, second_shift)
    grad_through_two, grad_second_gain, grad_second_shift = norm_back_two(grad_normed_two)
    grad_down_bias = column_sums(grad_rows)
    grad_stream_one = grad_rows.astype(jnp.float32) + grad_through_two
    grad_one_low = round_low(grad_stream_one)
    grad_output_bias = column_sums(grad_one_low)
    grad_self_output = contract_rows(attended_low, grad_one_low)
    grad_attended_low = round_low(contract_cols(grad_one_low, self_output)).reshape(
        sample_count, token_count, head_count, HEAD_DIM
    )
    key_back = pair_all[..., :local_dim].reshape(sample_count, length, head_count, HEAD_DIM)
    value_back = pair_all[..., local_dim:].reshape(sample_count, length, head_count, HEAD_DIM)
    logits_back = (
        jnp.einsum("bqhe,bkhe->bhqk", query_view, key_back, preferred_element_type=jnp.float32)
        * score_scale
    )
    probs_exact = jnp.exp(logits_back - log_total)
    probs_again = round_low(probs_exact)
    grad_probs = jnp.einsum(
        "bqhe,bkhe->bhqk", grad_attended_low, value_back, preferred_element_type=jnp.float32
    )
    grad_logits_low = round_low(
        probs_exact * (grad_probs - jnp.sum(probs_exact * grad_probs, -1, keepdims=True))
    )
    grad_query = (
        jnp.einsum("bhqk,bkhe->bqhe", grad_logits_low, key_back, preferred_element_type=jnp.float32)
        * score_scale
    )
    grad_keys = (
        jnp.einsum(
            "bhqk,bqhe->bkhe", grad_logits_low, query_view, preferred_element_type=jnp.float32
        )
        * score_scale
    )
    grad_values = jnp.einsum(
        "bhqk,bqhe->bkhe", probs_again, grad_attended_low, preferred_element_type=jnp.float32
    )
    grad_pair = jnp.concatenate(
        [
            grad_keys.reshape(sample_count, length, local_dim),
            grad_values.reshape(sample_count, length, local_dim),
        ],
        -1,
    )
    grad_pair_low = round_low(
        lax.psum_scatter(grad_pair, "wide", scatter_dimension=1, tiled=True)
    ).reshape(row_count, 2 * local_dim)
    grad_query_low = round_low(grad_query.reshape(row_count, local_dim))
    grad_triple = jnp.concatenate([grad_query_low, grad_pair_low], -1)
    grad_query_bias = column_sums(grad_query_low)
    grad_value_bias = column_sums(grad_pair_low[:, local_dim:])
    grad_self_weights = contract_rows(normed_one, grad_triple).reshape(model_width, 3, local_dim)
    grad_normed_one = reduce_to(contract_cols(grad_triple, weights_flat))
    unused_one, norm_back_one = jax.vjp(layer_norm, stream_zero, first_gain, first_shift)
    grad_through_one, grad_first_gain, grad_first_shift = norm_back_one(grad_normed_one)
    grad_stream_zero = grad_stream_one + grad_through_one
    grad_zero_low = round_low(grad_stream_zero)
    grad_pool_bias = column_sums(grad_zero_low)
    grad_pool_output = contract_rows(pooled_low, grad_zero_low)
    grad_pooled_low = round_low(contract_cols(grad_zero_low, pool_output)).reshape(
        row_count, head_count, HEAD_DIM
    )
    grad_value_shift = column_sums(grad_pooled_low).reshape(local_dim)
    grad_pool_value = jnp.einsum(
        "nhd,nhe->dhe", embedded_low, grad_pooled_low, preferred_element_type=jnp.float32
    ).reshape(model_width, local_dim)
    grad_embedded_low = round_low(
        jnp.einsum("nhe,dhe->nhd", grad_pooled_low, value_heads, preferred_element_type=jnp.float32)
    )
    grad_table = jnp.einsum(
        "nhr,nhd->rd", mixed_low, grad_embedded_low, preferred_element_type=jnp.float32
    )
    grad_mixed = jnp.einsum(
        "nhd,rd->nhr", grad_embedded_low, embed_table, preferred_element_type=jnp.float32
    )
    grad_pixel_mixed = grad_mixed[..., :input_width].reshape(row_count, head_count, VARS, PIX)
    grad_weights = jnp.sum(grad_pixel_mixed * pixels[:, None], -1) + grad_mixed[..., input_width:]
    grad_scores = weights * (grad_weights - jnp.sum(weights * grad_weights, -1, keepdims=True))
    grad_pixels = jnp.sum(weights[..., None] * grad_pixel_mixed, 1)
    grad_pixels = grad_pixels + jnp.einsum(
        "nhv,vch->nvc", grad_scores, patch_terms, precision=highest
    )
    grad_variables = lax.psum(grad_pixels.reshape(row_count, input_width), "narrow")
    grad_variables = grad_variables.reshape(sample_count, token_count, input_width)
    grad_patch_terms = jnp.einsum("nhv,nvc->vch", grad_scores, pixels, precision=highest)
    grad_slot_terms = jnp.sum(grad_scores, 0).T
    grad_proj = (
        jnp.concatenate([grad_patch_terms.reshape(input_width, head_count), grad_slot_terms], 0)
        * score_scale
    )
    grad_table = grad_table + jnp.einsum("rh,hd->rd", grad_proj, folded, precision=highest)
    grad_folded = jnp.einsum("rh,rd->hd", grad_proj, table_wide, precision=highest)
    grad_pool_key = jnp.einsum("hd,he->dhe", grad_folded, query_heads, precision=highest).reshape(
        model_width, local_dim
    )
    grad_pool_query = jnp.einsum("dhe,hd->he", key_heads, grad_folded, precision=highest).reshape(
        local_dim
    )
    (
        grad_pool_query,
        grad_pool_key,
        grad_pool_value,
        grad_value_shift,
        grad_pool_output,
        grad_self_weights,
        grad_query_bias,
        grad_value_bias,
        grad_self_output,
        grad_feed_up,
        grad_up_bias,
        grad_feed_down,
    ) = lax.psum(
        (
            grad_pool_query,
            grad_pool_key,
            grad_pool_value,
            grad_value_shift,
            grad_pool_output,
            grad_self_weights,
            grad_query_bias,
            grad_value_bias,
            grad_self_output,
            grad_feed_up,
            grad_up_bias,
            grad_feed_down,
        ),
        "wide",
    )
    (
        grad_pool_bias,
        grad_first_gain,
        grad_first_shift,
        grad_output_bias,
        grad_second_gain,
        grad_second_shift,
        grad_down_bias,
    ) = lax.psum(
        (
            grad_pool_bias,
            grad_first_gain,
            grad_first_shift,
            grad_output_bias,
            grad_second_gain,
            grad_second_shift,
            grad_down_bias,
        ),
        "wide",
    )
    grad_table = lax.psum(grad_table, ("wide", "narrow"))
    return (
        block_out,
        grad_variables,
        grad_table[:input_width],
        grad_table[input_width:],
        grad_pool_query,
        grad_pool_key,
        grad_pool_value,
        grad_value_shift,
        grad_pool_output,
        grad_pool_bias,
        grad_first_gain,
        grad_first_shift,
        grad_self_weights,
        grad_query_bias,
        grad_value_bias,
        grad_self_output,
        grad_output_bias,
        grad_second_gain,
        grad_second_shift,
        grad_feed_up,
        grad_up_bias,
        grad_feed_down,
        grad_down_bias,
    )


def solution(mesh):
    return jax.shard_map(
        on_device,
        mesh=mesh,
        in_specs=(
            P(None, "wide", None),
            P(),
            P(None, "wide", None),
            P(),
            P(),
            P("narrow"),
            P(None, "narrow"),
            P(None, "narrow"),
            P("narrow"),
            P("narrow", None),
            P(),
            P(),
            P(),
            P(None, None, "narrow"),
            P("narrow"),
            P("narrow"),
            P("narrow", None),
            P(),
            P(),
            P(),
            P(None, "narrow"),
            P("narrow"),
            P("narrow", None),
            P(),
        ),
        out_specs=(
            P(None, "wide", None),
            P(None, "wide", None),
            P(),
            P(),
            P("narrow"),
            P(None, "narrow"),
            P(None, "narrow"),
            P("narrow"),
            P("narrow", None),
            P(),
            P(),
            P(),
            P(None, None, "narrow"),
            P("narrow"),
            P("narrow"),
            P("narrow", None),
            P(),
            P(),
            P(),
            P(None, "narrow"),
            P("narrow"),
            P("narrow", None),
            P(),
        ),
        check_vma=False,
    )
```

profile of v0, /device:TPU:0, one launch (start us, length us, event | category | flops | bytes accessed | tf_op | source)
XLA Modules:
  0.0 4139.1 jit_solution(18351796046438727141)
XLA Ops:
  81.2 24.2 convolution_convert_fusion
  125.1 511.0 %all-reduce.11.cloned.1.call-done = f32[4096,1024]{1,0:T(8,128)} async-done(((f32[4096,1024]{1,0:T(8,128)}), f32[4096,1024]{1,0:T(8,128)}) %all-reduce.11.cloned.1.call-update) | async-done | bytes 16777232 | tf_op jit(solution)/shard_map/psum | solution.py:49
  669.4 53.2 %all-gather.2.cloned.1.call-done = bf16[8,2048,256]{2,1,0:T(8,128)(2,1)} async-done(((bf16[8,512,256]{2,1,0:T(8,128)(2,1)}), bf16[8,2048,256]{2,1,0:T(8,128)(2,1)}) %all-gather.2.cloned.1.call-update) | async-done | bytes 8388624 | tf_op jit(solution)/shard_map/all_gather | solution.py:123
  741.6 25.6 multiply_reduce_fusion.1
  767.2 21.3 exponential_reduce_fusion
  788.5 25.0 fusion.32
  823.7 509.6 %all-reduce.13.cloned.1.call-done = f32[4096,1024]{1,0:T(8,128)} async-done(((f32[4096,1024]{1,0:T(8,128)}), f32[4096,1024]{1,0:T(8,128)}) %all-reduce.13.cloned.1.call-update) | async-done | bytes 16777232 | tf_op jit(solution)/shard_map/psum | solution.py:49
  1359.2 25.4 convert_reduce_fusion.3
  1395.1 508.7 %all-reduce.15.cloned.1.call-done = f32[4096,1024]{1,0:T(8,128)} async-done(((f32[4096,1024]{1,0:T(8,128)}), f32[4096,1024]{1,0:T(8,128)}) %all-reduce.15.cloned.1.call-update) | async-done | bytes 16777232 | tf_op jit(solution)/shard_map/psum | solution.py:49
  1950.0 47.7 %multiply_reduce_fusion = (f32[8,2,512]{2,1,0:T(2,128)S(1)}, f32[8,2,512,2048]{3,2,1,0:T(8,128)}) fusion(f32[8,2,512,2048]{3,2,1,0:T(8,128)} %get-tuple-element.122, f32[8,2,512]{2,1,0:T(2,128)S(1)} %bitcast.217, bf16[8,512,2,64]{1,3,2,0:T(8,128)(2,1)S(1)} %copy.117, bf16[8,2048,2,64]{1,3,2,0:T(8,128)(2,1)} %bitcast.185), kind=kOutput, calls=%fused_computation.1 | convolution fusion | flops 2214584320 | bytes 139526144 | tf_op jit(solution)/shard_map/bqhe,bkhe->bhqk/dot_general | solution.py:171
  1997.7 27.4 fusion.16
  2025.1 53.4 %multiply_convert_fusion = bf16[8,2,512,2048]{3,2,1,0:T(8,128)(2,1)} fusion(f32[8,2,512,2048]{3,2,1,0:T(8,128)} %get-tuple-element.124, f32[8,2,512,2048]{3,2,1,0:T(8,128)} %get-tuple-element.122, f32[8,2,512]{2,1,0:T(2,128)S(1)} %get-tuple-element.123, f32[8,2,512]{2,1,0:T(2,128)S(1)} %bitcast.219), kind=kLoop, calls=%fused_computation | loop fusion | flops 83886080 | bytes 167837696 | tf_op jit(solution)/shard_map/convert_element_type | solution.py:25
  2078.5 20.0 broadcast_multiply_fusion
  2128.2 23.2 convert_reduce_fusion.5
  2157.7 95.9 %reduce-scatter.2.cloned.1.call-done = f32[8,512,256]{2,1,0:T(8,128)} async-done(((f32[8,2048,256]{2,1,0:T(8,128)}), f32[8,512,256]{2,1,0:T(8,128)}) %reduce-scatter.2.cloned.1.call-update) | async-done | bytes 4194320 | tf_op jit(solution)/shard_map/reduce_scatter | solution.py:198
  2333.3 444.9 %all-reduce.17.cloned.1.call-done = f32[4096,1024]{1,0:T(8,128)} async-done(((f32[4096,1024]{1,0:T(8,128)}), f32[4096,1024]{1,0:T(8,128)}) %all-reduce.17.cloned.1.call-update) | async-done | bytes 16777232 | tf_op jit(solution)/shard_map/psum | solution.py:49
  2791.3 17.9 fusion.66
  2841.0 22.9 fusion.5
  2863.9 24.6 fusion.71
  2922.8 23.0 bitcast_add_fusion.1
  2992.6 21.8 copy.146
  3045.0 38.2 all-reduce.19.cloned.1.call-done
  3088.8 145.1 %all-reduce.23.cloned.1.call-done = (f32[1024,128]{0,1:T(8,128)}, f32[1024,128]{1,0:T(8,128)}, f32[128,1024]{1,0:T(8,128)}, f32[1024,3,128]{2,0,1:T(8,128)}, f32...) async-done(((f32[1024,128]{0,1:T(8,128)}, f32[1024,128]{1,0:T(8,128)}, f32[128,1024]{1,0:T(8,128)}, f32[1024,3,128]{2,0,1:T(8,128)}, ...) | async-done | bytes 7864336 | tf_op jit(solution)/shard_map/psum | solution.py:264
  3236.0 864.6 %all-reduce.21.cloned.1.call-done = (f32[4096,1024]{1,0:T(8,128)}, f32[8,512,768]{2,1,0:T(8,128)}) async-done(((f32[4096,1024]{1,0:T(8,128)}, f32[8,512,768]{2,1,0:T(8,128)}), (f32[4096,1024]{1,0:T(8,128)}, f32[8,512,768]{2,1,0:T(8,128)})) %all-reduce.21.cloned.1.call-update) | async-done | bytes 29360144 | tf_op jit(solution)/shard_map/psum | solution.py:49
  (334 shorter events, 549.2 us)
Async XLA Ops:
  7.2 1351.3 %copy-start = (bf16[512,1024]{1,0:T(8,128)(2,1)S(1)}, bf16[512,1024]{1,0:T(8,128)(2,1)}, u32[]{:S(2)}) copy-start(bf16[512,1024]{1,0:T(8,128)(2,1)} %param.46) | copy-start | bytes 3145732
  7.2 628.8 %all-reduce.11.cloned.1.call-start = ((), (), s32[]{:S(2)}) async-start(), calls=%async_computation.1 | async-start | bytes 33554432 | tf_op jit(solution)/shard_map/psum | solution.py:49
  11.6 69.5 %copy-start.10 = (bf16[816,1024]{1,0:T(8,128)(2,1)}, bf16[816,1024]{1,0:T(8,128)(2,1)S(1)}, u32[]{:S(2)}) copy-start(bf16[816,1024]{1,0:T(8,128)(2,1)S(1)} %constant_dynamic-update-slice_fusion) | copy-start | bytes 5013508
  69.6 35.8 copy-start.23
  123.6 512.4 %copy-start.52 = (f32[1024]{0:T(1024)S(1)}, f32[1024]{0:T(1024)}, u32[]{:S(2)}) copy-start(f32[1024]{0:T(1024)} %param.34) | copy-start | bytes 12292
  123.7 599.0 %all-gather.2.cloned.1.call-start = ((), (), s32[]{:S(2)}) async-start(), calls=%async_computation.2 | async-start | bytes 10485760 | tf_op jit(solution)/shard_map/all_gather | solution.py:123
  125.0 532.0 %copy-start.22 = (bf16[1024,3,128]{0,2,1:T(8,128)(2,1)}, bf16[1024,3,128]{0,2,1:T(8,128)(2,1)S(1)}, u32[]{:S(2)}) copy-start(bf16[1024,3,128]{0,2,1:T(8,128)(2,1)S(1)} %copy.110) | copy-start | bytes 2359300
  665.1 668.3 %all-reduce.13.cloned.1.call-start = ((), (), s32[]{:S(2)}) async-start(), calls=%async_computation.3 | async-start | bytes 33554432 | tf_op jit(solution)/shard_map/psum | solution.py:49
  669.4 72.2 %copy-start.16 = (bf16[8,512,2,64]{1,0,3,2:T(8,128)(2,1)}, bf16[8,512,2,64]{1,0,3,2:T(8,128)(2,1)S(1)}, u32[]{:S(2)}) copy-start(bf16[8,512,2,64]{1,0,3,2:T(8,128)(2,1)S(1)} %add_convert_fusion.5) | copy-start | bytes 3145732
  823.7 509.7 %copy-start.66 = (f32[1024]{0:T(1024)S(1)}, f32[1024]{0:T(1024)}, u32[]{:S(2)}) copy-start(f32[1024]{0:T(1024)} %param.41) | copy-start | bytes 12292
  823.7 1080.1 %all-reduce.15.cloned.1.call-start = ((), (), s32[]{:S(2)}) async-start(), calls=%async_computation.4 | async-start | bytes 33554432 | tf_op jit(solution)/shard_map/psum | solution.py:49
  1395.0 858.5 %reduce-scatter.2.cloned.1.call-start = ((), (), s32[]{:S(2)}) async-start(), calls=%async_computation.5 | async-start | bytes 20971520 | tf_op jit(solution)/shard_map/reduce_scatter | solution.py:198
  2025.1 53.5 %copy-start.17 = (bf16[8,512,2,64]{1,0,3,2:T(8,128)(2,1)S(1)}, bf16[8,512,2,64]{1,0,3,2:T(8,128)(2,1)}, u32[]{:S(2)}) copy-start(bf16[8,512,2,64]{1,0,3,2:T(8,128)(2,1)} %copy-done.16) | copy-start | bytes 3145732
  2128.1 650.1 %all-reduce.17.cloned.1.call-start = ((), (), s32[]{:S(2)}) async-start(), calls=%async_computation.6 | async-start | bytes 33554432 | tf_op jit(solution)/shard_map/psum | solution.py:49
  2256.0 69.5 %copy-start.14 = (bf16[8,512,256]{2,1,0:T(8,128)(2,1)}, bf16[8,512,256]{2,1,0:T(8,128)(2,1)S(1)}, u32[]{:S(2)}) copy-start(bf16[8,512,256]{2,1,0:T(8,128)(2,1)S(1)} %convert_element_type.146) | copy-start | bytes 6291460
  2268.5 814.7 %all-reduce.19.cloned.1.call-start = ((), (), s32[]{:S(2)}) async-start(), calls=%async_computation.7 | async-start | bytes 6684672 | tf_op jit(solution)/shard_map/psum | solution.py:301
  2325.6 452.6 %copy-start.41 = (f32[4096]{0:T(1024)S(1)}, f32[4096]{0:T(1024)}, u32[]{:S(2)}) copy-start(f32[4096]{0:T(1024)} %copy-done.40) | copy-start | bytes 49156
  2325.6 452.6 %copy-start.47 = (f32[4096]{0:T(1024)S(1)}, f32[4096]{0:T(1024)}, u32[]{:S(2)}) copy-start(f32[4096]{0:T(1024)} %copy-done.46) | copy-start | bytes 49156
  2325.6 452.6 %copy-start.53 = (f32[1024]{0:T(1024)S(1)}, f32[1024]{0:T(1024)}, u32[]{:S(2)}) copy-start(f32[1024]{0:T(1024)} %param.34) | copy-start | bytes 12292
  2325.6 452.6 %copy-start.58 = (f32[1024]{0:T(1024)S(1)}, f32[1024]{0:T(1024)}, u32[]{:S(2)}) copy-start(f32[1024]{0:T(1024)} %param.35) | copy-start | bytes 12292
  2333.3 458.0 %copy-start.51 = (f32[4096]{0:T(1024)S(1)}, f32[4096]{0:T(1024)}, u32[]{:S(2)}) copy-start(f32[4096]{0:T(1024)} %copy-done.50) | copy-start | bytes 49156
  2945.9 288.1 %all-reduce.23.cloned.1.call-start = ((), (), s32[]{:S(2)}) async-start(), calls=%async_computation.9 | async-start | bytes 15728640 | tf_op jit(solution)/shard_map/psum | solution.py:264
  2966.8 1133.8 %all-reduce.21.cloned.1.call-start = ((), (), s32[]{:S(2)}) async-start(), calls=%async_computation.8 | async-start | bytes 58720256 | tf_op jit(solution)/shard_map/psum | solution.py:49
  3027.2 1073.4 %copy-start.69 = (f32[1024]{0:T(1024)S(1)}, f32[1024]{0:T(1024)}, u32[]{:S(2)}) copy-start(f32[1024]{0:T(1024)} %param.47) | copy-start | bytes 12292
  (80 other events, 820.8 us)
Sparse Core Ops, SparseCore 0:
  123.8 512.2 all-reduce.10
  665.2 57.3 all-gather.1
  823.8 509.5 all-reduce.12
  1395.2 508.5 all-reduce.14
  2128.2 125.3 reduce-scatter.1
  2268.6 509.5 all-reduce.16
  2946.0 137.2 all-reduce.18
  3088.1 145.8 all-reduce.22
  3239.6 860.9 all-reduce.20
where the time goes:
time: 4150 us; the launch traced here: 4140 us
  waiting for transfers between devices  3170 us (76%)
  matrix products  430 us (10%)
  other arithmetic  302 us (7%)
  local copies, waits for them, and re-layouts  207 us (5%)
    psum x5, waiting for transfers between devices, reduce_to(): return lax.psum(partial_value, 'narrow')  2840 us
    psum x1, waiting for transfers between devices, on_device(): lax.psum((grad_pool_query, grad_pool_key, grad_pool_value, grad_value_shi...  145 us
    reduce_scatter x1, waiting for transfers between devices, on_device(): lax.psum_scatter(grad_pair, 'wide', scatter_dimension=1, tiled=True)  95.9 us
    convert_element_type x8, other arithmetic, round_low(): return tensor.astype(jnp.bfloat16)  87.7 us
  transfers between devices with their start and end apart: 9, of which 9 were waited for; matrix products, arithmetic and copies ran while one was open for 5% of the time, Pallas kernels for 0%

commit v1 on v0

v1 whole, which is shorter than its diff:
```python
import jax
import jax.numpy as jnp
from jax import lax
from jax.experimental import pallas as pl
from jax.experimental.pallas import tpu as pltpu
from jax.sharding import PartitionSpec as P

HEAD_DIM = 64
VARS = 48
PIX = 16
SCALE = HEAD_DIM ** (-0.5)
VMEM_BYTES = 56 * 1024 * 1024

highest = lax.Precision.HIGHEST
AXES = ("wide", "narrow")
F32 = jnp.float32
BF16 = jnp.bfloat16


def low(tensor):
    return tensor.astype(BF16)


def dot(left, right, dims=((1,), (0,)), precision=None):
    return lax.dot_general(
        left, right, (dims, ((), ())), precision=precision, preferred_element_type=F32
    )


NT = ((1,), (1,))
TN = ((0,), (0,))


def params(bytes_limit=VMEM_BYTES):
    return pltpu.CompilerParams(vmem_limit_bytes=bytes_limit)


def struct(shape, dtype):
    return jax.ShapeDtypeStruct(shape, dtype)


def tie(tensor, *others):
    return lax.optimization_barrier((tensor,) + others)[0]


def fixed(shape, *start):
    start = start or (0,) * len(shape)
    return pl.BlockSpec(shape, lambda *_: start)


def per_block(shape, offset=0, *rest):
    rest = rest or (0,) * len(shape)
    return pl.BlockSpec((1,) + shape, lambda n: (n + offset,) + rest)


def cost(flops, bytes_accessed):
    return pl.CostEstimate(flops=flops, bytes_accessed=bytes_accessed, transcendentals=0)


class Ring:
    def __init__(self, wide_size, narrow_size):
        self.wide, self.narrow = wide_size, narrow_size
        self.order = list(range(0, narrow_size, 2)) + list(range(1, narrow_size, 2))[::-1]
        place = {device: index for index, device in enumerate(self.order)}
        self.w = lax.axis_index("wide")
        self.n = lax.axis_index("narrow")
        self.core = self.w % 2
        self.pos = jnp.where(self.n % 2 == 0, self.n // 2, narrow_size - 1 - self.n // 2)

        def step(device, hops):
            return self.order[(place[device] + hops) % narrow_size]

        every = [(w, n) for w in range(wide_size) for n in range(narrow_size)]
        flat = lambda w, n: w * narrow_size + n
        bits = lambda size: [1 << i for i in range(size.bit_length() - 1)]
        self.forward = [(flat(w, n), flat(w, step(n, 1))) for w, n in every]
        self.backward = [(flat(w, n), flat(w, step(n, -1))) for w, n in every]
        self.by_core = [(flat(w, n), flat(w, step(n, 1 - 2 * (w % 2)))) for w, n in every]
        self.by_core_back = [(dst, src) for src, dst in self.by_core]
        self.wide_swap = {
            bit: [(flat(w, n), flat(w ^ bit, n)) for w, n in every] for bit in bits(wide_size)
        }
        self.narrow_swap = {
            bit: [(flat(w, n), flat(w, n ^ bit)) for w, n in every] for bit in bits(narrow_size)
        }

    def move(self, tensor, pairs):
        return lax.ppermute(tensor, AXES, pairs)

    def swap(self, tensor, bit=1):
        return self.move(tensor, self.wide_swap[bit])

    def at(self, hops):
        index = (self.pos + hops + self.narrow) % self.narrow
        return jnp.where(2 * index < self.narrow, 2 * index, 2 * (self.narrow - 1 - index) + 1)

    def first(self, hops):
        return self.at(jnp.where(self.core == 0, -hops, hops))

    def second(self, hops):
        return self.at(jnp.where(self.core == 0, hops, -hops))

    def add_everywhere(self, tensor):
        for pairs in list(self.wide_swap.values()) + list(self.narrow_swap.values()):
            tensor = tensor + self.move(tensor, pairs)
        return tensor

    def gather_wide(self, block):
        pieces = {0: block}
        for bit in self.wide_swap:
            for shift in list(pieces):
                pieces[shift | bit] = self.swap(pieces[shift], bit)
        return [pieces[shift] for shift in range(self.wide)]

    def finish_shared(self, partial):
        half = partial.shape[0] // 2
        mine = lax.dynamic_slice_in_dim(partial, self.core * half, half, 0)
        theirs = lax.dynamic_slice_in_dim(partial, (1 - self.core) * half, half, 0)
        total = mine.astype(F32) + self.swap(theirs).astype(F32)
        for bit in self.wide_swap:
            if bit > 1:
                total = total + self.swap(low(total), bit).astype(F32)
        total = low(total)
        other = self.swap(total)
        first = jnp.where(self.core == 0, total, other).astype(F32)
        second = jnp.where(self.core == 0, other, total).astype(F32)
        return first, second


def blank(shape, dtype):
    return pl.pallas_call(
        lambda o_ref: None,
        out_shape=struct(shape, dtype),
        out_specs=pl.BlockSpec(memory_space=pl.ANY),
        compiler_params=params(),
        name="blank",
    )()


def put(out, piece, index):
    return lax.dynamic_update_index_in_dim(out, piece, index, 0)


class GatherShared:
    def __init__(self, ring, block):
        self.ring, self.current, self.hops = ring, block, 0
        self.out = put(blank((ring.narrow,) + block.shape, block.dtype), block, ring.n)

    def step(self):
        ring, self.hops = self.ring, self.hops + 1
        self.current = ring.move(self.current, ring.by_core)
        self.out = put(self.out, self.current, ring.first(self.hops))
        if 2 * self.hops < ring.narrow:
            other = ring.swap(self.current)
            self.out = put(self.out, other, ring.second(self.hops))
        return self.current

    def finish(self):
        while 2 * self.hops < self.ring.narrow:
            self.step()
        return self.out


class GatherOwn:
    def __init__(self, ring, block, dtype):
        self.ring, self.hops, self.dtype = ring, 0, dtype
        self.ahead = self.behind = block
        self.out = blank((ring.narrow,) + block.shape, dtype)
        self.out = put(self.out, block.astype(dtype), ring.n)

    def step(self):
        ring, self.hops = self.ring, self.hops + 1
        self.ahead = ring.move(self.ahead, ring.forward)
        self.out = put(self.out, self.ahead.astype(self.dtype), ring.at(-self.hops))
        if 2 * self.hops < ring.narrow:
            self.behind = ring.move(self.behind, ring.backward)
            self.out = put(self.out, self.behind.astype(self.dtype), ring.at(self.hops))
        return self.ahead, self.behind

    def finish(self):
        while 2 * self.hops < self.ring.narrow:
            self.step()
        return self.out


class ScatterShared:
    def __init__(self, ring, blocks):
        self.ring, self.blocks, self.hops = ring, blocks, ring.narrow // 2
        self.current = self.pick(ring.first(self.hops))
        self.others = [self.ring.swap(self.pick(ring.second(h))) for h in range(1, self.hops)]

    def pick(self, index):
        return lax.dynamic_index_in_dim(self.blocks, index, 0, keepdims=False)

    def step(self):
        ring, self.hops = self.ring, self.hops - 1
        moved = ring.move(self.current, ring.by_core_back).astype(F32)
        if self.hops:
            own = self.pick(ring.first(self.hops)).astype(F32)
            self.current = low(moved + own + self.others[self.hops - 1].astype(F32))
        else:
            self.current = low(moved + self.pick(ring.n).astype(F32))
        return self.current

    def finish(self):
        while self.hops:
            self.step()
        return self.current


def split_three(tensor):
    top = low(tensor)
    rest = tensor - top.astype(F32)
    middle = low(rest)
    return top, middle, low(rest - middle.astype(F32))


def join(rows, start, count, step):
    picked = [rows[start + i * step : start + i * step + count].astype(F32) for i in range(3)]
    return picked[0] + (picked[1] + picked[2])


def prepare_kernel(
    heads, key_ref, query_ref, table_ref, value_ref, output_ref, triple_ref, bias_ref, o_ref, p_ref
):
    cols = key_ref.shape[1]
    keys, table = key_ref[...], table_ref[...]
    lane = lax.broadcasted_iota(jnp.int32, (8, cols), 1)
    row = lax.broadcasted_iota(jnp.int32, (8, cols), 0)
    masked = jnp.where(lane // HEAD_DIM == row, query_ref[...], 0.0)
    folded = sum(dot(part, keys, NT) for part in split_three(masked)[::-1])
    folded_parts = split_three(folded)
    terms = sum(dot(part, table, NT) for part in folded_parts[::-1]) * SCALE
    bias = split_three(bias_ref[...])
    rows = [part[:heads].astype(F32) for part in split_three(terms)]
    rows += [part[:heads].astype(F32) for part in folded_parts[:2]]
    rows += [part.astype(F32) for part in bias]
    count = sum(part.shape[0] for part in rows)
    extra = o_ref.shape[0] - cols
    if extra > count:
        rows.append(jnp.zeros((extra - count, o_ref.shape[1]), F32))
    o_ref[:cols] = low(dot(table, value_ref[...]).T)
    o_ref[cols:] = low(jnp.concatenate(rows, 0))
    p_ref[:3] = triple_ref[...]
    p_ref[3] = output_ref[...].astype(F32).T.astype(BF16)


def prepare_call(heads, keys, query, table, values, output, triple, bias):
    depth, cols = keys.shape
    extra = -(-(5 * heads + 3) // 16) * 16
    return pl.pallas_call(
        lambda *refs: prepare_kernel(heads, *refs),
        out_shape=[struct((cols + extra, depth), BF16), struct((4, depth, cols), BF16)],
        compiler_params=params(),
        cost_estimate=cost(4 << 30, 4 << 20),
        name="prepare",
    )(keys, query, table, values, output, triple, bias)


def stage_kernel(up_ref, down_ref, output_ref, value_ref, o_ref):
    flip = lambda ref: ref[...].astype(F32).T.astype(BF16)
    o_ref[...] = jnp.concatenate([up_ref[...], flip(down_ref), flip(output_ref), value_ref[...]], 1)


def stage_call(up, down, output, value):
    lanes = up.shape[1] + down.shape[0] + output.shape[0] + value.shape[1]
    return pl.pallas_call(
        stage_kernel,
        out_shape=struct((up.shape[0], lanes), BF16),
        compiler_params=params(),
        cost_estimate=cost(1 << 28, 4 << 20),
        name="stage",
    )(up, down, output, value)


def arrange_kernel(x_ref, g_ref, x1_ref, xt_ref, gt_ref):
    pixels = x_ref[...]
    x1_ref[...] = jnp.concatenate([pixels, jnp.ones((pixels.shape[0], VARS), BF16)], 1)
    xt_ref[...] = pixels.astype(F32).T.astype(BF16)
    gt_ref[...] = g_ref[...].astype(F32).T.astype(BF16)


def arrange_call(pixels, grads):
    tokens, width = pixels.shape
    return pl.pallas_call(
        arrange_kernel,
        out_shape=[
            struct((tokens, width + VARS), BF16),
            struct((width, tokens), BF16),
            struct((grads.shape[1], tokens), BF16),
        ],
        compiler_params=params(),
        cost_estimate=cost(1 << 28, 4 << 20),
        name="arrange",
    )(pixels, grads)


def slot_mask():
    slot = lax.broadcasted_iota(jnp.int32, (VARS, VARS * PIX + VARS), 0)
    column = lax.broadcasted_iota(jnp.int32, (VARS, VARS * PIX + VARS), 1)
    return slot == jnp.where(column < VARS * PIX, column // PIX, column - VARS * PIX)


def mix(weights, pixels_wide):
    tokens = weights.shape[1]
    spread = weights[:, None, :] * pixels_wide
    return jnp.concatenate([low(spread.reshape(VARS * PIX, tokens)), low(weights)], 0)


def pool_kernel(x_ref, xt_ref, valid_ref, tvt_ref, extra_ref, w_ref, o_ref):
    cols = tvt_ref.shape[1]
    heads = cols // HEAD_DIM
    tokens, width = x_ref.shape
    pixels = x_ref[...]
    pixels_wide = xt_ref[...].astype(F32).reshape(VARS, PIX, tokens)
    valid = valid_ref[...] > 0
    extra = extra_ref[0].astype(F32)
    mask = slot_mask()
    parts = []
    for h in range(heads):
        scores = jnp.zeros((VARS, tokens), F32)
        for part in (2, 1, 0):
            row = extra[part * heads + h : part * heads + h + 1, :width]
            scores = scores + dot(low(jnp.where(mask, row, 0.0)), pixels, NT)
        scores = jnp.where(valid, scores, -1e30)
        weights = jnp.exp(scores - jnp.max(scores, 0, keepdims=True))
        weights = weights / jnp.sum(weights, 0, keepdims=True)
        w_ref[0, h] = weights
        mixed = mix(weights, pixels_wide)
        parts.append(dot(tvt_ref[0, h * HEAD_DIM : (h + 1) * HEAD_DIM, :width], mixed))
    pooled = jnp.concatenate(parts, 0) if heads > 1 else parts[0]
    shift = join(extra, 5 * heads, 1, 1)[:, :cols]
    o_ref[0] = low(pooled.T + shift)


def pool_call(pixels, pixels_t, valid, pack, cols, start, count):
    heads = cols // HEAD_DIM
    tokens, width = pixels.shape
    depth, extra = pack.shape[2], pack.shape[1] - cols
    return pl.pallas_call(
        pool_kernel,
        grid=(count,),
        in_specs=[
            fixed((tokens, width)),
            fixed(pixels_t.shape),
            fixed((VARS, 1)),
            per_block((cols, depth), start),
            per_block((extra, depth), start, cols // extra, 0),
        ],
        out_specs=[per_block((heads, VARS, tokens)), per_block((tokens, cols))],
        out_shape=[
            struct((count, heads, VARS, tokens), F32),
            struct((count, tokens, cols), BF16),
        ],
        compiler_params=params(),
        cost_estimate=cost(count * heads * tokens * 1400000, 4 << 20),
        name="pool",
    )(pixels, pixels_t, valid, pack, pack)


def pool_back_kernel(
    first, last, x_ref, xt_ref, w_ref, tvt_ref, out_ref, extra_ref, p_ref, g_ref, gt_ref, *rest
):
    if not first:
        before_ref, rest = rest[1], rest[2:]
    pack_ref, gx_ref, terms_ref, shift_ref = rest[:4]
    sum_ref = rest[4] if last else gx_ref
    cols = tvt_ref.shape[1]
    heads = cols // HEAD_DIM
    tokens, full = x_ref.shape
    width = VARS * PIX
    pixels = x_ref[...]
    pixels_wide = xt_ref[...].astype(F32).reshape(VARS, PIX, tokens)
    extra = extra_ref[0].astype(F32)
    mask = slot_mask()
    grads = low(dot(g_ref[...], out_ref[0, 0]))
    shift_ref[0] = jnp.sum(grads.astype(F32), 0, keepdims=True)
    lane = lax.broadcasted_iota(jnp.int32, grads.shape, 1)
    table_value = tvt_ref[0, :, :full].astype(F32).T.astype(BF16)
    product = jnp.zeros((full, cols), F32)
    total = jnp.zeros((width, tokens), F32)
    for h in range(heads):
        weights = w_ref[0, h]
        own = jnp.where(lane // HEAD_DIM == h, grads, 0) if heads > 1 else grads
        grad_mixed = dot(table_value, own, NT)
        grad_wide = grad_mixed[:width].reshape(VARS, PIX, tokens)
        grad_weights = jnp.sum(grad_wide * pixels_wide, 1) + grad_mixed[width:]
        inner = jnp.sum(weights * grad_weights, 0, keepdims=True)
        grad_scores = weights * (grad_weights - inner)
        product = product + dot(mix(weights, pixels_wide), own)
        total = total + (weights[:, None, :] * grad_wide).reshape(width, tokens)
        gs_top = low(grad_scores)
        gs_rest = low(grad_scores - gs_top.astype(F32))
        top, middle = [
            low(jnp.where(mask, extra[part * heads + h : part * heads + h + 1, :full], 0.0))[
                :, :width
            ]
            for part in (0, 1)
        ]
        stacked = jnp.concatenate([top, top, middle], 0)
        total = total + dot(stacked, jnp.concatenate([gs_top, gs_rest, gs_top], 0), TN)
        both = dot(jnp.concatenate([gs_top, gs_rest], 0), pixels)
        by_slot = jnp.where(mask, both[:VARS] + both[VARS:], 0.0)
        terms_ref[0, h : h + 1, :] = jnp.sum(by_slot, 0, keepdims=True)
    pack_ref[0, 0] = low(dot(gt_ref[...], p_ref[0]))
    pack_ref[0, 1, :full] = low(product)
    pack_ref[0, 1, full:] = jnp.zeros((pack_ref.shape[2] - full, cols), BF16)
    step = pl.program_id(0)

    @pl.when(step == 0)
    def _():
        if first:
            sum_ref[...] = total
        else:
            sum_ref[...] = before_ref[...] + total

    @pl.when(step > 0)
    def _():
        sum_ref[...] += total

    if last:

        @pl.when(step == pl.num_programs(0) - 1)
        def _():
            gx_ref[...] = low(sum_ref[...].T)


def pool_back_call(
    pixels, pixels_t, weights, pack, mixers, pooled, grads, grads_t, start, before, last
):
    count, heads, _, tokens = weights.shape
    depth = pack.shape[2]
    cols = heads * HEAD_DIM
    extra = pack.shape[1] - cols
    full = pixels.shape[1]
    width = pixels_t.shape[0]
    in_specs = [
        fixed(pixels.shape),
        fixed(pixels_t.shape),
        per_block((heads, VARS, tokens)),
        per_block((cols, depth), start),
        per_block((1, depth, cols), start, 3, 0, 0),
        per_block((extra, depth), start, cols // extra, 0),
        per_block((tokens, cols)),
        fixed(grads.shape),
        fixed(grads_t.shape),
    ]
    operands = [pixels, pixels_t, weights, pack, mixers, pack, pooled, grads, grads_t]
    aliases = {}
    if before:
        in_specs += [pl.BlockSpec(memory_space=pl.ANY), fixed((width, tokens))]
        aliases = {len(operands): 0}
        operands += list(before)
    total = struct((tokens, width), BF16) if last else struct((width, tokens), F32)
    return pl.pallas_call(
        lambda *refs: pool_back_kernel(not before, last, *refs),
        grid=(count,),
        in_specs=in_specs,
        out_specs=[
            per_block((2, depth, cols), start),
            fixed(total.shape),
            per_block((heads, full)),
            per_block((1, cols)),
        ],
        out_shape=[
            struct((pack.shape[0], 2, depth, cols), BF16),
            total,
            struct((count, heads, full), F32),
            struct((count, 1, cols), F32),
        ],
        scratch_shapes=[pltpu.VMEM((width, tokens), F32)] if last else [],
        input_output_aliases=aliases,
        compiler_params=params(),
        cost_estimate=cost(count * heads * tokens * 1700000, 6 << 20),
        name="pool_back",
    )(*operands)


def normalise(stream):
    centered = stream - jnp.mean(stream, -1, keepdims=True)
    scale = lax.rsqrt(jnp.mean(centered * centered, -1, keepdims=True) + 1e-05)
    return centered * scale, scale


def normalise_back(grad, stream, gain):
    hat, scale = normalise(stream)
    through = grad * gain
    inner = through - jnp.mean(through, -1, keepdims=True)
    inner = inner - hat * jnp.mean(through * hat, -1, keepdims=True)
    add = lambda tensor: jnp.sum(tensor, 0, keepdims=True)
    return scale * inner, add(grad * hat), add(grad)


def enter_kernel(p_refs, w_ref, bias_ref, gain_ref, shift_ref, s_ref, x_ref, xt_ref):
    stream = jnp.zeros(s_ref.shape, F32) + bias_ref[...]
    index = 0
    for p_ref in p_refs:
        for i in range(p_ref.shape[0]):
            stream = stream + dot(p_ref[i], w_ref[index, 0], NT)
            index += 1
    s_ref[...] = stream
    hat, _ = normalise(stream)
    rows = hat * gain_ref[...] + shift_ref[...]
    x_ref[...] = low(rows)
    xt_ref[...] = low(rows.T)


def enter_call(pooled, mixers, bias, gain, shift):
    tokens = pooled[0].shape[1]
    blocks, _, depth, cols = mixers.shape
    row = fixed((1, depth))
    count = len(pooled)
    return pl.pallas_call(
        lambda *refs: enter_kernel(refs[:count], *refs[count:]),
        grid=(1,),
        in_specs=[fixed(p.shape) for p in pooled]
        + [fixed((blocks, 1, depth, cols), 0, 3, 0, 0), row, row, row],
        out_specs=[fixed((tokens, depth)), fixed((tokens, depth)), fixed((depth, tokens))],
        out_shape=[
            struct((tokens, depth), F32),
            struct((tokens, depth), BF16),
            struct((depth, tokens), BF16),
        ],
        compiler_params=params(),
        cost_estimate=cost(2 << 30, 8 << 20),
        name="enter",
    )(*pooled, mixers, bias, gain, shift)


def beside(ref):
    return jnp.concatenate([ref[0, i] for i in range(3)], 1)


def project_kernel(x_ref, w_ref, extra_ref, q_ref, kv_ref):
    cols = q_ref.shape[2]
    heads = cols // HEAD_DIM
    bias = join(extra_ref[0], 5 * heads, 1, 1)
    triple = dot(x_ref[...], beside(w_ref))
    q_ref[0] = low(triple[:, :cols] + bias[:, cols : 2 * cols])
    kv_ref[0, 0] = low(triple[:, cols : 2 * cols])
    kv_ref[0, 1] = low(triple[:, 2 * cols :] + bias[:, 2 * cols : 3 * cols])


def project_call(rows, mixers, pack, start, count):
    _, _, depth, cols = mixers.shape
    tokens = rows.shape[0]
    extra = pack.shape[1] - cols
    return pl.pallas_call(
        project_kernel,
        grid=(count,),
        in_specs=[
            fixed((tokens, depth)),
            per_block((3, depth, cols), start),
            per_block((extra, depth), start, cols // extra, 0),
        ],
        out_specs=[per_block((tokens, cols)), per_block((2, tokens, cols))],
        out_shape=[
            struct((count, tokens, cols), BF16),
            struct((count, 2, tokens, cols), BF16),
        ],
        compiler_params=params(),
        cost_estimate=cost(9 * count * tokens * depth * cols, 3 << 20),
        name="project",
    )(rows, mixers, pack)


def project_back_kernel(first, xt_ref, w_ref, gq_ref, gkv_ref, *rest):
    before_ref, gx_ref, gw_ref, sums_ref = rest[1:] if not first else (None,) + rest[1:]
    cols = gq_ref.shape[2]
    grads = jnp.concatenate([gq_ref[0], gkv_ref[0, 0], gkv_ref[0, 1]], 1)
    total = dot(grads, beside(w_ref), NT)
    products = low(dot(xt_ref[...], grads))
    for i in range(3):
        gw_ref[0, i] = products[:, i * cols : (i + 1) * cols]
    sums_ref[0] = jnp.sum(grads.astype(F32), 0, keepdims=True)

    @pl.when(pl.program_id(0) == 0)
    def _():
        if first:
            gx_ref[...] = total
        else:
            gx_ref[...] = before_ref[...] + total

    @pl.when(pl.program_id(0) > 0)
    def _():
        gx_ref[...] += total


def project_back_call(rows_t, mixers, grad_query, grad_pair, start, grad_mixers, before):
    _, _, depth, cols = mixers.shape
    count, tokens, _ = grad_query.shape
    in_specs = [
        fixed((depth, tokens)),
        per_block((3, depth, cols), start),
        per_block((tokens, cols)),
        per_block((2, tokens, cols)),
        pl.BlockSpec(memory_space=pl.ANY),
    ]
    operands = [rows_t, mixers, grad_query, grad_pair, grad_mixers]
    if before is not None:
        in_specs.append(fixed((tokens, depth)))
        operands.append(before)
    return pl.pallas_call(
        lambda *refs: project_back_kernel(before is None, *refs),
        grid=(count,),
        in_specs=in_specs,
        out_specs=[
            fixed((tokens, depth)),
            per_block((3, depth, cols), start),
            per_block((1, 3 * cols)),
        ],
        out_shape=[
            struct((tokens, depth), F32),
            struct(grad_mixers.shape, BF16),
            struct((count, 1, 3 * cols), F32),
        ],
        input_output_aliases={4: 1},
        compiler_params=params(),
        cost_estimate=cost(15 * count * tokens * depth * cols, 8 << 20),
        name="project_back",
    )(*operands)


def leave_kernel(g_ref, s_ref, before_ref, gain_ref, o_ref, ot_ref, sums_ref):
    through, gain, shift = normalise_back(g_ref[...], s_ref[...], gain_ref[...])
    total = before_ref[...] + through
    rounded = low(total)
    o_ref[...] = rounded
    ot_ref[...] = low(total.T)
    bias = jnp.sum(rounded.astype(F32), 0, keepdims=True)
    sums_ref[...] = jnp.concatenate([gain, shift, bias], 0)


def leave_call(grad_normed, stream, before, gain):
    tokens, depth = stream.shape
    return pl.pallas_call(
        leave_kernel,
        out_shape=[
            struct((tokens, depth), BF16),
            struct((depth, tokens), BF16),
            struct((3, depth), F32),
        ],
        compiler_params=params(),
        cost_estimate=cost(1 << 30, 10 << 20),
        name="leave",
    )(grad_normed, stream, before, gain)


def attend_kernel(count, q_ref, *refs):
    sources, (o_ref, total_ref) = refs[:count], refs[count:]
    cols = q_ref.shape[2]
    heads = cols // HEAD_DIM
    scaled = q_ref[0] * SCALE
    lane = lax.broadcasted_iota(jnp.int32, scaled.shape, 1)
    values_t = [source[0, 1].T for source in sources]
    parts = []
    for h in range(heads):
        own = jnp.where(lane // HEAD_DIM == h, scaled, 0) if heads > 1 else scaled
        logits = [dot(source[0, 0], own, NT) for source in sources]
        peak = jnp.max(logits[0], 0, keepdims=True)
        for piece in logits[1:]:
            peak = jnp.maximum(peak, jnp.max(piece, 0, keepdims=True))
        norm = jnp.zeros_like(peak)
        out = jnp.zeros((HEAD_DIM, peak.shape[1]), F32)
        for piece, value in zip(logits, values_t):
            weight = jnp.exp(piece - peak)
            norm = norm + jnp.sum(weight, 0, keepdims=True)
            out = out + dot(value[h * HEAD_DIM : (h + 1) * HEAD_DIM], low(weight))
        parts.append(out / norm)
        total_ref[0, h] = peak + jnp.log(norm)
    full = jnp.concatenate(parts, 0) if heads > 1 else parts[0]
    o_ref[0] = full.T


def attend_call(queries, sources):
    count, tokens, cols = queries.shape
    heads = cols // HEAD_DIM
    keys = sum(array.shape[2] for array in sources)
    work = count * tokens * keys * cols
    return pl.pallas_call(
        lambda *refs: attend_kernel(len(sources), *refs),
        grid=(count,),
        in_specs=[per_block((tokens, cols))] + [per_block(array.shape[1:]) for array in sources],
        out_specs=[per_block((tokens, cols)), per_block((heads, 1, tokens))],
        out_shape=[
            struct((count, tokens, cols), F32),
            struct((count, heads, 1, tokens), F32),
        ],
        compiler_params=params(),
        cost_estimate=cost(25 * work, 4 << 20),
        name="attend",
    )(queries, *sources)


def middle_kernel(count, s_ref, *refs):
    o_refs, (w_ref, bias_ref, gain_ref, shift_ref, s1_ref, x_ref, xt_ref) = (
        refs[:count],
        refs[count:],
    )
    stream = s_ref[...] + bias_ref[...]
    index = 0
    for o_ref in o_refs:
        for i in range(o_ref.shape[0]):
            stream = stream + dot(low(o_ref[i]), w_ref[index], NT)
            index += 1
    s1_ref[...] = stream
    hat, _ = normalise(stream)
    rows = hat * gain_ref[...] + shift_ref[...]
    x_ref[...] = low(rows)
    xt_ref[...] = low(rows.T)


def middle_call(stream, attended, weights, bias, gain, shift):
    tokens, depth = stream.shape
    return pl.pallas_call(
        lambda *refs: middle_kernel(len(attended), *refs),
        out_shape=[
            struct((tokens, depth), F32),
            struct((tokens, depth), BF16),
            struct((depth, tokens), BF16),
        ],
        compiler_params=params(),
        cost_estimate=cost(2 << 30, 12 << 20),
        name="middle",
    )(stream, *attended, weights, bias, gain, shift)


def middle_back_kernel(g_ref, gt_ref, w_ref, o_ref, go_ref, gw_ref, delta_ref):
    cols = o_ref.shape[2]
    heads = cols // HEAD_DIM
    grads = low(dot(g_ref[...], w_ref[0]))
    go_ref[0] = grads
    attended = o_ref[0]
    gw_ref[0, 0] = low(dot(gt_ref[...], low(attended)))
    lane = lax.broadcasted_iota(jnp.int32, (8, cols), 1)
    row = lax.broadcasted_iota(jnp.int32, (8, cols), 0)
    mask = jnp.where(lane // HEAD_DIM == row, 1.0, 0.0)
    sums = dot(mask, grads.astype(F32) * attended, NT, precision=highest)
    for h in range(heads):
        delta_ref[0, h] = sums[h : h + 1]


def middle_back_call(grads, grads_t, weights, attended):
    blocks, tokens, cols = attended.shape
    depth = grads.shape[1]
    heads = cols // HEAD_DIM
    return pl.pallas_call(
        middle_back_kernel,
        grid=(blocks,),
        in_specs=[
            fixed((tokens, depth)),
            fixed((depth, tokens)),
            per_block((depth, cols)),
            per_block((tokens, cols)),
        ],
        out_specs=[
            per_block((tokens, cols)),
            per_block((1, depth, cols), 0, 3, 0, 0),
            per_block((heads, 1, tokens)),
        ],
        out_shape=[
            struct((blocks, tokens, cols), BF16),
            struct((blocks, 4, depth, cols), BF16),
            struct((blocks, heads, 1, tokens), F32),
        ],
        compiler_params=params(),
        cost_estimate=cost(6 << 30, 8 << 20),
        name="middle_back",
    )(grads, grads_t, weights, attended)


def attend_back_kernel(count, first, last, q_ref, g_ref, total_ref, delta_ref, *refs):
    sources, rest = refs[:count], refs[count:]
    before_ref, gq_ref, targets = (
        (None, rest[0], rest[1:]) if first else (rest[0], rest[1], rest[2:])
    )
    cols = q_ref.shape[2]
    heads = cols // HEAD_DIM
    scaled = q_ref[0] * SCALE
    grads = g_ref[0]
    lane = lax.broadcasted_iota(jnp.int32, scaled.shape, 1)
    pick = lambda tensor, h: jnp.where(lane // HEAD_DIM == h, tensor, 0) if heads > 1 else tensor
    own_q = [pick(scaled, h) for h in range(heads)]
    own_g = [pick(grads, h) for h in range(heads)]
    queries_t = [jnp.zeros((HEAD_DIM, scaled.shape[0]), F32) for h in range(heads)]
    for source, target in zip(sources, targets):
        keys, values = source[0, 0], source[0, 1]
        keys_t = keys.T
        grad_keys = jnp.zeros(keys.shape, F32)
        grad_values = jnp.zeros(keys.shape, F32)
        for h in range(heads):
            weight = jnp.exp(dot(keys, own_q[h], NT) - total_ref[0, h])
            grad_weight = dot(values, own_g[h], NT)
            grad_logit = low(weight * (grad_weight - delta_ref[0, h]))
            grad_values = grad_values + dot(low(weight), own_g[h])
            grad_keys = grad_keys + dot(grad_logit, own_q[h])
            queries_t[h] = queries_t[h] + dot(
                keys_t[h * HEAD_DIM : (h + 1) * HEAD_DIM], grad_logit
            )
        target[0, 0] = low(grad_keys)
        target[0, 1] = low(grad_values)
    full = jnp.concatenate(queries_t, 0) if heads > 1 else queries_t[0]
    if before_ref is not None:
        full = full + before_ref[0]
    gq_ref[0] = low(full * SCALE).T if last else full


def attend_back_call(queries, grads, totals, deltas, sources, start, before, last):
    count, tokens, cols = queries.shape
    heads = cols // HEAD_DIM
    keys = sum(array.shape[2] for array in sources)
    work = count * tokens * keys * cols
    block = sources[0].shape[1:]
    first = before is None
    result = struct((count, tokens, cols), BF16) if last else struct((count, cols, tokens), F32)
    return pl.pallas_call(
        lambda *refs: attend_back_kernel(len(sources), first, last, *refs),
        grid=(count,),
        in_specs=[
            per_block((tokens, cols)),
            per_block((tokens, cols), start),
            per_block((heads, 1, tokens)),
            per_block((heads, 1, tokens), start),
        ]
        + [per_block(block) for _ in sources]
        + ([] if first else [per_block((cols, tokens))]),
        out_specs=[per_block(result.shape[1:])] + [per_block(block) for _ in sources],
        out_shape=[result] + [struct((count,) + block, BF16) for _ in sources],
        compiler_params=params(),
        cost_estimate=cost(40 * work, 8 << 20),
        name="attend_back",
    )(queries, grads, totals, deltas, *sources, *([] if first else [before]))


def feed_kernel(
    cols,
    x_ref,
    xt_ref,
    g_ref,
    gt_ref,
    w_ref,
    extra_ref,
    s_ref,
    bias_ref,
    gain_ref,
    y_ref,
    gw_ref,
    gb_ref,
    gs_ref,
    g1_ref,
    g1t_ref,
    sums_ref,
    y_sum,
    gx_sum,
):
    parts, rows, wide = w_ref.shape
    depth, hidden = parts * rows, wide // 2
    heads = cols // HEAD_DIM
    step = pl.program_id(0)

    @pl.when(step == 0)
    def _():
        y_sum[...] = s_ref[...] + bias_ref[...]
        gx_sum[...] = jnp.zeros_like(gx_sum)

    up = w_ref[:, :, :hidden].reshape(depth, hidden)
    down = w_ref[:, :, hidden:].reshape(depth, hidden)
    up_bias = join(extra_ref[0], 5 * heads, 1, 1)[:, 3 * cols : 3 * cols + hidden]
    before = dot(x_ref[...], up) + up_bias
    bell = 0.5 * (1.0 + lax.erf(before * 0.7071067811865476))
    active = low(before * bell)
    slope = bell + before * (0.3989422804014327 * jnp.exp(-0.5 * before * before))
    grad_hidden = low(slope * dot(g_ref[...], down))
    y_sum[...] += dot(active, down, NT)
    gx_sum[...] += dot(grad_hidden, up, NT)
    gw_ref[:, :, :hidden] = low(dot(xt_ref[...], grad_hidden)).reshape(parts, rows, hidden)
    gw_ref[:, :, hidden:] = low(dot(gt_ref[...], active)).reshape(parts, rows, hidden)
    gb_ref[0] = jnp.sum(grad_hidden.astype(F32), 0, keepdims=True)

    @pl.when(step == pl.num_programs(0) - 1)
    def _():
        y_ref[...] = low(y_sum[...])
        through, gain, shift = normalise_back(gx_sum[...], s_ref[...], gain_ref[...])
        grads = g_ref[...].astype(F32)
        total = grads + through
        gs_ref[...] = total
        rounded = low(total)
        g1_ref[...] = rounded
        g1t_ref[...] = low(total.T)
        add = lambda tensor: jnp.sum(tensor, 0, keepdims=True)
        sums_ref[...] = jnp.concatenate([gain, shift, add(grads), add(rounded.astype(F32))], 0)


def feed_call(cols, rows, rows_t, grads, grads_t, weights, hidden, pack, stream, bias, gain, parts):
    tokens, depth = rows.shape
    pieces, slab, _ = weights.shape
    blocks = pieces // parts
    extra = pack.shape[1] - cols
    whole = fixed((tokens, depth))
    flipped = fixed((depth, tokens))
    row = fixed((1, depth))
    slabs = pl.BlockSpec((parts, slab, 2 * hidden), lambda n: (n, 0, 0))
    return pl.pallas_call(
        lambda *refs: feed_kernel(cols, *refs),
        grid=(blocks,),
        in_specs=[
            whole,
            flipped,
            whole,
            flipped,
            slabs,
            per_block((extra, depth), 0, cols // extra, 0),
            whole,
            row,
            row,
        ],
        out_specs=[whole, slabs, per_block((1, hidden)), whole, whole, flipped, fixed((4, depth))],
        out_shape=[
            struct((tokens, depth), BF16),
            struct((pieces, slab, 2 * hidden), BF16),
            struct((blocks, 1, hidden), F32),
            struct((tokens, depth), F32),
            struct((tokens, depth), BF16),
            struct((depth, tokens), BF16),
            struct((4, depth), F32),
        ],
        scratch_shapes=[pltpu.VMEM((tokens, depth), F32), pltpu.VMEM((tokens, depth), F32)],
        compiler_params=params(),
        cost_estimate=cost(18 * blocks * tokens * depth * hidden, 40 << 20),
        name="feed",
    )(rows, rows_t, grads, grads_t, weights, pack, stream, bias, gain)


def assemble_kernel(w_ref, *refs):
    pieces, (up_ref, down_ref) = refs[:-2], refs[-2:]
    hidden = up_ref.shape[1]
    for index, piece in enumerate(pieces):

        @pl.when(pl.program_id(0) == index)
        def _():
            up_ref[...] = piece[:, :hidden].astype(F32)
            down_ref[...] = piece[:, hidden:].astype(F32).T


def assemble_call(w, pieces):
    count = len(pieces)
    slab, lanes = pieces[0].shape
    hidden = lanes // 2
    direct = slab % 128 == 0
    down_shape = (hidden, count * slab) if direct else (count * hidden, slab)
    down_spec = (
        pl.BlockSpec((hidden, slab), lambda i, w_ref: (0, w_ref[0] ^ i))
        if direct
        else pl.BlockSpec((hidden, slab), lambda i, w_ref: (w_ref[0] ^ i, 0))
    )
    up, down = pl.pallas_call(
        assemble_kernel,
        grid_spec=pltpu.PrefetchScalarGridSpec(
            num_scalar_prefetch=1,
            grid=(count,),
            in_specs=[pl.BlockSpec((slab, lanes), lambda i, w_ref: (0, 0)) for _ in pieces],
            out_specs=[pl.BlockSpec((slab, hidden), lambda i, w_ref: (w_ref[0] ^ i, 0)), down_spec],
        ),
        out_shape=[struct((count * slab, hidden), F32), struct(down_shape, F32)],
        compiler_params=params(),
        cost_estimate=cost(1 << 28, 8 << 20),
        name="assemble",
    )(w.reshape(1), *pieces)
    if not direct:
        down = down.reshape(count, hidden, slab).transpose(1, 0, 2).reshape(hidden, count * slab)
    return up, down


def on_device(
    wide_size,
    narrow_size,
    variables,
    valid_slots,
    out_grad,
    patch_embed,
    variable_embed,
    pool_query,
    pool_key,
    pool_value,
    value_shift,
    pool_output,
    pool_bias,
    first_gain,
    first_shift,
    self_weights,
    query_bias,
    value_bias,
    self_output,
    output_bias,
    second_gain,
    second_shift,
    feed_up,
    up_bias,
    feed_down,
    down_bias,
):
    ring = Ring(wide_size, narrow_size)
    samples, token_count, input_width = variables.shape
    model_width = patch_embed.shape[1]
    local_dim = pool_query.shape[0]
    heads = local_dim // HEAD_DIM
    hidden = up_bias.shape[0]
    slab = model_width // wide_size
    shares = narrow_size // samples
    tokens = token_count // shares
    row = lambda vector: vector.reshape(1, -1)
    place = (ring.n // shares, (ring.n % shares) * tokens, 0)
    pixels = lax.dynamic_slice(variables, place, (1, tokens, input_width))[0]
    grads = lax.dynamic_slice(out_grad, place, (1, tokens, model_width))[0]
    valid = lax.dynamic_index_in_dim(valid_slots, ring.n // shares, 0, keepdims=False)
    valid = valid.reshape(VARS, 1)

    filler = jnp.zeros((model_width - input_width - VARS, model_width), BF16)
    table_full = jnp.concatenate([patch_embed, variable_embed, filler], 0)
    table_low = table_full[: input_width + VARS]
    bias_own = jnp.concatenate([value_shift, query_bias, value_bias, up_bias])
    bias_own = row(jnp.pad(bias_own, (0, model_width - bias_own.shape[0])))
    pack_own, mixers_own = prepare_call(
        heads,
        pool_key,
        row(pool_query),
        table_full,
        pool_value,
        pool_output,
        self_weights.transpose(1, 0, 2),
        bias_own,
    )
    pack = GatherShared(ring, pack_own).finish()
    gather = GatherShared(ring, tie(mixers_own, pack))
    pixels_one, pixels_t, grads_t = arrange_call(pixels, grads)
    rows_of = lambda tensor: lax.dynamic_slice_in_dim(tensor, ring.w * slab, slab, 0)
    columns_of = lambda tensor: lax.dynamic_slice_in_dim(tensor, ring.w * slab, slab, 1)
    feed_own = stage_call(
        rows_of(feed_up), columns_of(feed_down), columns_of(self_output), rows_of(pool_value)
    )
    feed_all = lax.all_gather(tie(feed_own, pack), ("narrow", "wide"))

    half = narrow_size // 2
    head_a = pool_call(pixels_one, pixels_t, valid, pack, local_dim, 0, half)
    head_b = pool_call(
        tie(pixels_one, gather.step(), head_a[1]), pixels_t, valid, pack, local_dim, half, half
    )
    pooled = [head_a[1], tie(head_b[1], gather.step())]
    mixers = gather.finish()
    stream_zero, normed_one, normed_one_t = enter_call(
        pooled, mixers, row(pool_bias), row(first_gain), row(first_shift)
    )

    permuted = wide_size == 4 and shares == 1
    groups = 4
    size = narrow_size // groups
    subsets = [[s * shares + i for i in range(shares)] for s in range(samples)]
    queries, sources = [], []
    for g in range(groups):
        mine, pair = project_call(normed_one, mixers, pack, g * size, size)
        queries.append(mine)
        if permuted:
            across = ring.swap(pair, 2)
            sources.append([pair, ring.swap(pair, 1), across, ring.swap(across, 1)])
        else:
            full = lax.all_gather(pair, "wide", axis=2, tiled=True)
            if shares > 1:
                full = lax.all_gather(
                    full, "narrow", axis=2, tiled=True, axis_index_groups=subsets
                )
            sources.append([full])
    attended, totals = [], []
    for g in range(groups):
        start = queries[g]
        if attended:
            start = tie(start, attended[-1])
        if permuted and g + 1 < groups:
            start = tie(start, sources[g + 1][2])
        got = attend_call(start, sources[g])
        attended.append(got[0])
        totals.append(got[1])
    part_of = lambda start, length: feed_all[:, :, start : start + length].reshape(
        narrow_size, model_width, length
    )
    self_all = part_of(2 * hidden, local_dim)
    value_all = part_of(2 * hidden + local_dim, local_dim)
    stream_one, normed_two, normed_two_t = middle_call(
        stream_zero, attended, self_all, row(output_bias), row(second_gain), row(second_shift)
    )

    block_own, grad_feed, grad_up_bias, grad_stream_one, grad_one, grad_one_t, sums_two = feed_call(
        local_dim,
        normed_two,
        normed_two_t,
        grads,
        grads_t,
        feed_all,
        hidden,
        pack,
        stream_one,
        row(down_bias),
        row(second_gain),
        wide_size,
    )
    gather_out = GatherOwn(ring, block_own, BF16)
    grad_feed = lax.psum_scatter(grad_feed, ("narrow", "wide"), scatter_dimension=0, tiled=True)
    grad_attended, grad_mixers, deltas = middle_back_call(
        grad_one, grad_one_t, self_all, jnp.concatenate(attended, 0)
    )

    token = grad_attended
    waiting = []
    for g in range(groups):
        back = lambda sources, before, last: attend_back_call(
            queries[g], token, totals[g], deltas, sources, g * size, before, last
        )
        if permuted:
            own, core, across, diagonal = sources[g]
            some, grad_core, grad_diagonal = back([core, diagonal], None, False)
            from_core = ring.swap(grad_core)
            from_diagonal = ring.swap(grad_diagonal)
            grad_query, grad_own, grad_across = back([own, across], some, True)
            far = low(grad_across.astype(F32) + from_diagonal.astype(F32))
            near = grad_own.astype(F32) + from_core.astype(F32)
            grad_pair = low(near + ring.swap(far, 2).astype(F32))
            token = tie(grad_attended, far)
        else:
            grad_query, full = back(sources[g], None, True)
            if shares > 1:
                full = lax.psum_scatter(
                    full, "narrow", scatter_dimension=2, tiled=True, axis_index_groups=subsets
                )
            grad_pair = lax.psum_scatter(full, "wide", scatter_dimension=2, tiled=True)
            token = tie(grad_attended, grad_query)
        if g == 1:
            token = tie(token, *gather_out.step())
        waiting.append((grad_query, grad_pair))
    grad_normed_one, sums_triple = None, []
    for g in range(groups):
        grad_query, grad_pair = waiting[g]
        if g == 1:
            grad_query = tie(grad_query, *gather_out.step())
        grad_normed_one, grad_mixers, sums = project_back_call(
            normed_one_t, mixers, grad_query, grad_pair, g * size, grad_mixers, grad_normed_one
        )
        sums_triple.append(sums)
    scatter = ScatterShared(ring, grad_mixers)
    grad_zero, grad_zero_t, sums_one = leave_call(
        grad_normed_one, stream_zero, grad_stream_one, row(first_gain)
    )

    quarter = half // 2 if half > 1 else half
    backs, before = [], None
    for start in range(0, narrow_size, quarter):
        weights, mixed = [piece[start % half : start % half + quarter] for piece in (
            head_a if start < half else head_b
        )]
        last = start + quarter == narrow_size
        first = pixels_one
        if start == quarter:
            first = tie(first, *gather_out.step())
        if start == 2 * quarter:
            first = tie(first, scatter.step())
        if last:
            first = tie(first, *gather_out.step())
        backs.append(
            pool_back_call(
                first,
                pixels_t,
                weights,
                pack,
                mixers,
                mixed,
                grad_zero,
                grad_zero_t,
                start,
                before,
                last,
            )
        )
        before = backs[-1][:2]
    grad_last, grad_pixels = before
    scatter_last = ScatterShared(ring, grad_last)
    scatter_last.step()
    scatter.step()
    gather_pixels = GatherOwn(ring, grad_pixels, F32)
    gather_pixels.step()
    block_out = gather_out.finish().reshape(samples, token_count, model_width)
    grad_pool_output, product = ring.finish_shared(scatter_last.finish())
    grad_pool_output = grad_pool_output[0].T
    product = low(product[0, : input_width + VARS])
    gather_product = GatherShared(ring, product)
    grad_variables = gather_pixels.finish().reshape(samples, token_count, input_width)
    grad_pool_value = dot(table_low, product, TN)
    grad_first, grad_second = ring.finish_shared(scatter.finish())
    grad_triple = jnp.concatenate([grad_first, grad_second[:1]], 0).transpose(1, 0, 2)
    grad_self_output = grad_second[1].T
    product_all = gather_product.finish()

    sums_triple = jnp.concatenate(sums_triple, 0).reshape(narrow_size, 3, local_dim)
    small = [
        sums_one,
        sums_two,
        jnp.concatenate([back[3] for back in backs], 0),
        sums_triple[:, 0],
        sums_triple[:, 2],
        grad_up_bias,
        jnp.concatenate([back[2] for back in backs], 0),
    ]
    lengths = [piece.size for piece in small]
    summed = jnp.concatenate([piece.reshape(-1) for piece in small])
    summed = ring.add_everywhere(summed.reshape(-1, 128)).reshape(-1)
    pieces, start = [], 0
    for length in lengths:
        pieces.append(summed[start : start + length])
        start += length
    grad_first_gain, grad_first_shift, grad_pool_bias = pieces[0].reshape(3, model_width)
    grad_second_gain, grad_second_shift, grad_down_bias, grad_output_bias = pieces[1].reshape(
        4, model_width
    )
    own_part = lambda piece, length: lax.dynamic_slice_in_dim(piece, ring.n * length, length, 0)
    grad_value_shift = own_part(pieces[2], local_dim)
    grad_query_bias = own_part(pieces[3], local_dim)
    grad_value_bias = own_part(pieces[4], local_dim)
    grad_up_bias = own_part(pieces[5], hidden)
    grad_terms = SCALE * pieces[6].reshape(narrow_size * heads, -1)
    grad_proj = own_part(grad_terms, heads)
    grad_folded = jnp.einsum("hr,rd->hd", grad_proj, table_low.astype(F32), precision=highest)
    query_heads = pool_query.reshape(heads, HEAD_DIM)
    key_heads = pool_key.astype(F32).reshape(model_width, heads, HEAD_DIM)
    grad_pool_key = (grad_folded.T[:, :, None] * query_heads).reshape(model_width, local_dim)
    grad_pool_query = jnp.einsum("dhe,hd->he", key_heads, grad_folded, precision=highest).reshape(
        local_dim
    )
    first_fold = local_dim + 3 * heads
    folded_all = pack[:, first_fold : first_fold + heads].astype(F32)
    folded_all = folded_all + pack[:, first_fold + heads : first_fold + 2 * heads].astype(F32)
    grad_table = jnp.einsum(
        "nrc,ndc->rd", product_all, value_all, preferred_element_type=F32
    ) + dot(
        grad_terms, folded_all.reshape(narrow_size * heads, model_width), TN, precision=highest
    )

    grad_feed_up, grad_feed_down = assemble_call(ring.w, ring.gather_wide(grad_feed[0]))
    return (
        block_out,
        grad_variables,
        grad_table[:input_width],
        grad_table[input_width:],
        grad_pool_query,
        grad_pool_key,
        grad_pool_value,
        grad_value_shift,
        grad_pool_output,
        grad_pool_bias,
        grad_first_gain,
        grad_first_shift,
        grad_triple,
        grad_query_bias,
        grad_value_bias,
        grad_self_output,
        grad_output_bias,
        grad_second_gain,
        grad_second_shift,
        grad_feed_up,
        grad_up_bias,
        grad_feed_down,
        grad_down_bias,
    )


def solution(mesh):
    wide_size, narrow_size = mesh.shape["wide"], mesh.shape["narrow"]

    def body(*arrays):
        return on_device(wide_size, narrow_size, *arrays)

    return jax.shard_map(
        body,
        mesh=mesh,
        in_specs=(
            P(None, "wide", None),
            P(),
            P(None, "wide", None),
            P(),
            P(),
            P("narrow"),
            P(None, "narrow"),
            P(None, "narrow"),
            P("narrow"),
            P("narrow", None),
            P(),
            P(),
            P(),
            P(None, None, "narrow"),
            P("narrow"),
            P("narrow"),
            P("narrow", None),
            P(),
            P(),
            P(),
            P(None, "narrow"),
            P("narrow"),
            P("narrow", None),
            P(),
        ),
        out_specs=(
            P(None, "wide", None),
            P(None, "wide", None),
            P(),
            P(),
            P("narrow"),
            P(None, "narrow"),
            P(None, "narrow"),
            P("narrow"),
            P("narrow", None),
            P(),
            P(),
            P(),
            P(None, None, "narrow"),
            P("narrow"),
            P("narrow"),
            P("narrow", None),
            P(),
            P(),
            P(),
            P(None, "narrow"),
            P("narrow"),
            P("narrow", None),
            P(),
        ),
        check_vma=False,
    )
```

time: 4150 us -> 810 us (0.20)
  waiting for transfers between devices: 3170 us -> 233 us
  matrix products: 430 us -> 14 us
  Pallas kernels: 0 us -> 293 us
  other arithmetic: 302 us -> 50.9 us
  local copies, waits for them, and re-layouts: 207 us -> 84 us
  starting transfers between devices: 0.37 us -> 110 us
    psum x7 -> x0, waiting for transfers between devices: 3020 us -> none  [the longest x5 2840 us: reduce_to(): return lax.psum(partial_value, 'narrow')]
    dot_general x34 -> x4, matrix products: 430 us -> 12.6 us  [the longest x2 6.87 us: dot(): lax.dot_general(left, right, (dims, ((), ())), precision=precision, prefe...]
    pallas_call x0 -> x40, Pallas kernels: none -> 293 us  [the longest x8 61.4 us: attend_back_call(): pl.pallas_call(lambda *refs: attend_back_kernel(len(sources), first, last...]
    ppermute x0 -> x87, waiting for transfers between devices: none -> 232 us  [move(): return lax.ppermute(tensor, AXES, pairs)]
    reduce_sum x17 -> x0, other arithmetic: 155 us -> none  [the longest x4 48.9 us: layer_norm(): centered = stream - jnp.mean(stream, -1, keepdims=True)]
    ppermute x0 -> x87, starting transfers between devices: none -> 110 us  [move(): return lax.ppermute(tensor, AXES, pairs)]
    reduce_scatter x1, waiting for transfers between devices: 95.9 us -> 0.01 us  [on_device(): lax.psum_scatter(grad_feed, ('narrow', 'wide'), scatter_dimension=0, tile...]
    convert_element_type x9 -> x22, other arithmetic: 96.4 us -> 25.5 us  [the longest x21 25.4 us: low(): return tensor.astype(BF16)]
  transfers between devices with their start and end apart: 9 -> 89, of which waited for: 9 -> 30; matrix products, arithmetic and copies ran while one was open for 5% -> 17% of each run, Pallas kernels for 0% -> 30%
where the time goes in v1:
time: 810 us; the launch traced here: 800 us
  Pallas kernels  293 us (36%)
  waiting for transfers between devices  233 us (29%)
  starting transfers between devices  110 us (14%)
  local copies, waits for them, and re-layouts  84 us (10%)
  other arithmetic  50.9 us (6%)
  between operations  15.6 us (2%)
  matrix products  14 us (2%)
    ppermute x87, waiting for transfers between devices, move(): return lax.ppermute(tensor, AXES, pairs)  232 us
    ppermute x87, starting transfers between devices, move(): return lax.ppermute(tensor, AXES, pairs)  110 us
    pallas_call x8, Pallas kernels, attend_back_call(): pl.pallas_call(lambda *refs: attend_back_kernel(len(sources), first, last...  61.4 us
    pallas_call x4, Pallas kernels, pool_back_call(): pl.pallas_call(lambda *refs: pool_back_kernel(not before, last, *refs), g...  44.2 us
    pallas_call x1, Pallas kernels, feed_call(): pl.pallas_call(lambda *refs: feed_kernel(cols, *refs), grid=(blocks,), in...  37 us
    pallas_call x4, Pallas kernels, attend_call(): pl.pallas_call(lambda *refs: attend_kernel(len(sources), *refs), grid=(co...  35 us
    dynamic_update_slice x31, local copies, waits for them, and re-layouts, put(): return lax.dynamic_update_index_in_dim(out, piece, index, 0)  32.6 us
    pallas_call x4, Pallas kernels, project_back_call(): pl.pallas_call(lambda *refs: project_back_kernel(before is None, *refs),...  27.8 us
  transfers between devices with their start and end apart: 89, of which 30 were waited for; matrix products, arithmetic and copies ran while one was open for 17% of the time, Pallas kernels for 30%

profile of v1, /device:TPU:0, one launch (start us, length us, event | category | flops | bytes accessed | tf_op | source)
XLA Modules:
  0.0 800.1 jit_solution(8639375838167678836)
XLA Ops:
  47.9 18.1 %collective-permute-done.7 = bf16[4,1024,128]{2,1,0:T(8,128)(2,1)S(1)} collective-permute-done((bf16[4,1024,128]{2,1,0:T(8,128)(2,1)S(1)}, bf16[4,1024,128]{2,1,0:T(8,128)(2,1)S(1)}, u32[]{:S(2)}, u32[]{:S(2)}) %collective-permute-start.7) | collective-permute-done | bytes 1048608 | tf_op jit(solution)/shard_map/ppermute | solution.py:88
  81.2 12.9 %pool.2 = (f32[4,2,48,512]{3,2,1,0:T(8,128)}, bf16[4,512,128]{2,1,0:T(8,128)(2,1)}) custom-call(bf16[512,816]{1,0:T(8,128)(2,1)} %get-tuple-element.227.x_ref.refs_0_, bf16[768,512]{1,0:T(8,128)(2,1)} %get-tuple-element.140.xt_ref.refs_1_, s32[48,1]{1,0:T(8,128)} %copy.59.valid_ref, ...), custom_call_target="tpu_custom_call" | custom-call | flops 5734400000 | bytes 4194304 | tf_op jit(solution)/shard_map/pool/pallas_call | solution.py:340
  99.6 13.0 %pool.3 = (f32[4,2,48,512]{3,2,1,0:T(8,128)}, bf16[4,512,128]{2,1,0:T(8,128)(2,1)}) custom-call(bf16[512,816]{1,0:T(8,128)(2,1)} %get-tuple-element.227.x_ref.refs_0_, bf16[768,512]{1,0:T(8,128)(2,1)} %get-tuple-element.140.xt_ref.refs_1_, s32[48,1]{1,0:T(8,128)} %copy.59.valid_ref, ...), custom_call_target="tpu_custom_call" | custom-call | flops 5734400000 | bytes 4194304 | tf_op jit(solution)/shard_map/pool/pallas_call | solution.py:340
  112.6 12.3 %collective-permute-done.11 = bf16[4,1024,128]{2,1,0:T(8,128)(2,1)S(1)} collective-permute-done((bf16[4,1024,128]{2,1,0:T(8,128)(2,1)S(1)}, bf16[4,1024,128]{2,1,0:T(8,128)(2,1)S(1)}, u32[]{:S(2)}, u32[]{:S(2)}) %collective-permute-start.11) | collective-permute-done | bytes 1048608 | tf_op jit(solution)/shard_map/ppermute | solution.py:88
  132.7 26.3 %collective-permute-done.13 = bf16[4,1024,128]{2,1,0:T(8,128)(2,1)S(1)} collective-permute-done((bf16[4,1024,128]{2,1,0:T(8,128)(2,1)S(1)}, bf16[4,1024,128]{2,1,0:T(8,128)(2,1)S(1)}, u32[]{:S(2)}, u32[]{:S(2)}) %collective-permute-start.13) | collective-permute-done | bytes 1048608 | tf_op jit(solution)/shard_map/ppermute | solution.py:88
  177.0 10.2 %collective-permute-start.15 = (bf16[2,2,512,128]{3,2,1,0:T(8,128)(2,1)S(1)}, bf16[2,2,512,128]{3,2,1,0:T(8,128)(2,1)S(1)}, u32[]{:S(2)}, u32[]{:S(2)}) collective-permute-start(bf16[2,2,512,128]{3,2,1,0:T(8,128)(2,1)S(1)} %copy-done.53), channel_id=1, source_target_pairs={{0,8},{1,9},{2,10},{3,11},{4,12},{5,13},{6,14},{7,15},{8,0},{9,1},... | collective-permute-start | bytes 1572872 | tf_op jit(solution)/shard_map/ppermute | solution.py:88
  211.8 9.9 %collective-permute-done.21.refs_3_.refs_5_ = bf16[2,2,512,128]{3,2,1,0:T(8,128)(2,1)S(1)} collective-permute-done((bf16[2,2,512,128]{3,2,1,0:T(8,128)(2,1)}, bf16[2,2,512,128]{3,2,1,0:T(8,128)(2,1)S(1)}, u32[]{:S(2)}, u32[]{:S(2)}) %collective-permute-start.21) | collective-permute-done | bytes 524320 | tf_op jit(solution)/shard_map/ppermute | solution.py:88
  233.7 9.0 %attend.6 = (f32[2,512,128]{2,1,0:T(8,128)}, f32[2,2,1,512]{3,2,1,0:T(1,128)}) custom-call(bf16[2,512,128]{2,1,0:T(8,128)(2,1)} %get-tuple-element.163.refs_0_, bf16[2,2,512,128]{3,2,1,0:T(8,128)(2,1)} %get-tuple-element.157.refs_1_.refs_4_, bf16[2,2,512,128]{3,2,1,0:T(8,128)(2,1)} %copy-done.52, bf16[2,2,512,128]{3,2,1,0:T(8,128)(2,1)} %copy-done.48, ...), custom_call_target="tpu_custom_call" | custom-call | flops 6710886400 | bytes 4194304 | tf_op jit(solution)/shard_map/attend/pallas_call | solution.py:680
  264.9 37.0 %feed.1 = (bf16[512,1024]{1,0:T(8,128)(2,1)}, bf16[32,256,1024]{2,1,0:T(8,128)(2,1)}, f32[8,1,512]{2,1,0:T(1,128)}, f32[512,1024]{1,0:T(8,128)}, bf16[512,1024]{...) custom-call(bf16[512,1024]{1,0:T(8,128)(2,1)} %get-tuple-element.169.refs_0_, ...), custom_call_target="tpu_custom_call" | custom-call | flops 38654705664 | bytes 41943040 | tf_op jit(solution)/shard_map/feed/pallas_call | solution.py:903
  313.9 10.5 %middle_back.1 = (bf16[8,512,128]{2,1,0:T(8,128)(2,1)}, bf16[8,4,1024,128]{3,2,1,0:T(8,128)(2,1)}, f32[8,2,1,512]{3,2,1,0:T(1,128)}) custom-call(bf16[512,1024]{1,0:T(8,128)(2,1)} %get-tuple-element.177.g_ref, bf16[1024,512]{1,0:T(8,128)(2,1)} %get-tuple-element.178.gt_ref, bf16[8,1024,128]{2,1,0:T(8,128)(2,1)} %bitcast.221, ...), custom_call_target="tpu_custom_call" | custom-call | flops 6442450944 | bytes 8388608 | tf_op jit(solution)/shard_map/middle_back/pallas_call | solution.py:747
  333.5 15.8 %collective-permute-start.26 = (bf16[512,1024]{1,0:T(8,128)(2,1)S(1)}, bf16[512,1024]{1,0:T(8,128)(2,1)S(1)}, u32[]{:S(2)}, u32[]{:S(2)}) collective-permute-start(bf16[512,1024]{1,0:T(8,128)(2,1)S(1)} %copy-done.6), channel_id=1, source_target_pairs={{0,2},{1,0},{2,4},{3,1},{4,6},{5,3},{6,7},{7,5},{8,10},{9,8},{10,1... | collective-permute-start | bytes 3145736 | tf_op jit(solution)/shard_map/ppermute | solution.py:88
  450.5 13.3 %collective-permute-done.40 = bf16[2,2,512,128]{3,2,1,0:T(8,128)(2,1)S(1)} collective-permute-done((bf16[2,2,512,128]{3,2,1,0:T(8,128)(2,1)S(1)}, bf16[2,2,512,128]{3,2,1,0:T(8,128)(2,1)S(1)}, u32[]{:S(2)}, u32[]{:S(2)}) %collective-permute-start.40) | collective-permute-done | bytes 524320 | tf_op jit(solution)/shard_map/ppermute | solution.py:88
  476.6 10.6 %collective-permute-done.38 = bf16[2,2,512,128]{3,2,1,0:T(8,128)(2,1)S(1)} collective-permute-done((bf16[2,2,512,128]{3,2,1,0:T(8,128)(2,1)S(1)}, bf16[2,2,512,128]{3,2,1,0:T(8,128)(2,1)S(1)}, u32[]{:S(2)}, u32[]{:S(2)}) %collective-permute-start.38) | collective-permute-done | bytes 524320 | tf_op jit(solution)/shard_map/ppermute | solution.py:88
  509.0 10.5 %pool_back.4 = (bf16[8,2,1024,128]{3,2,1,0:T(8,128)(2,1)}, f32[768,512]{1,0:T(8,128)}, f32[2,2,816]{2,1,0:T(2,128)}, f32[2,1,128]{2,1,0:T(1,128)}) custom-call(bf16[512,816]{1,0:T(8,128)(2,1)} %get-tuple-element.227.x_ref.refs_0_, bf16[768,512]{1,0:T(8,128)(2,1)} %get-tuple-element.140.xt_ref.refs_1_, f32[2,2,48,512]{3,2,1,0:T(8,128)} %get-tuple-element.315.refs_2_, ...), custom_call_target="tpu_custom_call" | custom-call | flops 3481600000 | bytes 6291456 | tf_op jit(solution)/shard_map/pool_back/pallas_call | solution.py:455
  522.9 11.3 %pool_back.5 = (bf16[8,2,1024,128]{3,2,1,0:T(8,128)(2,1)}, f32[768,512]{1,0:T(8,128)}, f32[2,2,816]{2,1,0:T(2,128)}, f32[2,1,128]{2,1,0:T(1,128)}) custom-call(bf16[512,816]{1,0:T(8,128)(2,1)} %get-tuple-element.227.x_ref.refs_0_, bf16[768,512]{1,0:T(8,128)(2,1)} %get-tuple-element.140.xt_ref.refs_1_, ...), custom_call_target="tpu_custom_call", output_to_operand_aliasing={{0}: (9, {})} | custom-call | flops 3481600000 | bytes 6291456 | tf_op jit(solution)/shard_map/pool_back/pallas_call | solution.py:455
  537.5 11.0 %pool_back.6 = (bf16[8,2,1024,128]{3,2,1,0:T(8,128)(2,1)}, f32[768,512]{1,0:T(8,128)}, f32[2,2,816]{2,1,0:T(2,128)}, f32[2,1,128]{2,1,0:T(1,128)}) custom-call(bf16[512,816]{1,0:T(8,128)(2,1)} %get-tuple-element.227.x_ref.refs_0_, bf16[768,512]{1,0:T(8,128)(2,1)} %get-tuple-element.140.xt_ref.refs_1_, ...), custom_call_target="tpu_custom_call", output_to_operand_aliasing={{0}: (9, {})} | custom-call | flops 3481600000 | bytes 6291456 | tf_op jit(solution)/shard_map/pool_back/pallas_call | solution.py:455
  556.8 11.4 %pool_back.7 = (bf16[8,2,1024,128]{3,2,1,0:T(8,128)(2,1)}, bf16[512,768]{1,0:T(8,128)(2,1)}, f32[2,2,816]{2,1,0:T(2,128)}, f32[2,1,128]{2,1,0:T(1,128)}) custom-call(bf16[512,816]{1,0:T(8,128)(2,1)} %get-tuple-element.227.x_ref.refs_0_, bf16[768,512]{1,0:T(8,128)(2,1)} %get-tuple-element.140.xt_ref.refs_1_, ...), custom_call_target="tpu_custom_call", output_to_operand_aliasing={{0}: (9, {})} | custom-call | flops 3481600000 | bytes 6291456 | tf_op jit(solution)/shard_map/pool_back/pallas_call | solution.py:455
  581.1 12.4 %collective-permute-done.73 = f32[214,128]{1,0:T(8,128)S(1)} collective-permute-done((f32[214,128]{1,0:T(8,128)S(1)}, f32[214,128]{1,0:T(8,128)S(1)}, u32[]{:S(2)}, u32[]{:S(2)}) %collective-permute-start.73) | collective-permute-done | bytes 109600 | tf_op jit(solution)/shard_map/ppermute | solution.py:88
  608.6 17.8 %collective-permute-done.75 = f32[214,128]{1,0:T(8,128)S(1)} collective-permute-done((f32[214,128]{1,0:T(8,128)S(1)}, f32[214,128]{1,0:T(8,128)S(1)}, u32[]{:S(2)}, u32[]{:S(2)}) %collective-permute-start.75) | collective-permute-done | bytes 109600 | tf_op jit(solution)/shard_map/ppermute | solution.py:88
  650.4 19.0 %collective-permute-done.58 = bf16[2,1024,128]{2,1,0:T(8,128)(2,1)S(1)} collective-permute-done((bf16[2,1024,128]{2,1,0:T(8,128)(2,1)S(1)}, bf16[2,1024,128]{2,1,0:T(8,128)(2,1)S(1)}, u32[]{:S(2)}, u32[]{:S(2)}) %collective-permute-start.58) | collective-permute-done | bytes 524320 | tf_op jit(solution)/shard_map/ppermute | solution.py:88
  699.1 12.4 %collective-permute-done.52 = bf16[512,768]{1,0:T(8,128)(2,1)S(1)} collective-permute-done((bf16[512,768]{1,0:T(8,128)(2,1)S(1)}, bf16[512,768]{1,0:T(8,128)(2,1)S(1)}, u32[]{:S(2)}, u32[]{:S(2)}) %collective-permute-start.52) | collective-permute-done | bytes 786464 | tf_op jit(solution)/shard_map/ppermute | solution.py:88
  712.8 12.0 %collective-permute-start.63 = (bf16[1,1024,128]{2,1,0:T(8,128)(2,1)S(1)}, bf16[1,1024,128]{2,1,0:T(8,128)(2,1)S(1)}, u32[]{:S(2)}, u32[]{:S(2)}) collective-permute-start(bf16[1,1024,128]{2,1,0:T(8,128)(2,1)S(1)} %add_convert_fusion.9), channel_id=1, source_target_pairs={{0,8},{1,9},{2,10},{3,11},{4,12},{5,13},{6,14},{7,15},{8,0},{9,1},... | collective-permute-start | bytes 786440 | tf_op jit(solution)/shard_map/ppermute | solution.py:88
  767.3 10.5 %collective-permute-done.85.refs_2_ = bf16[256,1024]{1,0:T(8,128)(2,1)} collective-permute-done((bf16[256,1024]{1,0:T(8,128)(2,1)}, bf16[256,1024]{1,0:T(8,128)(2,1)}, u32[]{:S(2)}, u32[]{:S(2)}) %collective-permute-start.85) | collective-permute-done | bytes 524320 | tf_op jit(solution)/shard_map/ppermute | solution.py:88
  777.8 10.9 %collective-permute-done.86.refs_3_ = bf16[256,1024]{1,0:T(8,128)(2,1)} collective-permute-done((bf16[256,1024]{1,0:T(8,128)(2,1)}, bf16[256,1024]{1,0:T(8,128)(2,1)}, u32[]{:S(2)}, u32[]{:S(2)}) %collective-permute-start.86) | collective-permute-done | bytes 524320 | tf_op jit(solution)/shard_map/ppermute | solution.py:88
  (445 shorter events, 446.3 us)
Async XLA Ops:
  7.2 245.8 %all-gather.3.cloned.1.call-start = ((), (), s32[]{:S(2)}) async-start(), calls=%async_computation.2 | async-start | bytes 21626880 | tf_op jit(solution)/shard_map/all_gather | solution.py:1041
  45.7 709.3 %reduce-scatter.2.cloned.1.call-start = ((), (), s32[]{:S(2)}) async-start(), calls=%async_computation.1 | async-start | bytes 17301504 | tf_op jit(solution)/shard_map/reduce_scatter | solution.py:1106
  333.5 49.2 %collective-permute-start.26 = (bf16[512,1024]{1,0:T(8,128)(2,1)S(1)}, bf16[512,1024]{1,0:T(8,128)(2,1)S(1)}, u32[]{:S(2)}, u32[]{:S(2)}) collective-permute-start(bf16[512,1024]{1,0:T(8,128)(2,1)S(1)} %copy-done.6), channel_id=1, source_target_pairs={{0,2},{1,0},{2,4},{3,1},{4,6},{5,3},{6,7},{7,5},{8,10},{9,8},{10,1... | collective-permute-start | bytes 3145736 | tf_op jit(solution)/shard_map/ppermute | solution.py:88
  349.3 36.7 %collective-permute-start.27 = (bf16[512,1024]{1,0:T(8,128)(2,1)S(1)}, bf16[512,1024]{1,0:T(8,128)(2,1)S(1)}, u32[]{:S(2)}, u32[]{:S(2)}) collective-permute-start(bf16[512,1024]{1,0:T(8,128)(2,1)S(1)} %copy-done.6), channel_id=1, source_target_pairs={{0,1},{1,3},{2,0},{3,5},{4,2},{5,7},{6,4},{7,6},{8,9},{9,11},{10,8... | collective-permute-start | bytes 3145736 | tf_op jit(solution)/shard_map/ppermute | solution.py:88
  349.3 44.3 %collective-permute-start.43 = (bf16[2,2,512,128]{3,2,1,0:T(8,128)(2,1)}, bf16[2,2,512,128]{3,2,1,0:T(8,128)(2,1)S(1)}, u32[]{:S(2)}, u32[]{:S(2)}) collective-permute-start(bf16[2,2,512,128]{3,2,1,0:T(8,128)(2,1)} %get-tuple-element.213), channel_id=1, source_target_pairs={{0,8},{1,9},{2,10},{3,11},{4,12},{5,13},{6,14},{7,15},{8,0},{9,1},... | collective-permute-start | bytes 1572872 | tf_op jit(solution)/shard_map/ppermute | solution.py:88
  367.5 34.0 %collective-permute-start.44 = (bf16[2,2,512,128]{3,2,1,0:T(8,128)(2,1)S(1)}, bf16[2,2,512,128]{3,2,1,0:T(8,128)(2,1)}, u32[]{:S(2)}, u32[]{:S(2)}) collective-permute-start(bf16[2,2,512,128]{3,2,1,0:T(8,128)(2,1)S(1)} %add_convert_fusion.8), channel_id=1, source_target_pairs={{0,16},{1,17},{2,18},{3,19},{4,20},{5,21},{6,22},{7,23},{8,24},{9,... | collective-permute-start | bytes 1572872 | tf_op jit(solution)/shard_map/ppermute | solution.py:88
  376.7 59.9 %collective-permute-start.41 = (bf16[2,2,512,128]{3,2,1,0:T(8,128)(2,1)}, bf16[2,2,512,128]{3,2,1,0:T(8,128)(2,1)S(1)}, u32[]{:S(2)}, u32[]{:S(2)}) collective-permute-start(bf16[2,2,512,128]{3,2,1,0:T(8,128)(2,1)} %get-tuple-element.210), channel_id=1, source_target_pairs={{0,8},{1,9},{2,10},{3,11},{4,12},{5,13},{6,14},{7,15},{8,0},{9,1},... | collective-permute-start | bytes 1572872 | tf_op jit(solution)/shard_map/ppermute | solution.py:88
  382.7 54.4 %collective-permute-start.42 = (bf16[2,2,512,128]{3,2,1,0:T(8,128)(2,1)S(1)}, bf16[2,2,512,128]{3,2,1,0:T(8,128)(2,1)S(1)}, u32[]{:S(2)}, u32[]{:S(2)}) collective-permute-start(bf16[2,2,512,128]{3,2,1,0:T(8,128)(2,1)S(1)} %add_convert_fusion.7), channel_id=1, source_target_pairs={{0,16},{1,17},{2,18},{3,19},{4,20},{5,21},{6,22},{7,23},{8,24},{9,... | collective-permute-start | bytes 1572872 | tf_op jit(solution)/shard_map/ppermute | solution.py:88
  393.6 47.3 %collective-permute-start.28 = (bf16[512,1024]{1,0:T(8,128)(2,1)S(1)}, bf16[512,1024]{1,0:T(8,128)(2,1)}, u32[]{:S(2)}, u32[]{:S(2)}) collective-permute-start(bf16[512,1024]{1,0:T(8,128)(2,1)S(1)} %collective-permute-done.26), channel_id=1, source_target_pairs={{0,2},{1,0},{2,4},{3,1},{4,6},{5,3},{6,7},{7,5},{8,10},{9,8},{10,1... | collective-permute-start | bytes 3145736 | tf_op jit(solution)/shard_map/ppermute | solution.py:88
  401.5 39.5 %collective-permute-start.29 = (bf16[512,1024]{1,0:T(8,128)(2,1)S(1)}, bf16[512,1024]{1,0:T(8,128)(2,1)}, u32[]{:S(2)}, u32[]{:S(2)}) collective-permute-start(bf16[512,1024]{1,0:T(8,128)(2,1)S(1)} %collective-permute-done.27), channel_id=1, source_target_pairs={{0,1},{1,3},{2,0},{3,5},{4,2},{5,7},{6,4},{7,6},{8,9},{9,11},{10,8... | collective-permute-start | bytes 3145736 | tf_op jit(solution)/shard_map/ppermute | solution.py:88
  441.0 35.6 %collective-permute-start.36 = (bf16[2,2,512,128]{3,2,1,0:T(8,128)(2,1)}, bf16[2,2,512,128]{3,2,1,0:T(8,128)(2,1)S(1)}, u32[]{:S(2)}, u32[]{:S(2)}) collective-permute-start(bf16[2,2,512,128]{3,2,1,0:T(8,128)(2,1)} %get-tuple-element.201), channel_id=1, source_target_pairs={{0,8},{1,9},{2,10},{3,11},{4,12},{5,13},{6,14},{7,15},{8,0},{9,1},... | collective-permute-start | bytes 1572872 | tf_op jit(solution)/shard_map/ppermute | solution.py:88
  441.2 46.0 %collective-permute-start.38 = (bf16[2,2,512,128]{3,2,1,0:T(8,128)(2,1)S(1)}, bf16[2,2,512,128]{3,2,1,0:T(8,128)(2,1)S(1)}, u32[]{:S(2)}, u32[]{:S(2)}) collective-permute-start(bf16[2,2,512,128]{3,2,1,0:T(8,128)(2,1)S(1)} %add_convert_fusion.5), channel_id=1, source_target_pairs={{0,16},{1,17},{2,18},{3,19},{4,20},{5,21},{6,22},{7,23},{8,24},{9,... | collective-permute-start | bytes 1572872 | tf_op jit(solution)/shard_map/ppermute | solution.py:88
  441.3 78.2 %collective-permute-start.30 = (bf16[512,1024]{1,0:T(8,128)(2,1)}, bf16[512,1024]{1,0:T(8,128)(2,1)}, u32[]{:S(2)}, u32[]{:S(2)}) collective-permute-start(bf16[512,1024]{1,0:T(8,128)(2,1)} %collective-permute-done.28), channel_id=1, source_target_pairs={{0,2},{1,0},{2,4},{3,1},{4,6},{5,3},{6,7},{7,5},{8,10},{9,8},{10,1... | collective-permute-start | bytes 3145736 | tf_op jit(solution)/shard_map/ppermute | solution.py:88
  450.4 72.5 %collective-permute-start.31 = (bf16[512,1024]{1,0:T(8,128)(2,1)}, bf16[512,1024]{1,0:T(8,128)(2,1)}, u32[]{:S(2)}, u32[]{:S(2)}) collective-permute-start(bf16[512,1024]{1,0:T(8,128)(2,1)} %collective-permute-done.29), channel_id=1, source_target_pairs={{0,1},{1,3},{2,0},{3,5},{4,2},{5,7},{6,4},{7,6},{8,9},{9,11},{10,8... | collective-permute-start | bytes 3145736 | tf_op jit(solution)/shard_map/ppermute | solution.py:88
  499.5 34.6 %collective-permute-start.45 = (bf16[4,1024,128]{2,1,0:T(8,128)(2,1)}, bf16[4,1024,128]{2,1,0:T(8,128)(2,1)}, u32[]{:S(2)}, u32[]{:S(2)}) collective-permute-start(bf16[4,1024,128]{2,1,0:T(8,128)(2,1)} %get-tuple-element.306), channel_id=1, source_target_pairs={{2,0},{0,1},{4,2},{1,3},{6,4},{3,5},{7,6},{5,7},{9,8},{11,9},{8,10... | collective-permute-start | bytes 3145736 | tf_op jit(solution)/shard_map/ppermute | solution.py:88
  499.5 34.6 %collective-permute-start.46 = (bf16[4,1024,128]{2,1,0:T(8,128)(2,1)}, bf16[4,1024,128]{2,1,0:T(8,128)(2,1)}, u32[]{:S(2)}, u32[]{:S(2)}) collective-permute-start(bf16[4,1024,128]{2,1,0:T(8,128)(2,1)} %get-tuple-element.305), channel_id=1, source_target_pairs={{0,8},{1,9},{2,10},{3,11},{4,12},{5,13},{6,14},{7,15},{8,0},{9,1},... | collective-permute-start | bytes 3145736 | tf_op jit(solution)/shard_map/ppermute | solution.py:88
  502.2 97.1 %collective-permute-start.77 = (bf16[4,1024,128]{2,1,0:T(8,128)(2,1)}, bf16[4,1024,128]{2,1,0:T(8,128)(2,1)S(1)}, u32[]{:S(2)}, u32[]{:S(2)}) collective-permute-start(bf16[4,1024,128]{2,1,0:T(8,128)(2,1)} %get-tuple-element.303), channel_id=1, source_target_pairs={{0,8},{1,9},{2,10},{3,11},{4,12},{5,13},{6,14},{7,15},{8,0},{9,1},... | collective-permute-start | bytes 3145736 | tf_op jit(solution)/shard_map/ppermute | solution.py:88
  519.5 37.2 %collective-permute-start.32 = (bf16[512,1024]{1,0:T(8,128)(2,1)}, bf16[512,1024]{1,0:T(8,128)(2,1)S(1)}, u32[]{:S(2)}, u32[]{:S(2)}) collective-permute-start(bf16[512,1024]{1,0:T(8,128)(2,1)} %collective-permute-done.30), channel_id=1, source_target_pairs={{0,2},{1,0},{2,4},{3,1},{4,6},{5,3},{6,7},{7,5},{8,10},{9,8},{10,1... | collective-permute-start | bytes 3145736 | tf_op jit(solution)/shard_map/ppermute | solution.py:88
  599.2 72.8 %collective-permute-start.79 = (bf16[4,1024,128]{2,1,0:T(8,128)(2,1)}, bf16[4,1024,128]{2,1,0:T(8,128)(2,1)}, u32[]{:S(2)}, u32[]{:S(2)}) collective-permute-start(bf16[4,1024,128]{2,1,0:T(8,128)(2,1)} %get-tuple-element.304), channel_id=1, source_target_pairs={{0,8},{1,9},{2,10},{3,11},{4,12},{5,13},{6,14},{7,15},{8,0},{9,1},... | collective-permute-start | bytes 3145736 | tf_op jit(solution)/shard_map/ppermute | solution.py:88
  599.3 44.1 %collective-permute-start.47 = (bf16[512,768]{1,0:T(8,128)(2,1)S(1)}, bf16[512,768]{1,0:T(8,128)(2,1)}, u32[]{:S(2)}, u32[]{:S(2)}) collective-permute-start(bf16[512,768]{1,0:T(8,128)(2,1)S(1)} %copy-done.9), channel_id=1, source_target_pairs={{0,2},{1,0},{2,4},{3,1},{4,6},{5,3},{6,7},{7,5},{8,10},{9,8},{10,1... | collective-permute-start | bytes 2359304 | tf_op jit(solution)/shard_map/ppermute | solution.py:88
  599.4 48.5 %collective-permute-start.48 = (bf16[512,768]{1,0:T(8,128)(2,1)S(1)}, bf16[512,768]{1,0:T(8,128)(2,1)}, u32[]{:S(2)}, u32[]{:S(2)}) collective-permute-start(bf16[512,768]{1,0:T(8,128)(2,1)S(1)} %copy-done.9), channel_id=1, source_target_pairs={{0,1},{1,3},{2,0},{3,5},{4,2},{5,7},{6,4},{7,6},{8,9},{9,11},{10,8... | collective-permute-start | bytes 2359304 | tf_op jit(solution)/shard_map/ppermute | solution.py:88
  604.3 36.1 %collective-permute-start.57 = (bf16[2,1024,128]{2,1,0:T(8,128)(2,1)}, bf16[2,1024,128]{2,1,0:T(8,128)(2,1)}, u32[]{:S(2)}, u32[]{:S(2)}) collective-permute-start(bf16[2,1024,128]{2,1,0:T(8,128)(2,1)} %get-tuple-element.309), channel_id=1, source_target_pairs={{0,8},{1,9},{2,10},{3,11},{4,12},{5,13},{6,14},{7,15},{8,0},{9,1},... | collective-permute-start | bytes 1572872 | tf_op jit(solution)/shard_map/ppermute | solution.py:88
  674.0 50.9 %collective-permute-start.80 = (bf16[4,1024,128]{2,1,0:T(8,128)(2,1)S(1)}, bf16[4,1024,128]{2,1,0:T(8,128)(2,1)S(1)}, u32[]{:S(2)}, u32[]{:S(2)}) collective-permute-start(bf16[4,1024,128]{2,1,0:T(8,128)(2,1)S(1)} %fusion.2), channel_id=1, source_target_pairs={{2,0},{0,1},{4,2},{1,3},{6,4},{3,5},{7,6},{5,7},{9,8},{11,9},{8,10... | collective-permute-start | bytes 3145736 | tf_op jit(solution)/shard_map/ppermute | solution.py:88
  694.7 43.2 %collective-permute-start.53 = (bf16[512,768]{1,0:T(8,128)(2,1)}, bf16[512,768]{1,0:T(8,128)(2,1)}, u32[]{:S(2)}, u32[]{:S(2)}) collective-permute-start(bf16[512,768]{1,0:T(8,128)(2,1)} %collective-permute-done.51), channel_id=1, source_target_pairs={{0,2},{1,0},{2,4},{3,1},{4,6},{5,3},{6,7},{7,5},{8,10},{9,8},{10,1... | collective-permute-start | bytes 2359304 | tf_op jit(solution)/shard_map/ppermute | solution.py:88
  (125 other events, 1580.9 us)
Sparse Core Ops, SparseCore 0:
  45.8 154.6 all-gather.2
  302.1 257.7 reduce-scatter.1

commit v2 on v0

v2 whole, which is shorter than its diff:
```python
import math

import jax
import jax.numpy as jnp
from jax import lax
from jax.experimental import pallas as pl
from jax.experimental.pallas import tpu as pltpu
from jax.sharding import PartitionSpec as P

HEAD_DIM = 64
VARS = 48
PIX = 16
SCALE = HEAD_DIM ** (-0.5)

highest = lax.Precision.HIGHEST
AXES = ("wide", "narrow")
F32 = jnp.float32
BF16 = jnp.bfloat16


def low(tensor):
    return tensor.astype(BF16)


def dot(left, right, dims=((1,), (0,)), precision=None):
    return lax.dot_general(
        left, right, (dims, ((), ())), precision=precision, preferred_element_type=F32
    )


NT = ((1,), (1,))
TN = ((0,), (0,))


def struct(shape, dtype):
    return jax.ShapeDtypeStruct(shape, dtype)


class Gate:
    waits, hands, handed = [], [], []


def wait_for(*arrays):
    Gate.waits += arrays


def hand_on(*arrays):
    Gate.hands += arrays


def whole_block():
    return pl.BlockSpec(memory_space=pltpu.VMEM)


def pallas(
    kernel,
    out_shape,
    grid=(),
    in_specs=None,
    out_specs=None,
    scratch_shapes=(),
    prefetch=0,
    input_output_aliases=None,
    us=1,
    mib=28,
    name=None,
):
    single = not isinstance(out_shape, (list, tuple))
    shapes = [out_shape] if single else list(out_shape)
    if out_specs is None:
        outs = [whole_block() for _ in shapes]
    else:
        outs = [out_specs] if single else list(out_specs)

    def call(*operands):
        waits, hands = Gate.waits, Gate.hands
        Gate.waits, Gate.hands = [], []
        given = len(operands)
        specs = list(in_specs) if in_specs is not None else [whole_block() for _ in operands]
        aliases = dict(input_output_aliases or {})
        aliases |= {given + len(waits) + i: len(shapes) + i for i in range(len(hands))}
        extra = len(waits) + len(hands)

        def body(*refs):
            kept = refs[:given] + refs[given + extra : given + extra + len(shapes)]
            kernel(*kept, *refs[given + extra + len(shapes) + len(hands) :])

        got = pl.pallas_call(
            body,
            grid_spec=pltpu.PrefetchScalarGridSpec(
                num_scalar_prefetch=prefetch,
                grid=grid,
                in_specs=specs + [anywhere() for _ in range(extra)],
                out_specs=outs + [anywhere() for _ in hands],
                scratch_shapes=scratch_shapes,
            ),
            out_shape=shapes + [struct(array.shape, array.dtype) for array in hands],
            input_output_aliases=aliases,
            compiler_params=pltpu.CompilerParams(vmem_limit_bytes=mib << 20),
            cost_estimate=pl.CostEstimate(
                flops=int(us * 1.15e9), bytes_accessed=0, transcendentals=0
            ),
            name=name,
        )(*operands, *waits, *hands)
        Gate.handed = list(got[len(shapes) :])
        return got[0] if single else list(got[: len(shapes)])

    return call


def fixed(shape, *start):
    start = start or (0,) * len(shape)
    return pl.BlockSpec(shape, lambda *_: start)


def per_block(shape, offset=0, *rest):
    rest = rest or (0,) * len(shape)
    return pl.BlockSpec((1,) + shape, lambda n: (n + offset,) + rest)


def anywhere():
    return pl.BlockSpec(memory_space=pl.ANY)


class Ring:
    def __init__(self, wide_size, narrow_size, in_order):
        self.wide, self.narrow, self.sorted = wide_size, narrow_size, in_order
        self.order = list(range(0, narrow_size, 2)) + list(range(1, narrow_size, 2))[::-1]
        place = {device: index for index, device in enumerate(self.order)}
        self.w = lax.axis_index("wide")
        self.n = lax.axis_index("narrow")
        self.core = self.w % 2
        self.pos = jnp.where(self.n % 2 == 0, self.n // 2, narrow_size - 1 - self.n // 2)

        def step(device, hops):
            return self.order[(place[device] + hops) % narrow_size]

        every = [(w, n) for w in range(wide_size) for n in range(narrow_size)]
        flat = lambda w, n: w * narrow_size + n
        bits = lambda size: [1 << i for i in range(size.bit_length() - 1)]
        self.forward = [(flat(w, n), flat(w, step(n, 1))) for w, n in every]
        self.backward = [(flat(w, n), flat(w, step(n, -1))) for w, n in every]
        self.by_core = [(flat(w, n), flat(w, step(n, 1 - 2 * (w % 2)))) for w, n in every]
        self.by_core_back = [(dst, src) for src, dst in self.by_core]
        self.wide_swap = {
            bit: [(flat(w, n), flat(w ^ bit, n)) for w, n in every] for bit in bits(wide_size)
        }
        self.narrow_swap = {
            bit: [(flat(w, n), flat(w, n ^ bit)) for w, n in every] for bit in bits(narrow_size)
        }

    def move(self, tensor, pairs):
        return lax.ppermute(tensor, AXES, pairs)

    def swap(self, tensor, bit=1):
        return self.move(tensor, self.wide_swap[bit])

    def at(self, hops):
        index = (self.pos + hops + 2 * self.narrow) % self.narrow
        return jnp.where(2 * index < self.narrow, 2 * index, 2 * (self.narrow - 1 - index) + 1)

    def ordered(self, first, second):
        if not self.sorted:
            return first, second
        pick = lambda a, b: jnp.where(self.core == 0, a, b)
        return pick(first, second), pick(second, first)

    def places(self):
        size = self.narrow
        sign = 1 if self.sorted else jnp.where(self.core == 0, 1, -1)
        order = [self.n, self.at(size // 2)]
        for hops in range(1, size // 2):
            order += [self.at(-sign * hops), self.at(sign * hops)]
        return order

    def scatter_wide(self, parts):
        parts = list(parts)
        for bit in self.wide_swap:
            kept = [index for index in range(self.wide) if index % (2 * bit) == 0]
            moved = [self.swap(parts[index | bit], bit) for index in kept]
            if len(kept) == 1:
                return parts[0], moved[0]
            sums = add_groups([[parts[index], got] for index, got in zip(kept, moved)])
            for index, total in zip(kept, sums):
                parts[index] = total

    def gather_wide(self, block):
        pieces = {0: block}
        for bit in self.wide_swap:
            for shift in list(pieces):
                pieces[shift | bit] = self.swap(pieces[shift], bit)
        return [pieces[shift] for shift in range(self.wide)]


def blank(shape, dtype):
    return pallas(
        lambda o_ref: None,
        out_shape=struct(shape, dtype),
        out_specs=anywhere(),
        us=0.1,
        name="blank",
    )()


def put(out, piece, index):
    return lax.dynamic_update_index_in_dim(out, piece, index, 0)


def add_kernel(groups, *refs):
    refs, outs = refs[: -len(groups)], refs[-len(groups) :]
    for size, out_ref in zip(groups, outs):
        total = refs[0][...].astype(F32)
        for ref in refs[1:size]:
            total = total + ref[...].astype(F32)
        out_ref[...] = low(total)
        refs = refs[size:]


def add_groups(groups):
    first = groups[0][0]
    shape = first[0].shape[1:] if isinstance(first, tuple) else first.shape
    width, size = shape[-1], math.prod(shape)
    rows = size // width
    steps = max(1, size * 2 >> 20)
    specs, flat = [], []
    for item in [item for group in groups for item in group]:
        array, part = item if isinstance(item, tuple) else (item, 0)
        start = part * steps
        specs.append(pl.BlockSpec((rows // steps, width), lambda i, start=start: (start + i, 0)))
        flat.append(array.reshape(-1, width))
    sums = pallas(
        lambda *refs: add_kernel([len(group) for group in groups], *refs),
        grid=(steps,),
        in_specs=specs,
        out_specs=[pl.BlockSpec((rows // steps, width), lambda i: (i, 0))] * len(groups),
        out_shape=[struct((rows, width), BF16)] * len(groups),
        us=2,
        mib=20,
        name="add",
    )(*flat)
    return [total.reshape(shape) for total in sums]


def add_up(*arrays):
    return add_groups([arrays])[0]


def pass_kernel(o_ref):
    o_ref[...] = jnp.zeros_like(o_ref)


def pass_on(arrays, *earlier):
    wait_for(*earlier)
    hand_on(*arrays)
    pallas(pass_kernel, out_shape=struct((8, 128), F32), us=0.5, mib=4, name="pass")()
    return Gate.handed


class GatherShared:
    def __init__(self, ring, block):
        self.ring, self.current, self.own = ring, block, block
        self.pairs, self.far = [], None

    def step(self, *earlier):
        ring = self.ring
        self.current = ring.move(self.current, ring.by_core)
        if earlier:
            (self.current,) = pass_on([self.current], *earlier)
        if 2 * (len(self.pairs) + 1) < ring.narrow:
            self.pairs.append(ring.ordered(self.current, ring.swap(self.current)))
            return self.pairs[-1]
        self.far = self.current
        return [self.far]

    def finish(self):
        while self.far is None:
            self.step()
        return [self.own, self.far] + [piece for pair in self.pairs for piece in pair]


class ScatterOwn:
    def __init__(self, ring, blocks):
        self.ring, self.blocks, self.hops = ring, blocks, ring.narrow // 2
        self.ahead, self.behind = self.pick(self.hops), None

    def pick(self, hops):
        return lax.dynamic_index_in_dim(self.blocks, self.ring.at(hops), 0, keepdims=False)

    def step(self):
        ring, self.hops = self.ring, self.hops - 1
        ahead = ring.move(self.ahead, ring.backward)
        behind = [] if self.behind is None else [ring.move(self.behind, ring.forward)]
        if not self.hops:
            self.ahead = add_up(ahead, *behind, self.pick(0))
        elif behind:
            self.ahead, self.behind = add_groups(
                [[ahead, self.pick(-self.hops)], [behind[0], self.pick(self.hops)]]
            )
        else:
            self.ahead, self.behind = add_up(ahead, self.pick(-self.hops)), self.pick(self.hops)
        return self.ahead


class GatherOwn:
    def __init__(self, ring, block, dtype):
        self.ring, self.hops, self.dtype = ring, 0, dtype
        self.moving = [block, block]
        self.out = blank((ring.narrow,) + block.shape, dtype)
        self.out = put(self.out, block.astype(dtype), ring.n)
        self.send()

    def send(self):
        ring, self.hops = self.ring, self.hops + 1
        ways = [ring.forward, ring.backward] if 2 * self.hops < ring.narrow else [ring.forward]
        self.moving = [ring.move(block, way) for block, way in zip(self.moving, ways)]

    def place(self):
        for block, sign in zip(self.moving, (-1, 1)):
            index = self.ring.at(sign * self.hops)
            self.out = put(self.out, block.astype(self.dtype), index)
        self.done = 2 * self.hops >= self.ring.narrow
        if not self.done:
            self.send()

    def beside(self, kernel):
        hand_on(*self.moving)
        got = kernel()
        self.moving = list(Gate.handed)
        self.place()
        return got

    def after(self, *earlier):
        self.moving = list(pass_on(self.moving, *earlier))
        self.place()

    def finish(self):
        while not self.done:
            self.place()
        return self.out


class ScatterShared:
    def __init__(self, ring, own, far):
        self.ring, self.own, self.current, self.got = ring, own, far, far

    def step(self, pair=None):
        ring = self.ring
        moved = ring.move(self.current, ring.by_core_back)
        if pair:
            first, second = ring.ordered(*pair)
            self.current = add_up(moved, first, ring.swap(second))
        else:
            self.current = add_up(moved, self.own)
        return self.current


class FinishShared:
    def __init__(self, ring, partial):
        self.ring, half = ring, partial.shape[0] // 2
        cut = lambda side: lax.dynamic_slice_in_dim(partial, side * half, half, 0)
        self.current, self.theirs = cut(ring.core), cut(1 - ring.core)
        self.bits = list(ring.wide_swap)

    def step(self):
        ring, bit = self.ring, self.bits.pop(0)
        sent = self.theirs if bit == 1 else self.current
        self.current = add_up(self.current, ring.swap(sent, bit))
        return self.current

    def finish(self):
        while self.bits:
            self.step()
        other = self.ring.swap(self.current)
        first = jnp.where(self.ring.core == 0, self.current, other).astype(F32)
        second = jnp.where(self.ring.core == 0, other, self.current).astype(F32)
        return first, second


class AddEverywhere:
    def __init__(self, ring, tensor):
        self.ring, self.current = ring, tensor
        self.pairs = list(ring.wide_swap.values()) + list(ring.narrow_swap.values())

    def step(self):
        self.current = self.current + self.ring.move(self.current, self.pairs.pop(0))
        return self.current

    def finish(self):
        while self.pairs:
            self.step()
        return self.current


def split_three(tensor):
    top = low(tensor)
    rest = tensor - top.astype(F32)
    middle = low(rest)
    return top, middle, low(rest - middle.astype(F32))


def lanes_to_rows(vector, cols):
    length = vector.shape[1]
    count = -(-length // cols)
    if count * cols > length:
        vector = jnp.concatenate([vector, jnp.zeros((1, count * cols - length), F32)], 1)
    return jnp.concatenate([vector[:, i * cols : (i + 1) * cols] for i in range(count)], 0)


def rows_to_lanes(rows, start, length):
    count = -(-length // rows.shape[1])
    return jnp.concatenate([rows[start + i : start + i + 1] for i in range(count)], 1)[:, :length]


class Extra:
    def __init__(self, cols, depth):
        self.heads, self.full = cols // HEAD_DIM, VARS * PIX + VARS
        self.term_rows, self.fold_rows = -(-self.full // cols), depth // cols
        self.fold_start = 3 * self.heads * self.term_rows
        self.bias_start = self.fold_start + 2 * self.heads * self.fold_rows

    def term(self, rows, part, head):
        return rows_to_lanes(rows, (part * self.heads + head) * self.term_rows, self.full)

    def folded(self, rows, head):
        place = lambda part: self.fold_start + (part * self.heads + head) * self.fold_rows
        length = self.fold_rows * rows.shape[1]
        return rows_to_lanes(rows, place(0), length) + rows_to_lanes(rows, place(1), length)

    def bias(self, rows, index):
        parts = [rows[self.bias_start + 3 * i + index :][:1] for i in range(3)]
        return parts[0] + (parts[1] + parts[2])


def prepare_kernel(
    key_ref, query_ref, table_ref, value_ref, output_ref, triple_ref, bias_ref, o_ref
):
    depth, cols = key_ref.shape
    extra = Extra(cols, depth)
    heads, full = extra.heads, extra.full
    keys, table = key_ref[...], table_ref[...]
    lane = lax.broadcasted_iota(jnp.int32, (8, cols), 1)
    row = lax.broadcasted_iota(jnp.int32, (8, cols), 0)
    masked = jnp.where(lane // HEAD_DIM == row, query_ref[...], 0.0)
    folded = sum(dot(part, keys, NT) for part in split_three(masked)[::-1])
    folded_parts = split_three(folded)
    terms = sum(dot(part, table, NT) for part in folded_parts[::-1]) * SCALE
    rows = [
        lanes_to_rows(part[h : h + 1, :full].astype(F32), cols)
        for part in split_three(terms)
        for h in range(heads)
    ]
    rows += [
        lanes_to_rows(part[h : h + 1].astype(F32), cols)
        for part in folded_parts[:2]
        for h in range(heads)
    ]
    rows += [lanes_to_rows(part.astype(F32), cols) for part in split_three(bias_ref[...])]
    rows.append(jnp.zeros((depth - full - sum(part.shape[0] for part in rows), cols), F32))
    o_ref[:3] = triple_ref[...]
    o_ref[3] = output_ref[...].astype(F32).T.astype(BF16)
    o_ref[4, :full] = low(dot(table, value_ref[...])[:full])
    o_ref[4, full:] = low(jnp.concatenate(rows, 0))


def prepare_call(keys, query, table, values, output, triple, bias):
    depth, cols = keys.shape
    return pallas(
        prepare_kernel,
        out_shape=struct((5, depth, cols), BF16),
        us=5.7,
        mib=40,
        name="prepare",
    )(keys, query, table, values, output, triple, bias)


def stage_kernel(up_ref, down_ref, value_ref, bias_ref, o_ref):
    depth, hidden = up_ref.shape
    cols = value_ref.shape[1]
    flip = lambda ref: ref[...].astype(F32).T.astype(BF16)
    o_ref[:cols] = flip(value_ref)
    o_ref[cols : cols + hidden] = flip(up_ref)
    o_ref[cols + hidden : cols + 2 * hidden] = down_ref[...]
    parts = [part.astype(F32) for part in split_three(bias_ref[...])]
    block = jnp.concatenate(parts + [jnp.zeros((13, hidden), F32)], 0)
    if hidden < depth:
        block = jnp.concatenate([block, jnp.zeros((16, depth - hidden), F32)], 1)
    o_ref[cols + 2 * hidden :] = low(block)


def stage_call(up, down, value, bias):
    depth, hidden = up.shape
    return pallas(
        stage_kernel,
        out_shape=struct((value.shape[1] + 2 * hidden + 16, depth), BF16),
        us=2,
        mib=40,
        name="stage",
    )(up, down, value, bias)


def arrange_kernel(x_ref, x1_ref, xt_ref):
    pixels = x_ref[...]
    x1_ref[...] = jnp.concatenate([pixels, jnp.ones((pixels.shape[0], VARS), BF16)], 1)
    xt_ref[...] = pixels.astype(F32).T.astype(BF16)


def arrange_call(pixels):
    tokens, width = pixels.shape
    return pallas(
        arrange_kernel,
        out_shape=[
            struct((tokens, width + VARS), BF16),
            struct((width, tokens), BF16),
        ],
        us=3.3,
        mib=40,
        name="arrange",
    )(pixels)


def slot_mask():
    slot = lax.broadcasted_iota(jnp.int32, (VARS, VARS * PIX + VARS), 0)
    column = lax.broadcasted_iota(jnp.int32, (VARS, VARS * PIX + VARS), 1)
    return slot == jnp.where(column < VARS * PIX, column // PIX, column - VARS * PIX)


def mix(weights, pixels_wide):
    tokens = weights.shape[1]
    spread = weights[:, None, :] * pixels_wide
    return jnp.concatenate([low(spread.reshape(VARS * PIX, tokens)), low(weights)], 0)


def pool_kernel(count, x_ref, xt_ref, valid_ref, *refs):
    p_refs, w_refs, o_refs = refs[:count], refs[count : 2 * count], refs[2 * count :]
    tokens, width = x_ref.shape
    pixels = x_ref[...]
    pixels_wide = xt_ref[...].astype(F32).reshape(VARS, PIX, tokens)
    valid = valid_ref[...] > 0
    mask = slot_mask()
    for p_ref, w_ref, o_ref in zip(p_refs, w_refs, o_refs):
        _, depth, cols = p_ref.shape
        extra = Extra(cols, depth)
        rows = p_ref[0, width:].astype(F32)
        table_value = p_ref[0, :width].astype(F32).T.astype(BF16)
        parts = []
        for h in range(extra.heads):
            scores = jnp.zeros((VARS, tokens), F32)
            for part in (2, 1, 0):
                spread = low(jnp.where(mask, extra.term(rows, part, h), 0.0))
                scores = scores + dot(spread, pixels, NT)
            scores = jnp.where(valid, scores, -1e30)
            weights = jnp.exp(scores - jnp.max(scores, 0, keepdims=True))
            weights = weights / jnp.sum(weights, 0, keepdims=True)
            w_ref[h] = weights
            mixed = mix(weights, pixels_wide)
            parts.append(dot(table_value[h * HEAD_DIM : (h + 1) * HEAD_DIM], mixed))
        pooled = jnp.concatenate(parts, 0) if len(parts) > 1 else parts[0]
        o_ref[...] = low(pooled.T + extra.bias(rows, 0))


def slot_of(piece, first, count=1):
    return fixed((count,) + piece.shape[1:], first // count, 0, 0)


def pool_call(pixels, pixels_t, valid, pieces):
    tokens = pixels.shape[0]
    cols = pieces[0].shape[2]
    count = len(pieces)
    weights, pooled = (cols // HEAD_DIM, VARS, tokens), (tokens, cols)
    got = pallas(
        lambda *refs: pool_kernel(count, *refs),
        grid=(1,),
        in_specs=[fixed(pixels.shape), fixed(pixels_t.shape), fixed((VARS, 1))]
        + [slot_of(piece, 4) for piece in pieces],
        out_specs=[fixed(weights)] * count + [fixed(pooled)] * count,
        out_shape=[struct(weights, F32)] * count + [struct(pooled, BF16)] * count,
        us=7,
        mib=40,
        name="pool",
    )(pixels, pixels_t, valid, *pieces)
    return list(zip(got[:count], got[count:]))


def pool_back_kernel(count, first, last, x_ref, xt_ref, g_ref, gt_ref, *refs):
    groups = [refs[i * count : (i + 1) * count] for i in range(4)]
    rest = refs[4 * count :]
    if not first:
        before_ref, rest = rest[0], rest[1:]
    pack_refs, (gx_ref, terms_ref, shift_ref) = rest[:count], rest[count:]
    tokens, full = x_ref.shape
    width = VARS * PIX
    pixels = x_ref[...]
    pixels_wide = xt_ref[...].astype(F32).reshape(VARS, PIX, tokens)
    mask = slot_mask()
    total = jnp.zeros((width, tokens), F32) if first else before_ref[...]
    for index, (v_ref, out_ref, w_ref, p_ref) in enumerate(zip(*groups)):
        _, depth, cols = v_ref.shape
        extra = Extra(cols, depth)
        rows = v_ref[0, full:].astype(F32)
        grads = low(dot(g_ref[...], out_ref[0]))
        shift_ref[index] = jnp.sum(grads.astype(F32), 0, keepdims=True)
        lane = lax.broadcasted_iota(jnp.int32, grads.shape, 1)
        table_value = v_ref[0, :full]
        product = jnp.zeros((full, cols), F32)
        for h in range(extra.heads):
            weights = w_ref[h]
            own = jnp.where(lane // HEAD_DIM == h, grads, 0) if extra.heads > 1 else grads
            grad_mixed = dot(table_value, own, NT)
            grad_wide = grad_mixed[:width].reshape(VARS, PIX, tokens)
            grad_weights = jnp.sum(grad_wide * pixels_wide, 1) + grad_mixed[width:]
            inner = jnp.sum(weights * grad_weights, 0, keepdims=True)
            grad_scores = weights * (grad_weights - inner)
            product = product + dot(mix(weights, pixels_wide), own)
            total = total + (weights[:, None, :] * grad_wide).reshape(width, tokens)
            gs_top = low(grad_scores)
            gs_rest = low(grad_scores - gs_top.astype(F32))
            top, middle = [
                low(jnp.where(mask, extra.term(rows, part, h), 0.0))[:, :width] for part in (0, 1)
            ]
            stacked = jnp.concatenate([top, top, middle], 0)
            total = total + dot(stacked, jnp.concatenate([gs_top, gs_rest, gs_top], 0), TN)
            both = dot(jnp.concatenate([gs_top, gs_rest], 0), pixels)
            by_slot = jnp.where(mask, both[:VARS] + both[VARS:], 0.0)
            terms_ref[index, h : h + 1, :] = jnp.sum(by_slot, 0, keepdims=True)
        pack_ref = pack_refs[index]
        pack_ref[0] = low(dot(gt_ref[...], p_ref[...]))
        pack_ref[1, :full] = low(product)
        pack_ref[1, full:] = jnp.zeros((depth - full, cols), BF16)
    gx_ref[...] = low(total.T) if last else total


def pool_back_call(pixels, pixels_t, heads, pieces, grads, grads_t, before, last):
    count = len(pieces)
    tokens, full = pixels.shape
    width = pixels_t.shape[0]
    _, depth, cols = pieces[0].shape
    in_specs = [fixed(array.shape) for array in (pixels, pixels_t, grads, grads_t)]
    in_specs += [slot_of(piece, 4) for piece in pieces] + [slot_of(piece, 3) for piece in pieces]
    in_specs += [fixed(head[0].shape) for head in heads] + [fixed(head[1].shape) for head in heads]
    operands = [pixels, pixels_t, grads, grads_t, *pieces, *pieces]
    operands += [head[0] for head in heads] + [head[1] for head in heads]
    if before is not None:
        in_specs.append(fixed((width, tokens)))
        operands.append(before)
    shapes = [struct((2, depth, cols), BF16)] * count
    shapes.append(struct((tokens, width), BF16) if last else struct((width, tokens), F32))
    shapes.append(struct((count, cols // HEAD_DIM, full), F32))
    shapes.append(struct((count, 1, cols), F32))
    got = pallas(
        lambda *refs: pool_back_kernel(count, before is None, last, *refs),
        grid=(1,),
        in_specs=in_specs,
        out_specs=[fixed(shape.shape) for shape in shapes],
        out_shape=shapes,
        us=21,
        name="pool_back",
    )(*operands)
    return list(got[:count]), *got[count:]


def normalise(stream):
    centered = stream - jnp.mean(stream, -1, keepdims=True)
    scale = lax.rsqrt(jnp.mean(centered * centered, -1, keepdims=True) + 1e-05)
    return centered * scale, scale


def normalise_back(grad, stream, gain):
    hat, scale = normalise(stream)
    through = grad * gain
    inner = through - jnp.mean(through, -1, keepdims=True)
    inner = inner - hat * jnp.mean(through * hat, -1, keepdims=True)
    add = lambda tensor: jnp.sum(tensor, 0, keepdims=True)
    return scale * inner, add(grad * hat), add(grad)


def enter_kernel(count, *refs):
    p_refs, w_refs = refs[:count], refs[count : 2 * count]
    bias_ref, gain_ref, shift_ref, s_ref, x_ref, xt_ref = refs[2 * count :]
    stream = jnp.zeros(s_ref.shape, F32) + bias_ref[...]
    for p_ref, w_ref in zip(p_refs, w_refs):
        stream = stream + dot(p_ref[...], w_ref[0], NT)
    s_ref[...] = stream
    hat, _ = normalise(stream)
    rows = hat * gain_ref[...] + shift_ref[...]
    x_ref[...] = low(rows)
    xt_ref[...] = low(rows.T)


def enter_call(pooled, pieces, bias, gain, shift):
    tokens = pooled[0].shape[0]
    depth = pieces[0].shape[1]
    row = fixed((1, depth))
    return pallas(
        lambda *refs: enter_kernel(len(pieces), *refs),
        grid=(1,),
        in_specs=[fixed(part.shape) for part in pooled]
        + [slot_of(piece, 3) for piece in pieces]
        + [row, row, row],
        out_specs=[fixed((tokens, depth)), fixed((tokens, depth)), fixed((depth, tokens))],
        out_shape=[
            struct((tokens, depth), F32),
            struct((tokens, depth), BF16),
            struct((depth, tokens), BF16),
        ],
        us=7,
        mib=40,
        name="enter",
    )(*pooled, *pieces, bias, gain, shift)


def beside(ref):
    return jnp.concatenate([ref[i] for i in range(3)], 1)


def project_kernel(count, x_ref, *refs):
    w_refs, e_refs, q_refs = refs[:count], refs[count : 2 * count], refs[2 * count : -1]
    kv_ref = refs[-1]
    for index, (w_ref, e_ref) in enumerate(zip(w_refs, e_refs)):
        _, depth, cols = w_ref.shape
        extra = Extra(cols, depth)
        rows = e_ref[0, extra.full :].astype(F32)
        triple = dot(x_ref[...], beside(w_ref))
        q_refs[index // 2][index % 2] = low(triple[:, :cols] + extra.bias(rows, 1))
        kv_ref[index, 0] = low(triple[:, cols : 2 * cols])
        kv_ref[index, 1] = low(triple[:, 2 * cols :] + extra.bias(rows, 2))


def project_call(rows, pieces):
    count = len(pieces)
    cols = pieces[0].shape[2]
    tokens = rows.shape[0]
    shapes = [struct((2, tokens, cols), BF16)] * (count // 2)
    shapes.append(struct((count, 2, tokens, cols), BF16))
    got = pallas(
        lambda *refs: project_kernel(count, *refs),
        grid=(1,),
        in_specs=[fixed(rows.shape)]
        + [slot_of(piece, 0, 3) for piece in pieces]
        + [slot_of(piece, 4) for piece in pieces],
        out_specs=[fixed(shape.shape) for shape in shapes],
        out_shape=shapes,
        us=1.2 * count,
        mib=40,
        name="project",
    )(rows, *pieces, *pieces)
    return got[:-1], got[-1]


def project_back_kernel(count, first, xt_ref, gq_ref, gkv_ref, *refs):
    w_refs, rest = refs[:count], refs[2 * count :]
    if not first:
        before_ref, rest = rest[0], rest[1:]
    gw_refs, (gx_ref, sums_ref) = rest[:count], rest[count:]
    cols = gq_ref.shape[2]
    total = jnp.zeros(gx_ref.shape, F32) if first else before_ref[...]
    for index, (w_ref, gw_ref) in enumerate(zip(w_refs, gw_refs)):
        grads = jnp.concatenate([gq_ref[index], gkv_ref[index, 0], gkv_ref[index, 1]], 1)
        total = total + dot(grads, beside(w_ref), NT)
        products = low(dot(xt_ref[...], grads))
        for i in range(3):
            gw_ref[i] = products[:, i * cols : (i + 1) * cols]
        sums_ref[index] = jnp.sum(grads.astype(F32), 0, keepdims=True)
    gx_ref[...] = total


def project_back_call(rows_t, pieces, grad_query, grad_pair, grad_pieces, before):
    count = len(pieces)
    depth, tokens = rows_t.shape
    cols = pieces[0].shape[2]
    in_specs = [fixed(array.shape) for array in (rows_t, grad_query, grad_pair)]
    in_specs += [slot_of(piece, 0, 3) for piece in pieces] + [anywhere()] * count
    operands = [rows_t, grad_query, grad_pair, *pieces, *grad_pieces]
    if before is not None:
        in_specs.append(fixed((tokens, depth)))
        operands.append(before)
    shapes = [struct(piece.shape, BF16) for piece in grad_pieces]
    shapes += [struct((tokens, depth), F32), struct((count, 1, 3 * cols), F32)]
    got = pallas(
        lambda *refs: project_back_kernel(count, before is None, *refs),
        grid=(1,),
        in_specs=in_specs,
        out_specs=[slot_of(piece, 0, 3) for piece in grad_pieces]
        + [fixed(shape.shape) for shape in shapes[count:]],
        out_shape=shapes,
        input_output_aliases={3 + count + i: i for i in range(count)},
        us=13.6,
        name="project_back",
    )(*operands)
    return list(got[:count]), *got[count:]


def leave_kernel(g_ref, s_ref, before_ref, gain_ref, o_ref, ot_ref, sums_ref):
    through, gain, shift = normalise_back(g_ref[...], s_ref[...], gain_ref[...])
    total = before_ref[...] + through
    rounded = low(total)
    o_ref[...] = rounded
    ot_ref[...] = low(total.T)
    bias = jnp.sum(rounded.astype(F32), 0, keepdims=True)
    sums_ref[...] = jnp.concatenate([gain, shift, bias], 0)


def leave_call(grad_normed, stream, before, gain):
    tokens, depth = stream.shape
    return pallas(
        leave_kernel,
        out_shape=[
            struct((tokens, depth), BF16),
            struct((depth, tokens), BF16),
            struct((3, depth), F32),
        ],
        us=12,
        name="leave",
    )(grad_normed, stream, before, gain)


def attend_kernel(count, q_ref, *refs):
    sources, (o_ref, total_ref) = refs[:count], refs[count:]
    cols = q_ref.shape[2]
    heads = cols // HEAD_DIM
    scaled = q_ref[0] * SCALE
    lane = lax.broadcasted_iota(jnp.int32, scaled.shape, 1)
    values_t = [source[0, 1].T for source in sources]
    parts = []
    for h in range(heads):
        own = jnp.where(lane // HEAD_DIM == h, scaled, 0) if heads > 1 else scaled
        logits = [dot(source[0, 0], own, NT) for source in sources]
        peak = jnp.max(logits[0], 0, keepdims=True)
        for piece in logits[1:]:
            peak = jnp.maximum(peak, jnp.max(piece, 0, keepdims=True))
        norm = jnp.zeros_like(peak)
        out = jnp.zeros((HEAD_DIM, peak.shape[1]), F32)
        for piece, value in zip(logits, values_t):
            weight = jnp.exp(piece - peak)
            norm = norm + jnp.sum(weight, 0, keepdims=True)
            out = out + dot(value[h * HEAD_DIM : (h + 1) * HEAD_DIM], low(weight))
        parts.append(out / norm)
        total_ref[0, h] = peak + jnp.log(norm)
    full = jnp.concatenate(parts, 0) if heads > 1 else parts[0]
    o_ref[0] = full.T


def pair_spec(shape, flip, start=0):
    place = lambda n: (start + (1 - n if flip else n),) + (0,) * len(shape)
    return pl.BlockSpec((1,) + shape, place)


def attend_call(queries, sources, flips, start):
    count, tokens, cols = queries.shape
    heads = cols // HEAD_DIM
    keys = sum(array.shape[2] for array in sources)
    work = count * tokens * keys * cols
    return pallas(
        lambda *refs: attend_kernel(len(sources), *refs),
        grid=(count,),
        in_specs=[per_block((tokens, cols))]
        + [pair_spec(array.shape[1:], flip, start) for array, flip in zip(sources, flips)],
        out_specs=[per_block((tokens, cols)), per_block((heads, 1, tokens))],
        out_shape=[
            struct((count, tokens, cols), F32),
            struct((count, heads, 1, tokens), F32),
        ],
        us=8.7,
        name="attend",
    )(queries, *sources)


def middle_kernel(count, s_ref, *refs):
    o_refs, w_refs = refs[:count], refs[count : 3 * count]
    bias_ref, gain_ref, shift_ref, s1_ref, x_ref, xt_ref = refs[3 * count :]
    stream = s_ref[...] + bias_ref[...]
    for index, w_ref in enumerate(w_refs):
        stream = stream + dot(low(o_refs[index // 2][index % 2]), w_ref[...])
    s1_ref[...] = stream
    hat, _ = normalise(stream)
    rows = hat * gain_ref[...] + shift_ref[...]
    x_ref[...] = low(rows)
    xt_ref[...] = low(rows.T)


def middle_call(stream, attended, weights, bias, gain, shift):
    tokens, depth = stream.shape
    operands = [stream, *attended, *weights, bias, gain, shift]
    shapes = [
        struct((tokens, depth), F32),
        struct((tokens, depth), BF16),
        struct((depth, tokens), BF16),
    ]
    return pallas(
        lambda *refs: middle_kernel(len(attended), *refs),
        grid=(1,),
        in_specs=[fixed(array.shape) for array in operands],
        out_specs=[fixed(shape.shape) for shape in shapes],
        out_shape=shapes,
        us=5,
        mib=40,
        name="middle",
    )(*operands)


def middle_back_kernel(g_ref, gt_ref, o_ref, wa_ref, wb_ref, go_ref, delta_ref, ga_ref, gb_ref):
    _, tokens, cols = o_ref.shape
    heads = cols // HEAD_DIM
    lane = lax.broadcasted_iota(jnp.int32, (8, cols), 1)
    row = lax.broadcasted_iota(jnp.int32, (8, cols), 0)
    mask = jnp.where(lane // HEAD_DIM == row, 1.0, 0.0)
    for index, (w_ref, gw_ref) in enumerate(((wa_ref, ga_ref), (wb_ref, gb_ref))):
        grads = low(dot(g_ref[...], w_ref[...], NT))
        go_ref[index] = grads
        attended = o_ref[index]
        gw_ref[0] = low(dot(gt_ref[...], low(attended)))
        sums = dot(mask, grads.astype(F32) * attended, NT, precision=highest)
        for h in range(heads):
            delta_ref[index, h] = sums[h : h + 1]


def middle_back_call(grads, grads_t, attended, weights):
    count, tokens, cols = attended.shape
    depth = grads.shape[1]
    heads = cols // HEAD_DIM
    piece = struct((4, depth, cols), BF16)
    operands = [grads, grads_t, attended, *weights]
    return pallas(
        middle_back_kernel,
        grid=(1,),
        in_specs=[fixed(array.shape) for array in operands],
        out_specs=[fixed(attended.shape), fixed((count, heads, 1, tokens))]
        + [slot_of(piece, 3)] * 2,
        out_shape=[
            struct(attended.shape, BF16),
            struct((count, heads, 1, tokens), F32),
            piece,
            piece,
        ],
        us=4,
        name="middle_back",
    )(*operands)


def attend_back_kernel(count, first, last, together, q_ref, g_ref, total_ref, delta_ref, *refs):
    sources, rest = refs[:count], refs[count:]
    before_ref, gq_ref, targets = (
        (None, rest[0], rest[1:]) if first else (rest[0], rest[1], rest[2:])
    )
    if together:
        targets = [targets[0].at[i] for i in range(count)]
    cols = q_ref.shape[2]
    heads = cols // HEAD_DIM
    scaled = q_ref[0] * SCALE
    grads = g_ref[0]
    lane = lax.broadcasted_iota(jnp.int32, scaled.shape, 1)
    pick = lambda tensor, h: jnp.where(lane // HEAD_DIM == h, tensor, 0) if heads > 1 else tensor
    own_q = [pick(scaled, h) for h in range(heads)]
    own_g = [pick(grads, h) for h in range(heads)]
    queries_t = [jnp.zeros((HEAD_DIM, scaled.shape[0]), F32) for h in range(heads)]
    for source, target in zip(sources, targets):
        keys, values = source[0, 0], source[0, 1]
        keys_t = keys.T
        grad_keys = jnp.zeros(keys.shape, F32)
        grad_values = jnp.zeros(keys.shape, F32)
        for h in range(heads):
            weight = jnp.exp(dot(keys, own_q[h], NT) - total_ref[0, h])
            grad_weight = dot(values, own_g[h], NT)
            grad_logit = low(weight * (grad_weight - delta_ref[0, h]))
            grad_values = grad_values + dot(low(weight), own_g[h])
            grad_keys = grad_keys + dot(grad_logit, own_q[h])
            queries_t[h] = queries_t[h] + dot(
                keys_t[h * HEAD_DIM : (h + 1) * HEAD_DIM], grad_logit
            )
        target[0, 0] = low(grad_keys)
        target[0, 1] = low(grad_values)
    full = jnp.concatenate(queries_t, 0) if heads > 1 else queries_t[0]
    if before_ref is not None:
        full = full + before_ref[0]
    gq_ref[0] = low(full * SCALE).T if last else full


def attend_back_call(queries, grads, totals, deltas, sources, flips, start, before, last, together):
    count, tokens, cols = queries.shape
    heads = cols // HEAD_DIM
    keys = sum(array.shape[2] for array in sources)
    work = count * tokens * keys * cols
    block = sources[0].shape[1:]
    first = before is None
    outs = [pair_spec(block, flip) for flip in flips]
    shapes = [struct((count,) + block, BF16) for _ in sources]
    if together:
        flip = flips[0]
        place = lambda n: (0, 1 - n if flip else n) + (0,) * len(block)
        outs = [pl.BlockSpec((len(sources), 1) + block, place)]
        shapes = [struct((len(sources), count) + block, BF16)]
    result = struct((count, tokens, cols), BF16) if last else struct((count, cols, tokens), F32)
    return pallas(
        lambda *refs: attend_back_kernel(len(sources), first, last, together, *refs),
        grid=(count,),
        in_specs=[
            per_block((tokens, cols)),
            per_block((tokens, cols)),
            per_block((heads, 1, tokens)),
            per_block((heads, 1, tokens)),
        ]
        + [pair_spec(block, flip, start) for flip in flips]
        + ([] if first else [per_block((cols, tokens))]),
        out_specs=[per_block(result.shape[1:])] + outs,
        out_shape=[result] + shapes,
        us=15.2,
        name="attend_back",
    )(queries, grads, totals, deltas, *sources, *([] if first else [before]))


def feed_kernel(first, cols, x_ref, g_ref, w_ref, *refs):
    if not first:
        before_ref, refs = refs[0], refs[1:]
    y_ref, gx_ref, gb_ref, gw_ref, y_sum, gx_sum = refs
    hidden = (w_ref.shape[1] - 16 - cols) // 2
    step = pl.program_id(0)

    @pl.when(step == 0)
    def _():
        y_sum[...] = jnp.zeros_like(y_sum)
        gx_sum[...] = jnp.zeros_like(gx_sum)

    rows_of = lambda start: jnp.concatenate([w_ref[i, start : start + hidden] for i in range(2)], 0)
    up, down = rows_of(cols), rows_of(cols + hidden)
    bias = []
    for i in range(2):
        rows = w_ref[i, cols + 2 * hidden :, :hidden].astype(F32)
        bias.append(rows[0:1] + (rows[1:2] + rows[2:3]))
    rows, grads = x_ref[...], g_ref[...]
    before = dot(rows, up, NT) + jnp.concatenate(bias, 1)
    bell = 0.5 * (1.0 + lax.erf(before * 0.7071067811865476))
    active = low(before * bell)
    slope = bell + before * (0.3989422804014327 * jnp.exp(-0.5 * before * before))
    grad_hidden = low(slope * dot(grads, down, NT))
    y_sum[...] += dot(active, down)
    gx_sum[...] += dot(grad_hidden, up)
    grad_up = dot(grad_hidden, rows, TN)
    grad_down = dot(active, grads, TN)
    gb_ref[0] = jnp.sum(grad_hidden.astype(F32), 0, keepdims=True)
    for i in range(2):
        part = slice(i * hidden, (i + 1) * hidden)
        made = jnp.concatenate([grad_up[part], grad_down[part]], 0)
        made = made if first else made + before_ref[i].astype(F32)
        gw_ref[i] = low(made)

    @pl.when(step == pl.num_programs(0) - 1)
    def _():
        y_ref[...] = low(y_sum[...])
        gx_ref[...] = low(gx_sum[...])


def feed_call(cols, rows, grads, staged, before):
    count, lines, depth = staged.shape
    tokens = rows.shape[0]
    lines = lines - 16 - cols
    whole = fixed((tokens, depth))
    pair = pl.BlockSpec((2, lines, depth), lambda n: (n, 0, 0))
    first = before is None
    return pallas(
        lambda *refs: feed_kernel(first, cols, *refs),
        grid=(count // 2,),
        in_specs=[whole, whole, pl.BlockSpec((2,) + staged.shape[1:], lambda n: (n, 0, 0))]
        + ([] if first else [pair]),
        out_specs=[whole, whole, pl.BlockSpec((1, 1, lines), lambda n: (n, 0, 0)), pair],
        out_shape=[
            struct((tokens, depth), BF16),
            struct((tokens, depth), BF16),
            struct((count // 2, 1, lines), F32),
            struct((count, lines, depth), BF16),
        ],
        scratch_shapes=[pltpu.VMEM((tokens, depth), F32), pltpu.VMEM((tokens, depth), F32)],
        us=11,
        mib=40,
        name="feed",
    )(rows, grads, staged, *([] if first else [before]))


def turn_kernel(count, *refs):
    g_ref, s_ref, gain_ref, gs_ref, g1_ref, g1t_ref, sums_ref = refs[count:]
    grad = refs[0][...].astype(F32)
    for ref in refs[1:count]:
        grad = grad + ref[...].astype(F32)
    through, gain, shift = normalise_back(grad, s_ref[...], gain_ref[...])
    grads = g_ref[...].astype(F32)
    total = grads + through
    gs_ref[...] = total
    rounded = low(total)
    g1_ref[...] = rounded
    g1t_ref[...] = low(total.T)
    add = lambda tensor: jnp.sum(tensor, 0, keepdims=True)
    sums_ref[...] = jnp.concatenate([gain, shift, add(grads), add(rounded.astype(F32))], 0)


def turn_call(parts, grads, stream, gain):
    tokens, depth = stream.shape
    return pallas(
        lambda *refs: turn_kernel(len(parts), *refs),
        out_shape=[
            struct((tokens, depth), F32),
            struct((tokens, depth), BF16),
            struct((depth, tokens), BF16),
            struct((4, depth), F32),
        ],
        us=8,
        name="turn",
    )(*parts, grads, stream, gain)


def assemble_kernel(w_ref, *refs):
    pieces, (up_ref, down_ref) = refs[:-2], refs[-2:]
    hidden = pieces[0].shape[0] // 2
    for index, piece in enumerate(pieces):

        @pl.when(pl.program_id(0) == index)
        def _():
            up_ref[...] = piece[:hidden].astype(F32).T
            down_ref[...] = piece[hidden:].astype(F32)


def assemble_call(w, pieces):
    count = len(pieces)
    lines, depth = pieces[0].shape
    hidden = lines // 2
    direct = hidden % 128 == 0
    up_place = (
        (lambda i, w_ref: (0, w_ref[0] ^ i)) if direct else (lambda i, w_ref: (w_ref[0] ^ i, 0))
    )
    up, down = pallas(
        assemble_kernel,
        prefetch=1,
        grid=(count,),
        in_specs=[pl.BlockSpec((lines, depth), lambda i, w_ref: (0, 0)) for _ in pieces],
        out_specs=[
            pl.BlockSpec((depth, hidden), up_place),
            pl.BlockSpec((hidden, depth), lambda i, w_ref: (w_ref[0] ^ i, 0)),
        ],
        out_shape=[
            struct((depth, count * hidden) if direct else (count * depth, hidden), F32),
            struct((count * hidden, depth), F32),
        ],
        us=3.3,
        name="assemble",
    )(w.reshape(1), *pieces)
    if not direct:
        up = up.reshape(count, depth, hidden).transpose(1, 0, 2).reshape(depth, count * hidden)
    return up, down


def table_kernel(count, order_ref, terms_ref, v_ref, *refs):
    p_refs, e_refs = refs[:count], refs[count : 2 * count]
    patch_ref, slot_ref = refs[2 * count :]
    depth = patch_ref.shape[1]
    cols = p_refs[0].shape[1]
    extra = Extra(cols, depth)
    folded = []
    total = jnp.zeros((extra.full, depth), F32)
    for index, (p_ref, e_ref) in enumerate(zip(p_refs, e_refs)):
        rows = e_ref[0, extra.full :].astype(F32)
        folded += [extra.folded(rows, h) for h in range(extra.heads)]
        total = total + dot(p_ref[...], v_ref[order_ref[index]])
    total = total + dot(terms_ref[...], jnp.concatenate(folded, 0), TN, precision=highest)
    width = patch_ref.shape[0]
    patch_ref[...] = total[:width]
    slot_ref[...] = total[width:]


def table_call(order, terms, values, products, pieces):
    _, depth, cols = pieces[0].shape
    width = VARS * PIX
    return pallas(
        lambda *refs: table_kernel(len(pieces), *refs),
        prefetch=1,
        grid=(1,),
        in_specs=[fixed(terms.shape), fixed((values.shape[0], cols, depth))]
        + [fixed(part.shape) for part in products]
        + [slot_of(piece, 4) for piece in pieces],
        out_specs=[fixed((width, depth)), fixed((VARS, depth))],
        out_shape=[struct((width, depth), F32), struct((VARS, depth), F32)],
        us=9,
        name="table_back",
    )(order, terms, values, *products, *pieces)


def on_device(
    wide_size,
    narrow_size,
    variables,
    valid_slots,
    out_grad,
    patch_embed,
    variable_embed,
    pool_query,
    pool_key,
    pool_value,
    value_shift,
    pool_output,
    pool_bias,
    first_gain,
    first_shift,
    self_weights,
    query_bias,
    value_bias,
    self_output,
    output_bias,
    second_gain,
    second_shift,
    feed_up,
    up_bias,
    feed_down,
    down_bias,
):
    samples, token_count, input_width = variables.shape
    model_width = patch_embed.shape[1]
    local_dim = pool_query.shape[0]
    heads = local_dim // HEAD_DIM
    hidden = up_bias.shape[0]
    shares = narrow_size // samples
    permuted = wide_size == 4 and shares == 1
    ring = Ring(wide_size, narrow_size, not permuted)
    tokens = token_count // shares
    groups = narrow_size // 2
    row = lambda vector: vector.reshape(1, -1)
    pair_of = lambda pieces, g: pieces[2 * g : 2 * g + 2]
    place = (ring.n // shares, (ring.n % shares) * tokens, 0)
    pixels = lax.dynamic_slice(variables, place, (1, tokens, input_width))[0]
    grads = lax.dynamic_slice(out_grad, place, (1, tokens, model_width))[0]
    valid = lax.dynamic_index_in_dim(valid_slots, ring.n // shares, 0, keepdims=False)
    valid = valid.reshape(VARS, 1)

    filler = jnp.zeros((model_width - input_width - VARS, model_width), BF16)
    table_full = jnp.concatenate([patch_embed, variable_embed, filler], 0)
    gather = GatherShared(
        ring,
        prepare_call(
            pool_key,
            row(pool_query),
            table_full,
            pool_value,
            pool_output,
            self_weights.transpose(1, 0, 2),
            row(jnp.concatenate([value_shift, query_bias, value_bias])),
        ),
    )
    pixels_one, pixels_t = arrange_call(pixels)
    all_grads = ring.gather_wide(grads)
    quarter = hidden // wide_size
    cut_out = lambda tensor, axis: lax.dynamic_slice_in_dim(tensor, ring.w * quarter, quarter, axis)
    feed_own = stage_call(
        cut_out(feed_up, 1), cut_out(feed_down, 0), pool_value, row(cut_out(up_bias, 0))
    )
    pool = lambda pieces: pool_call(pixels_one, pixels_t, valid, pieces)
    wait_for(feed_own)
    pooled = pool([gather.own])
    for g in range(1, groups):
        got = list(gather.step())
        wait_for(pooled[-1][1])
        if g == 2:
            wait_for(*all_grads)
        pooled += pool(got)
    gather.step()
    wait_for(pooled[-1][1])
    hand_on(feed_own, self_output)
    far = pool([gather.far])
    feed_all = lax.all_gather(Gate.handed[0], "narrow")
    gather_mixer = GatherShared(ring, Gate.handed[1])
    pooled = [pooled[0], far[0]] + pooled[1:]
    pieces = gather.finish()
    stream_zero, normed_one, normed_one_t = enter_call(
        [head[1] for head in pooled], pieces, row(pool_bias), row(first_gain), row(first_shift)
    )

    subsets = [[s * shares + i for i in range(shares)] for s in range(samples)]
    chunks = [[g] for g in range(groups)]
    gather_mixer.step(stream_zero)
    queries, sources, flips, starts = [], [], [], []
    for chunk in chunks:
        if queries:
            wait_for(queries[-1])
        mine, pair = project_call(normed_one, pieces[2 * chunk[0] : 2 * chunk[-1] + 2])
        queries += mine
        if permuted:
            across = ring.swap(pair, 2)
            got = [pair, ring.swap(pair, 1), across, ring.swap(across, 1)]
        else:
            full = lax.all_gather(pair, "wide", axis=2, tiled=True)
            if shares > 1:
                full = lax.all_gather(
                    full, "narrow", axis=2, tiled=True, axis_index_groups=subsets
                )
            got = [full]
        for g in chunk:
            sources.append(got)
            flips.append([False, g > 0, False, g > 0] if permuted else [False])
            starts.append(2 * (g - chunk[0]))
    gather_mixer.step(queries[-1])
    attended, totals = [], []
    for g in range(groups):
        if attended:
            wait_for(attended[-1])
        got = attend_call(queries[g], sources[g], flips[g], starts[g])
        attended.append(got[0])
        totals.append(got[1])
        if g < 2:
            gather_mixer.step(got[0])
    self_pieces = gather_mixer.finish()
    order = jnp.stack(ring.places()).astype(jnp.int32)
    stream_one, normed_two, _ = middle_call(
        stream_zero, attended, self_pieces, row(output_bias), row(second_gain), row(second_shift)
    )

    all_rows = ring.gather_wide(normed_two)
    y_all, gx_all, gb_all, grad_feed = [], [], [], None
    for index in range(wide_size):
        if grad_feed is not None:
            wait_for(gx_all[-1])
        got = feed_call(
            local_dim, all_rows[index], all_grads[index], feed_all, grad_feed
        )
        y_all.append(got[0])
        gx_all.append(got[1])
        gb_all.append(got[2])
        grad_feed = got[3]
    scatter_feed = ScatterOwn(ring, grad_feed)
    grad_parts = ring.scatter_wide(gx_all)
    wait_for(grad_parts[0])
    for _ in range(narrow_size // 2 - 2):
        scatter_feed.step()
    y_parts = ring.scatter_wide(pass_on(y_all, grad_parts[1]))
    grad_up_bias = sum(gb_all).reshape(narrow_size, quarter)
    wait_for(scatter_feed.ahead)
    grad_stream_one, grad_one, grad_one_t, sums_two = turn_call(
        grad_parts, grads, stream_one, row(second_gain)
    )
    block_own = low(stream_one + down_bias + (y_parts[0].astype(F32) + y_parts[1].astype(F32)))
    gather_out = GatherOwn(ring, block_own, BF16)

    waiting = {}
    backward = [0] + list(range(groups - 1, 0, -1))
    for turn, g in enumerate(backward):
        if turn == 1:
            wait_for(block_own)
        back = lambda: middle_back_call(
            grad_one, grad_one_t, attended[g], pair_of(self_pieces, g)
        )
        got = gather_out.beside(back) if turn in (2, 3) else back()
        grad_attended, deltas, *grad_pair_mixers = got
        back = lambda chosen, before, last, together: attend_back_call(
            queries[g],
            grad_attended,
            totals[g],
            deltas,
            [sources[g][i] for i in chosen],
            [flips[g][i] for i in chosen],
            starts[g],
            before,
            last,
            together,
        )
        if permuted:
            some, crossing = back([1, 3], None, False, True)
            crossed = ring.swap(crossing)
            grad_query, grad_own, grad_across = back([0, 2], some, True, False)
            far = add_up(grad_across, (crossed, 1))
            grad_pair = [grad_own, (crossed, 0), ring.swap(far, 2)]
        else:
            grad_query, full = back([0], None, True, False)
            if shares > 1:
                full = lax.psum_scatter(
                    full, "narrow", scatter_dimension=2, tiled=True, axis_index_groups=subsets
                )
            far = lax.psum_scatter(full, "wide", scatter_dimension=2, tiled=True)
            grad_pair = [far]
        waiting[g] = (grad_query, grad_pair, grad_pair_mixers)
        wait_for(far)
        if turn < 2:
            wait_for(scatter_feed.step())
    grad_normed_one, grad_pieces, sums_triple = None, {}, [None] * groups
    for turn, g in enumerate(backward):
        grad_query, grad_pair, grad_pair_mixers = waiting[g]
        if grad_normed_one is not None:
            wait_for(grad_normed_one)
        grad_pair = add_up(*grad_pair)
        back = lambda: project_back_call(
            normed_one_t,
            pair_of(pieces, g),
            grad_query,
            grad_pair,
            grad_pair_mixers,
            grad_normed_one,
        )
        made, grad_normed_one, sums = gather_out.beside(back) if turn in (0, 3) else back()
        grad_pieces[g], sums_triple[g] = made, sums
    scatter = ScatterShared(ring, *grad_pieces[0])
    grad_zero, grad_zero_t, sums_one = leave_call(
        grad_normed_one, stream_zero, grad_stream_one, row(first_gain)
    )

    grad_pixels, grad_terms, grad_shifts = None, [None] * groups, [None] * groups
    for turn, g in enumerate(backward):
        if turn > 1:
            wait_for(grad_pixels)
            added = scatter.step(grad_pieces[backward[turn - 1]])
            wait_for(added)
            wait_for(scatter_last.step(made))
        back = lambda: pool_back_call(
            pixels_one,
            pixels_t,
            pair_of(pooled, g),
            pair_of(pieces, g),
            grad_zero,
            grad_zero_t,
            grad_pixels,
            turn == groups - 1,
        )
        made, grad_pixels, terms, shifts = back()
        if turn == 0:
            scatter_last = ScatterShared(ring, *made)
        grad_terms[g], grad_shifts[g] = terms, shifts

    def sort_into(places, tensor, back=False):
        same = jnp.stack([jnp.stack([p == i for p in places]) for i in range(narrow_size)])
        same = same.T if back else same
        return jnp.sum(jnp.where(same[:, :, None], tensor[None], 0.0), 1)

    places = ring.places()
    sums_triple = jnp.concatenate(sums_triple, 0).reshape(narrow_size, -1)
    up_bias_row = lax.dynamic_update_slice(
        jnp.zeros((narrow_size, hidden), F32),
        grad_up_bias,
        (0, ring.w * quarter),
    )
    own_sums = jnp.concatenate(
        [
            jnp.concatenate(grad_shifts, 0).reshape(narrow_size, -1),
            sums_triple[:, :local_dim],
            sums_triple[:, 2 * local_dim :],
            jnp.concatenate(grad_terms, 0).reshape(narrow_size, -1),
        ],
        1,
    )
    own_sums = jnp.concatenate([up_bias_row, sort_into(places, own_sums)], 1)
    own_length = own_sums.shape[1]
    shared_sums = jnp.concatenate([sums_one, sums_two], 0)
    all_sums = jnp.concatenate([own_sums.reshape(-1), shared_sums.reshape(-1)]).reshape(-1, 128)
    scatter_last.step(made)
    hand_on(grad_pixels)
    scatter_last.step()
    gather_pixels = GatherOwn(ring, Gate.handed[0], F32)
    finish_last = FinishShared(ring, scatter_last.current)
    finish_last.step()
    finish_last.step()
    grad_pool_output, product = finish_last.finish()
    product = low(product[0, : input_width + VARS])
    gather_product = GatherShared(ring, product)
    adder = AddEverywhere(ring, *pass_on([all_sums], product))
    adder.step()
    block_out = gather_out.finish().reshape(samples, token_count, model_width)
    gather_pixels.after(product)
    wait_for(product)
    scatter.step(grad_pieces[backward[-1]])
    adder.step()
    hop = gather_product.step()[0]
    gather_pixels.after(hop)
    wait_for(hop)
    scatter.step()
    finish = FinishShared(ring, scatter.current)
    hop = gather_product.step()[0]
    gather_pixels.after(hop)
    wait_for(hop)
    finish.step()
    finish.step()
    products = gather_product.finish()
    grad_feed_pieces = ring.gather_wide(scatter_feed.ahead)
    grad_feed_up, grad_feed_down = assemble_call(ring.w, grad_feed_pieces)
    grad_first, grad_second = finish.finish()
    adder.finish()
    grad_variables = gather_pixels.finish().reshape(samples, token_count, input_width)
    grad_triple = jnp.concatenate([grad_first, grad_second[:1]], 0).transpose(1, 0, 2)
    grad_self_output = grad_second[1].T
    grad_pool_output = grad_pool_output[0].T
    grad_pool_value = dot(patch_embed, product[:input_width], TN)
    grad_pool_value = grad_pool_value + dot(variable_embed, product[input_width:], TN)

    summed = adder.current.reshape(-1)
    own_all = summed[: narrow_size * own_length].reshape(narrow_size, own_length)
    shared_all = summed[narrow_size * own_length :].reshape(-1, model_width)
    grad_first_gain, grad_first_shift, grad_pool_bias = shared_all[:3]
    grad_second_gain, grad_second_shift, grad_down_bias, grad_output_bias = shared_all[3:]
    own = lax.dynamic_index_in_dim(own_all, ring.n, 0, keepdims=False)
    grad_up_bias = own[:hidden]
    grad_value_shift, grad_query_bias, grad_value_bias = own[hidden : hidden + 3 * local_dim].reshape(
        3, local_dim
    )
    terms_start = 3 * local_dim + hidden
    grad_proj = SCALE * own[terms_start:].reshape(heads, -1)
    grad_folded = dot(grad_proj[:, :input_width], patch_embed.astype(F32), precision=highest)
    grad_folded = grad_folded + dot(
        grad_proj[:, input_width:], variable_embed.astype(F32), precision=highest
    )
    query_heads = pool_query.reshape(heads, HEAD_DIM)
    key_heads = pool_key.astype(F32).reshape(model_width, heads, HEAD_DIM)
    grad_pool_key = (grad_folded.T[:, :, None] * query_heads).reshape(model_width, local_dim)
    grad_pool_query = jnp.einsum("dhe,hd->he", key_heads, grad_folded, precision=highest).reshape(
        local_dim
    )
    grad_terms = SCALE * sort_into(places, own_all[:, terms_start:], True)
    grad_patch, grad_slot = table_call(
        order,
        grad_terms.reshape(narrow_size * heads, -1),
        feed_all,
        products,
        pieces,
    )
    return (
        block_out,
        grad_variables,
        grad_patch,
        grad_slot,
        grad_pool_query,
        grad_pool_key,
        grad_pool_value,
        grad_value_shift,
        grad_pool_output,
        grad_pool_bias,
        grad_first_gain,
        grad_first_shift,
        grad_triple,
        grad_query_bias,
        grad_value_bias,
        grad_self_output,
        grad_output_bias,
        grad_second_gain,
        grad_second_shift,
        grad_feed_up,
        grad_up_bias,
        grad_feed_down,
        grad_down_bias,
    )


def solution(mesh):
    wide_size, narrow_size = mesh.shape["wide"], mesh.shape["narrow"]

    def body(*arrays):
        return on_device(wide_size, narrow_size, *arrays)

    return jax.shard_map(
        body,
        mesh=mesh,
        in_specs=(
            P(None, "wide", None),
            P(),
            P(None, "wide", None),
            P(),
            P(),
            P("narrow"),
            P(None, "narrow"),
            P(None, "narrow"),
            P("narrow"),
            P("narrow", None),
            P(),
            P(),
            P(),
            P(None, None, "narrow"),
            P("narrow"),
            P("narrow"),
            P("narrow", None),
            P(),
            P(),
            P(),
            P(None, "narrow"),
            P("narrow"),
            P("narrow", None),
            P(),
        ),
        out_specs=(
            P(None, "wide", None),
            P(None, "wide", None),
            P(),
            P(),
            P("narrow"),
            P(None, "narrow"),
            P(None, "narrow"),
            P("narrow"),
            P("narrow", None),
            P(),
            P(),
            P(),
            P(None, None, "narrow"),
            P("narrow"),
            P("narrow"),
            P("narrow", None),
            P(),
            P(),
            P(),
            P(None, "narrow"),
            P("narrow"),
            P("narrow", None),
            P(),
        ),
        check_vma=False,
    )
```

time: 4150 us -> 721 us (0.17)
  waiting for transfers between devices: 3170 us -> 240 us
  matrix products: 430 us -> 5.86 us
  other arithmetic: 302 us -> 20.9 us
  Pallas kernels: 0 us -> 248 us
  local copies, waits for them, and re-layouts: 207 us -> 76.6 us
  starting transfers between devices: 0.37 us -> 104 us
    psum x7 -> x0, waiting for transfers between devices: 3020 us -> none  [the longest x5 2840 us: reduce_to(): return lax.psum(partial_value, 'narrow')]
    dot_general x34 -> x4, matrix products: 430 us -> 4.61 us  [dot(): lax.dot_general(left, right, (dims, ((), ())), precision=precision, prefe...]
    pallas_call x0 -> x83, Pallas kernels: none -> 248 us  [call(): pl.pallas_call(body, grid_spec=pltpu.PrefetchScalarGridSpec(num_scalar_pr...]
    ppermute x0 -> x102, waiting for transfers between devices: none -> 240 us  [move(): return lax.ppermute(tensor, AXES, pairs)]
    reduce_sum x17 -> x2, other arithmetic: 155 us -> 0.4 us  [sort_into(): return jnp.sum(jnp.where(same[:, :, None], tensor[None], 0.0), 1)]
    ppermute x0 -> x102, starting transfers between devices: none -> 104 us  [move(): return lax.ppermute(tensor, AXES, pairs)]
    convert_element_type x9 -> x1, other arithmetic: 96.4 us -> 0.14 us  [finish(): first = jnp.where(self.ring.core == 0, self.current, other).astype(F32)]
    reduce_scatter x1 -> x0, waiting for transfers between devices: 95.9 us -> none  [on_device(): lax.psum_scatter(grad_pair, 'wide', scatter_dimension=1, tiled=True)]
  transfers between devices with their start and end apart: 9 -> 103, of which waited for: 9 -> 38; matrix products, arithmetic and copies ran while one was open for 5% -> 8% of each run, Pallas kernels for 0% -> 32%
where the time goes in v2:
time: 721 us; the launch traced here: 713 us
  Pallas kernels  248 us (34%)
  waiting for transfers between devices  240 us (33%)
  starting transfers between devices  104 us (14%)
  local copies, waits for them, and re-layouts  76.6 us (11%)
  other arithmetic  20.9 us (3%)
  between operations  17.1 us (2%)
    pallas_call x83, Pallas kernels, call(): pl.pallas_call(body, grid_spec=pltpu.PrefetchScalarGridSpec(num_scalar_pr...  248 us
    ppermute x102, waiting for transfers between devices, move(): return lax.ppermute(tensor, AXES, pairs)  240 us
    ppermute x102, starting transfers between devices, move(): return lax.ppermute(tensor, AXES, pairs)  104 us
    unnamed x425, local copies, waits for them, and re-layouts  48.5 us
  transfers between devices with their start and end apart: 103, of which 38 were waited for; matrix products, arithmetic and copies ran while one was open for 8% of the time, Pallas kernels for 32%

profile of v2, /device:TPU:0, one launch (start us, length us, event | category | flops | bytes accessed | tf_op | source)
XLA Modules:
  0.0 712.5 jit_solution(7262148151305691839)
XLA Ops:
  17.8 14.6 %collective-permute-done.refs_3_.refs_10_.refs_1_.refs_4_.refs_6_.refs_13_ = bf16[5,1024,128]{2,1,0:T(8,128)(2,1)} collective-permute-done((bf16[5,1024,128]{2,1,0:T(8,128)(2,1)S(1)}, bf16[5,1024,128]{2,1,0:T(8,128)(2,1)}, u32[]{:S(2)}, u32[]{:S(2)}) %collective-permute-start) | collective-permute-done | bytes 1310752 | tf_op jit(solution)/shard_map/ppermute | solution.py:153
  41.7 8.6 %collective-permute-done.1.refs_3_.refs_12_.refs_1_.refs_4_.refs_6_.refs_15_ = bf16[5,1024,128]{2,1,0:T(8,128)(2,1)} collective-permute-done((bf16[5,1024,128]{2,1,0:T(8,128)(2,1)}, bf16[5,1024,128]{2,1,0:T(8,128)(2,1)}, u32[]{:S(2)}, u32[]{:S(2)}) %collective-permute-start.1) | collective-permute-done | bytes 1310752 | tf_op jit(solution)/shard_map/ppermute | solution.py:153
  59.6 8.4 %collective-permute-done.2.refs_3_.refs_14_.refs_1_.refs_4_.refs_6_.refs_17_ = bf16[5,1024,128]{2,1,0:T(8,128)(2,1)S(1)} collective-permute-done((bf16[5,1024,128]{2,1,0:T(8,128)(2,1)}, bf16[5,1024,128]{2,1,0:T(8,128)(2,1)S(1)}, u32[]{:S(2)}, u32[]{:S(2)}) %collective-permute-start.2) | collective-permute-done | bytes 1310752 | tf_op jit(solution)/shard_map/ppermute | solution.py:153
  166.5 7.0 attend.5
  183.7 7.0 attend.7
  195.9 7.1 collective-permute-start.29
  208.7 10.4 %feed.4 = (bf16[512,1024]{1,0:T(8,128)(2,1)S(1)}, bf16[512,1024]{1,0:T(8,128)(2,1)S(1)}, f32[4,1,256]{2,1,0:T(1,128)S(1)}, bf16[8,256,1024]{2,1,0:T(8,128)(2,1)S(1)}) custom-call(bf16[512,1024]{1,0:T(8,128)(2,1)} %get-tuple-element.225.refs_0_, bf16[512,1024]{1,0:T(8,128)(2,1)S(1)} %copy-done.14, bf16[8,400,1024]{2,1,0:T(8,128)(2,1)} %bitcast.289), custom_call_target="tpu_custom_call" | custom-call | flops 12650000384 | tf_op jit(solution)/shard_map/feed/pallas_call | solution.py:88
  220.1 11.8 %feed.5 = (bf16[512,1024]{1,0:T(8,128)(2,1)S(1)}, bf16[512,1024]{1,0:T(8,128)(2,1)}, f32[4,1,256]{2,1,0:T(1,128)S(1)}, bf16[8,256,1024]{2,1,0:T(8,128)(2,1)S(1)}) custom-call(bf16[512,1024]{1,0:T(8,128)(2,1)S(1)} %collective-permute-done.29.refs_0_, bf16[512,1024]{1,0:T(8,128)(2,1)} %collective-permute-done.7.refs_7_.refs_1_, ...), custom_call_target="tpu_custom_call" | custom-call | flops 12650000384 | tf_op jit(solution)/shard_map/feed/pallas_call | solution.py:88
  232.8 10.7 %feed.6 = (bf16[512,1024]{1,0:T(8,128)(2,1)S(1)}, bf16[512,1024]{1,0:T(8,128)(2,1)S(1)}, f32[4,1,256]{2,1,0:T(1,128)S(1)}, bf16[8,256,1024]{2,1,0:T(8,128)(2,1)S(1)}) custom-call(bf16[512,1024]{1,0:T(8,128)(2,1)} %collective-permute-done.31.refs_0_, bf16[512,1024]{1,0:T(8,128)(2,1)S(1)} %copy-done.64, bf16[8,400,1024]{2,1,0:T(8,128)(2,1)} %bitcast.291, ...), custom_call_target="tpu_custom_call" | custom-call | flops 12650000384 | tf_op jit(solution)/shard_map/feed/pallas_call | solution.py:88
  251.1 11.4 %feed.7 = (bf16[512,1024]{1,0:T(8,128)(2,1)S(1)}, bf16[512,1024]{1,0:T(8,128)(2,1)}, f32[4,1,256]{2,1,0:T(1,128)S(1)}, bf16[8,256,1024]{2,1,0:T(8,128)(2,1)S(1)}) custom-call(bf16[512,1024]{1,0:T(8,128)(2,1)} %collective-permute-done.32.refs_0_, bf16[512,1024]{1,0:T(8,128)(2,1)S(1)} %copy-done.66, bf16[8,400,1024]{2,1,0:T(8,128)(2,1)} %bitcast.292, ...), custom_call_target="tpu_custom_call" | custom-call | flops 12650000384 | tf_op jit(solution)/shard_map/feed/pallas_call | solution.py:88
  278.8 8.3 %collective-permute-done.38.refs_0_ = bf16[256,1024]{1,0:T(8,128)(2,1)S(1)} collective-permute-done((bf16[256,1024]{1,0:T(8,128)(2,1)S(1)}, bf16[256,1024]{1,0:T(8,128)(2,1)S(1)}, u32[]{:S(2)}, u32[]{:S(2)}) %collective-permute-start.38) | collective-permute-done | bytes 524320 | tf_op jit(solution)/shard_map/ppermute | solution.py:153
  293.1 9.2 %collective-permute-done.39.refs_0_ = bf16[256,1024]{1,0:T(8,128)(2,1)} collective-permute-done((bf16[256,1024]{1,0:T(8,128)(2,1)}, bf16[256,1024]{1,0:T(8,128)(2,1)}, u32[]{:S(2)}, u32[]{:S(2)}) %collective-permute-start.39) | collective-permute-done | bytes 524320 | tf_op jit(solution)/shard_map/ppermute | solution.py:153
  329.3 15.8 %collective-permute-done.37 = bf16[512,1024]{1,0:T(8,128)(2,1)S(1)} collective-permute-done((bf16[512,1024]{1,0:T(8,128)(2,1)S(1)}, bf16[512,1024]{1,0:T(8,128)(2,1)S(1)}, u32[]{:S(2)}, u32[]{:S(2)}) %collective-permute-start.37) | collective-permute-done | bytes 1048608 | tf_op jit(solution)/shard_map/ppermute | solution.py:153
  363.3 8.1 %collective-permute-done.47.refs_6_ = bf16[512,1024]{1,0:T(8,128)(2,1)S(1)} collective-permute-done((bf16[512,1024]{1,0:T(8,128)(2,1)S(1)}, bf16[512,1024]{1,0:T(8,128)(2,1)S(1)}, u32[]{:S(2)}, u32[]{:S(2)}) %collective-permute-start.47) | collective-permute-done | bytes 1048608 | tf_op jit(solution)/shard_map/ppermute | solution.py:153
  390.8 15.3 %collective-permute-done.50.refs_6_ = bf16[512,1024]{1,0:T(8,128)(2,1)S(1)} collective-permute-done((bf16[512,1024]{1,0:T(8,128)(2,1)S(1)}, bf16[512,1024]{1,0:T(8,128)(2,1)S(1)}, u32[]{:S(2)}, u32[]{:S(2)}) %collective-permute-start.50) | collective-permute-done | bytes 1048608 | tf_op jit(solution)/shard_map/ppermute | solution.py:153
  426.0 14.9 %collective-permute-done.54.refs_7_ = bf16[512,1024]{1,0:T(8,128)(2,1)S(1)} collective-permute-done((bf16[512,1024]{1,0:T(8,128)(2,1)S(1)}, bf16[512,1024]{1,0:T(8,128)(2,1)S(1)}, u32[]{:S(2)}, u32[]{:S(2)}) %collective-permute-start.54) | collective-permute-done | bytes 1048608 | tf_op jit(solution)/shard_map/ppermute | solution.py:153
  454.2 17.6 %collective-permute-done.57 = bf16[2,2,512,128]{3,2,1,0:T(8,128)(2,1)S(1)} collective-permute-done((bf16[2,2,512,128]{3,2,1,0:T(8,128)(2,1)S(1)}, bf16[2,2,512,128]{3,2,1,0:T(8,128)(2,1)S(1)}, u32[]{:S(2)}, u32[]{:S(2)}) %collective-permute-start.57) | collective-permute-done | bytes 524320 | tf_op jit(solution)/shard_map/ppermute | solution.py:153
  482.1 13.1 %collective-permute-done.59.refs_8_ = bf16[512,1024]{1,0:T(8,128)(2,1)S(1)} collective-permute-done((bf16[512,1024]{1,0:T(8,128)(2,1)S(1)}, bf16[512,1024]{1,0:T(8,128)(2,1)S(1)}, u32[]{:S(2)}, u32[]{:S(2)}) %collective-permute-start.59) | collective-permute-done | bytes 1048608 | tf_op jit(solution)/shard_map/ppermute | solution.py:153
  523.2 7.4 %pool_back.6 = (bf16[2,1024,128]{2,1,0:T(8,128)(2,1)S(1)}, bf16[2,1024,128]{2,1,0:T(8,128)(2,1)S(1)}, f32[768,512]{1,0:T(8,128)S(1)}, f32[2,2,816]{2,1,0:T(2,128)S(1)}, f32[2,1,128]{2,1,0:T(1,128)S(1)}) custom-call(bf16[512,816]{1,0:T(8,128)(2,1)S(1)} %copy-done.146, bf16[768,512]{1,0:T(8,128)(2,1)S(1)} %copy-done.148, ...), custom_call_target="tpu_custom_call" | custom-call | flops 24149999616 | tf_op jit(solution)/shard_map/pool_back/pallas_call | solution.py:88
  542.4 7.4 %pool_back.7 = (bf16[2,1024,128]{2,1,0:T(8,128)(2,1)S(1)}, bf16[2,1024,128]{2,1,0:T(8,128)(2,1)S(1)}, bf16[512,768]{1,0:T(8,128)(2,1)S(1)}, f32[2,2,816]{2,1,0:T(2,128)S(1)}, f32[2,1,128]{2,1,0:T(1,128)S(1)}) custom-call(bf16[512,816]{1,0:T(8,128)(2,1)S(1)} %copy-done.146, bf16[768,512]{1,0:T(8,128)(2,1)S(1)} %copy-done.148, ...), custom_call_target="tpu_custom_call" | custom-call | flops 24149999616 | tf_op jit(solution)/shard_map/pool_back/pallas_call | solution.py:88
  577.8 13.4 %collective-permute-done.75.refs_2_ = bf16[512,768]{1,0:T(8,128)(2,1)S(1)} collective-permute-done((bf16[512,768]{1,0:T(8,128)(2,1)S(1)}, bf16[512,768]{1,0:T(8,128)(2,1)S(1)}, u32[]{:S(2)}, u32[]{:S(2)}) %collective-permute-start.75) | collective-permute-done | bytes 786464 | tf_op jit(solution)/shard_map/ppermute | solution.py:153
  597.7 15.8 %collective-permute-done.85 = f32[214,128]{1,0:T(8,128)S(1)} collective-permute-done((f32[214,128]{1,0:T(8,128)S(1)}, f32[214,128]{1,0:T(8,128)S(1)}, u32[]{:S(2)}, u32[]{:S(2)}) %collective-permute-start.85) | collective-permute-done | bytes 109600 | tf_op jit(solution)/shard_map/ppermute | solution.py:153
  634.3 7.5 %collective-permute-done.87 = f32[214,128]{1,0:T(8,128)S(1)} collective-permute-done((f32[214,128]{1,0:T(8,128)S(1)}, f32[214,128]{1,0:T(8,128)S(1)}, u32[]{:S(2)}, u32[]{:S(2)}) %collective-permute-start.87) | collective-permute-done | bytes 109600 | tf_op jit(solution)/shard_map/ppermute | solution.py:153
  683.1 9.6 %table_back.1 = (f32[768,1024]{1,0:T(8,128)}, f32[48,1024]{1,0:T(8,128)}) custom-call(s32[8]{0:T(128)S(1)} %stack.359.refs_0_, f32[16,816]{1,0:T(8,128)S(1)} %mul.269.refs_1_, bf16[8,400,1024]{2,1,0:T(8,128)(2,1)S(1)} %bitcast.295, bf16[816,128]{1,0:T(8,128)(2,1)S(1)} %slice_bitcast_fusion.1.refs_0_.refs_3_, ...), custom_call_target="tpu_custom_call" | custom-call | flops 10350000128 | tf_op jit(solution)/shard_map/table_back/pallas_call | solution.py:88
  (778 shorter events, 435.1 us)
Async XLA Ops:
  7.3 200.2 %all-gather.3.cloned.1.call-start = ((), (), s32[]{:S(2)}) async-start(), calls=%async_computation | async-start | bytes 7372800 | tf_op jit(solution)/shard_map/all_gather | solution.py:1263
  35.7 41.4 %collective-permute-start.8 = (bf16[512,1024]{1,0:T(8,128)(2,1)S(1)}, bf16[512,1024]{1,0:T(8,128)(2,1)S(1)}, u32[]{:S(2)}, u32[]{:S(2)}) collective-permute-start(bf16[512,1024]{1,0:T(8,128)(2,1)S(1)} %dynamic-slice_bitcast_fusion.refs_6_.refs_1_.refs_2_), channel_id=1, source_target_pairs={{0,16},{1,17},{2,18},{3,19},{4,20},{5,21},{6,22},{7,23},{8,24},{9,... | collective-permute-start | bytes 3145736 | tf_op jit(solution)/shard_map/ppermute | solution.py:153
  54.7 27.2 %collective-permute-start.9 = (bf16[512,1024]{1,0:T(8,128)(2,1)}, bf16[512,1024]{1,0:T(8,128)(2,1)S(1)}, u32[]{:S(2)}, u32[]{:S(2)}) collective-permute-start(bf16[512,1024]{1,0:T(8,128)(2,1)} %collective-permute-done.7.refs_7_.refs_1_), channel_id=1, source_target_pairs={{0,16},{1,17},{2,18},{3,19},{4,20},{5,21},{6,22},{7,23},{8,24},{9,... | collective-permute-start | bytes 3145736 | tf_op jit(solution)/shard_map/ppermute | solution.py:153
  123.2 40.7 %collective-permute-start.13 = (bf16[2,2,512,128]{3,2,1,0:T(8,128)(2,1)S(1)}, bf16[2,2,512,128]{3,2,1,0:T(8,128)(2,1)S(1)}, u32[]{:S(2)}, u32[]{:S(2)}) collective-permute-start(bf16[2,2,512,128]{3,2,1,0:T(8,128)(2,1)S(1)} %get-tuple-element.211.refs_1_.refs_4_), channel_id=1, source_target_pairs={{0,8},{1,9},{2,10},{3,11},{4,12},{5,13},{6,14},{7,15},{8,0},{9,1},... | collective-permute-start | bytes 1572872 | tf_op jit(solution)/shard_map/ppermute | solution.py:153
  163.9 27.5 %collective-permute-start.26 = (bf16[128,1024]{1,0:T(8,128)(2,1)S(1)}, bf16[128,1024]{1,0:T(8,128)(2,1)S(1)}, u32[]{:S(2)}, u32[]{:S(2)}) collective-permute-start(bf16[128,1024]{1,0:T(8,128)(2,1)S(1)} %get-tuple-element.220.refs_7_.refs_3_), channel_id=1, source_target_pairs={{0,8},{1,9},{2,10},{3,11},{4,12},{5,13},{6,14},{7,15},{8,0},{9,1},... | collective-permute-start | bytes 786440 | tf_op jit(solution)/shard_map/ppermute | solution.py:153
  203.0 29.9 %collective-permute-start.31 = (bf16[512,1024]{1,0:T(8,128)(2,1)}, bf16[512,1024]{1,0:T(8,128)(2,1)}, u32[]{:S(2)}, u32[]{:S(2)}) collective-permute-start(bf16[512,1024]{1,0:T(8,128)(2,1)} %get-tuple-element.225.refs_0_), channel_id=1, source_target_pairs={{0,16},{1,17},{2,18},{3,19},{4,20},{5,21},{6,22},{7,23},{8,24},{9,... | collective-permute-start | bytes 3145736 | tf_op jit(solution)/shard_map/ppermute | solution.py:153
  205.4 45.7 %collective-permute-start.32 = (bf16[512,1024]{1,0:T(8,128)(2,1)S(1)}, bf16[512,1024]{1,0:T(8,128)(2,1)}, u32[]{:S(2)}, u32[]{:S(2)}) collective-permute-start(bf16[512,1024]{1,0:T(8,128)(2,1)S(1)} %collective-permute-done.29.refs_0_), channel_id=1, source_target_pairs={{0,16},{1,17},{2,18},{3,19},{4,20},{5,21},{6,22},{7,23},{8,24},{9,... | collective-permute-start | bytes 3145736 | tf_op jit(solution)/shard_map/ppermute | solution.py:153
  278.6 27.5 %collective-permute-start.34 = (bf16[512,1024]{1,0:T(8,128)(2,1)}, bf16[512,1024]{1,0:T(8,128)(2,1)}, u32[]{:S(2)}, u32[]{:S(2)}) collective-permute-start(bf16[512,1024]{1,0:T(8,128)(2,1)} %get-tuple-element.234), channel_id=1, source_target_pairs={{0,16},{1,17},{2,18},{3,19},{4,20},{5,21},{6,22},{7,23},{8,24},{9,... | collective-permute-start | bytes 3145736 | tf_op jit(solution)/shard_map/ppermute | solution.py:153
  327.2 35.6 %collective-permute-start.45 = (bf16[256,1024]{1,0:T(8,128)(2,1)S(1)}, bf16[256,1024]{1,0:T(8,128)(2,1)S(1)}, u32[]{:S(2)}, u32[]{:S(2)}) collective-permute-start(bf16[256,1024]{1,0:T(8,128)(2,1)S(1)} %get-tuple-element.258), channel_id=1, source_target_pairs={{0,2},{1,0},{2,4},{3,1},{4,6},{5,3},{6,7},{7,5},{8,10},{9,8},{10,1... | collective-permute-start | bytes 1572872 | tf_op jit(solution)/shard_map/ppermute | solution.py:153
  329.0 33.8 %collective-permute-start.44 = (bf16[256,1024]{1,0:T(8,128)(2,1)S(1)}, bf16[256,1024]{1,0:T(8,128)(2,1)S(1)}, u32[]{:S(2)}, u32[]{:S(2)}) collective-permute-start(bf16[256,1024]{1,0:T(8,128)(2,1)S(1)} %get-tuple-element.257.refs_5_), channel_id=1, source_target_pairs={{0,1},{1,3},{2,0},{3,5},{4,2},{5,7},{6,4},{7,6},{8,9},{9,11},{10,8... | collective-permute-start | bytes 1572872 | tf_op jit(solution)/shard_map/ppermute | solution.py:153
  362.3 61.4 %collective-permute-start.52 = (bf16[2,2,512,128]{3,2,1,0:T(8,128)(2,1)S(1)}, bf16[2,2,512,128]{3,2,1,0:T(8,128)(2,1)S(1)}, u32[]{:S(2)}, u32[]{:S(2)}) collective-permute-start(bf16[2,2,512,128]{3,2,1,0:T(8,128)(2,1)S(1)} %bitcast.312), channel_id=1, source_target_pairs={{0,16},{1,17},{2,18},{3,19},{4,20},{5,21},{6,22},{7,23},{8,24},{9,... | collective-permute-start | bytes 1572872 | tf_op jit(solution)/shard_map/ppermute | solution.py:153
  363.1 62.5 %collective-permute-start.99 = (bf16[256,1024]{1,0:T(8,128)(2,1)S(1)}, bf16[256,1024]{1,0:T(8,128)(2,1)S(1)}, u32[]{:S(2)}, u32[]{:S(2)}) collective-permute-start(bf16[256,1024]{1,0:T(8,128)(2,1)S(1)} %add.533.refs_5_.refs_1_), channel_id=1, source_target_pairs={{0,8},{1,9},{2,10},{3,11},{4,12},{5,13},{6,14},{7,15},{8,0},{9,1},... | collective-permute-start | bytes 1572872 | tf_op jit(solution)/shard_map/ppermute | solution.py:153
  423.2 92.9 %collective-permute-start.100 = (bf16[256,1024]{1,0:T(8,128)(2,1)S(1)}, bf16[256,1024]{1,0:T(8,128)(2,1)S(1)}, u32[]{:S(2)}, u32[]{:S(2)}) collective-permute-start(bf16[256,1024]{1,0:T(8,128)(2,1)S(1)} %add.533.refs_5_.refs_1_), channel_id=1, source_target_pairs={{0,16},{1,17},{2,18},{3,19},{4,20},{5,21},{6,22},{7,23},{8,24},{9,... | collective-permute-start | bytes 1572872 | tf_op jit(solution)/shard_map/ppermute | solution.py:153
  425.5 90.7 %collective-permute-start.101 = (bf16[256,1024]{1,0:T(8,128)(2,1)S(1)}, bf16[256,1024]{1,0:T(8,128)(2,1)S(1)}, u32[]{:S(2)}, u32[]{:S(2)}) collective-permute-start(bf16[256,1024]{1,0:T(8,128)(2,1)S(1)} %collective-permute-done.99.refs_2_), channel_id=1, source_target_pairs={{0,16},{1,17},{2,18},{3,19},{4,20},{5,21},{6,22},{7,23},{8,24},{9,... | collective-permute-start | bytes 1572872 | tf_op jit(solution)/shard_map/ppermute | solution.py:153
  440.9 30.9 %collective-permute-start.57 = (bf16[2,2,512,128]{3,2,1,0:T(8,128)(2,1)S(1)}, bf16[2,2,512,128]{3,2,1,0:T(8,128)(2,1)S(1)}, u32[]{:S(2)}, u32[]{:S(2)}) collective-permute-start(bf16[2,2,512,128]{3,2,1,0:T(8,128)(2,1)S(1)} %bitcast.317), channel_id=1, source_target_pairs={{0,16},{1,17},{2,18},{3,19},{4,20},{5,21},{6,22},{7,23},{8,24},{9,... | collective-permute-start | bytes 1572872 | tf_op jit(solution)/shard_map/ppermute | solution.py:153
  441.2 40.7 %collective-permute-start.56 = (bf16[2,2,512,128]{3,2,1,0:T(8,128)(2,1)S(1)}, bf16[2,2,512,128]{3,2,1,0:T(8,128)(2,1)S(1)}, u32[]{:S(2)}, u32[]{:S(2)}) collective-permute-start(bf16[2,2,512,128]{3,2,1,0:T(8,128)(2,1)S(1)} %bitcast.319), channel_id=1, source_target_pairs={{0,16},{1,17},{2,18},{3,19},{4,20},{5,21},{6,22},{7,23},{8,24},{9,... | collective-permute-start | bytes 1572872 | tf_op jit(solution)/shard_map/ppermute | solution.py:153
  449.3 71.0 %collective-permute-start.62 = (bf16[4,1024,128]{2,1,0:T(8,128)(2,1)S(1)}, bf16[4,1024,128]{2,1,0:T(8,128)(2,1)S(1)}, u32[]{:S(2)}, u32[]{:S(2)}) collective-permute-start(bf16[4,1024,128]{2,1,0:T(8,128)(2,1)S(1)} %get-tuple-element.316), channel_id=1, source_target_pairs={{2,0},{0,1},{4,2},{1,3},{6,4},{3,5},{7,6},{5,7},{9,8},{11,9},{8,10... | collective-permute-start | bytes 3145736 | tf_op jit(solution)/shard_map/ppermute | solution.py:153
  481.9 38.4 %collective-permute-start.63 = (bf16[4,1024,128]{2,1,0:T(8,128)(2,1)S(1)}, bf16[4,1024,128]{2,1,0:T(8,128)(2,1)S(1)}, u32[]{:S(2)}, u32[]{:S(2)}) collective-permute-start(bf16[4,1024,128]{2,1,0:T(8,128)(2,1)S(1)} %get-tuple-element.318), channel_id=1, source_target_pairs={{0,8},{1,9},{2,10},{3,11},{4,12},{5,13},{6,14},{7,15},{8,0},{9,1},... | collective-permute-start | bytes 3145736 | tf_op jit(solution)/shard_map/ppermute | solution.py:153
  553.5 66.4 %collective-permute-start.94 = (bf16[4,1024,128]{2,1,0:T(8,128)(2,1)}, bf16[4,1024,128]{2,1,0:T(8,128)(2,1)}, u32[]{:S(2)}, u32[]{:S(2)}) collective-permute-start(bf16[4,1024,128]{2,1,0:T(8,128)(2,1)} %get-tuple-element.363), channel_id=1, source_target_pairs={{0,8},{1,9},{2,10},{3,11},{4,12},{5,13},{6,14},{7,15},{8,0},{9,1},... | collective-permute-start | bytes 3145736 | tf_op jit(solution)/shard_map/ppermute | solution.py:153
  554.7 66.8 %collective-permute-start.93 = (bf16[4,1024,128]{2,1,0:T(8,128)(2,1)}, bf16[4,1024,128]{2,1,0:T(8,128)(2,1)}, u32[]{:S(2)}, u32[]{:S(2)}) collective-permute-start(bf16[4,1024,128]{2,1,0:T(8,128)(2,1)} %bitcast.67.refs_3_), channel_id=1, source_target_pairs={{2,0},{0,1},{4,2},{1,3},{6,4},{3,5},{7,6},{5,7},{9,8},{11,9},{8,10... | collective-permute-start | bytes 3145736 | tf_op jit(solution)/shard_map/ppermute | solution.py:153
  593.2 67.1 %collective-permute-start.77 = (bf16[512,768]{1,0:T(8,128)(2,1)}, bf16[512,768]{1,0:T(8,128)(2,1)S(1)}, u32[]{:S(2)}, u32[]{:S(2)}) collective-permute-start(bf16[512,768]{1,0:T(8,128)(2,1)} %get-tuple-element.335), channel_id=1, source_target_pairs={{0,2},{1,0},{2,4},{3,1},{4,6},{5,3},{6,7},{7,5},{8,10},{9,8},{10,1... | collective-permute-start | bytes 2359304 | tf_op jit(solution)/shard_map/ppermute | solution.py:153
  617.8 42.4 %collective-permute-start.78 = (bf16[512,768]{1,0:T(8,128)(2,1)S(1)}, bf16[512,768]{1,0:T(8,128)(2,1)S(1)}, u32[]{:S(2)}, u32[]{:S(2)}) collective-permute-start(bf16[512,768]{1,0:T(8,128)(2,1)S(1)} %get-tuple-element.336), channel_id=1, source_target_pairs={{0,1},{1,3},{2,0},{3,5},{4,2},{5,7},{6,4},{7,6},{8,9},{9,11},{10,8... | collective-permute-start | bytes 2359304 | tf_op jit(solution)/shard_map/ppermute | solution.py:153
  625.6 37.5 %collective-permute-start.95 = (bf16[4,1024,128]{2,1,0:T(8,128)(2,1)}, bf16[4,1024,128]{2,1,0:T(8,128)(2,1)}, u32[]{:S(2)}, u32[]{:S(2)}) collective-permute-start(bf16[4,1024,128]{2,1,0:T(8,128)(2,1)} %bitcast.192), channel_id=1, source_target_pairs={{2,0},{0,1},{4,2},{1,3},{6,4},{3,5},{7,6},{5,7},{9,8},{11,9},{8,10... | collective-permute-start | bytes 3145736 | tf_op jit(solution)/shard_map/ppermute | solution.py:153
  627.9 51.3 %collective-permute-start.90 = (bf16[816,128]{1,0:T(8,128)(2,1)S(1)}, bf16[816,128]{1,0:T(8,128)(2,1)S(1)}, u32[]{:S(2)}, u32[]{:S(2)}) collective-permute-start(bf16[816,128]{1,0:T(8,128)(2,1)S(1)} %collective-permute-done.76.refs_0_.refs_5_.refs_2_), channel_id=1, source_target_pairs={{0,8},{1,9},{2,10},{3,11},{4,12},{5,13},{6,14},{7,15},{8,0},{9,1},... | collective-permute-start | bytes 626696 | tf_op jit(solution)/shard_map/ppermute | solution.py:153
  (288 other events, 3124.6 us)
Sparse Core Ops, SparseCore 0:
  97.4 109.9 all-gather.2

commit v3 on v2

--- a/solution.py
+++ b/solution.py
@@ -141,6 +141,9 @@
         self.forward = [(flat(w, n), flat(w, step(n, 1))) for w, n in every]
         self.backward = [(flat(w, n), flat(w, step(n, -1))) for w, n in every]
         self.by_core = [(flat(w, n), flat(w, step(n, 1 - 2 * (w % 2)))) for w, n in every]
+        self.far_by_core = lambda hops: [
+            (flat(w, n), flat(w, step(n, hops * (1 - 2 * (w % 2))))) for w, n in every
+        ]
         self.by_core_back = [(dst, src) for src, dst in self.by_core]
         self.wide_swap = {
             bit: [(flat(w, n), flat(w ^ bit, n)) for w, n in every] for bit in bits(wide_size)
@@ -261,16 +264,20 @@
         self.ring, self.current, self.own = ring, block, block
         self.pairs, self.far = [], None
 
-    def step(self, *earlier):
-        ring = self.ring
-        self.current = ring.move(self.current, ring.by_core)
-        if earlier:
-            (self.current,) = pass_on([self.current], *earlier)
+    def send(self):
+        self.moved = self.ring.move(self.current, self.ring.by_core)
+
+    def take(self, moved):
+        ring, self.current = self.ring, moved
         if 2 * (len(self.pairs) + 1) < ring.narrow:
             self.pairs.append(ring.ordered(self.current, ring.swap(self.current)))
             return self.pairs[-1]
         self.far = self.current
         return [self.far]
+
+    def step(self, *earlier):
+        self.send()
+        return self.take(pass_on([self.moved], *earlier)[0] if earlier else self.moved)
 
     def finish(self):
         while self.far is None:
@@ -301,6 +308,13 @@
         return self.ahead
 
 
+def gather_direct(ring, block):
+    half = ring.narrow // 2
+    came = [ring.move(block, ring.far_by_core(hops)) for hops in range(1, half + 1)]
+    pairs = [ring.ordered(piece, ring.swap(piece)) for piece in came[:-1]]
+    return [block, came[-1]] + [piece for pair in pairs for piece in pair]
+
+
 class GatherOwn:
     def __init__(self, ring, block, dtype):
         self.ring, self.hops, self.dtype = ring, 0, dtype
@@ -330,7 +344,7 @@
         return got
 
     def after(self, *earlier):
-        self.moving = list(pass_on(self.moving, *earlier))
+        self.moving = self.handed = list(pass_on(self.moving, *earlier))
         self.place()
 
     def finish(self):
@@ -370,7 +384,7 @@
     def finish(self):
         while self.bits:
             self.step()
-        other = self.ring.swap(self.current)
+        self.other = other = self.ring.swap(self.current)
         first = jnp.where(self.ring.core == 0, self.current, other).astype(F32)
         second = jnp.where(self.ring.core == 0, other, self.current).astype(F32)
         return first, second
@@ -381,9 +395,16 @@
         self.ring, self.current = ring, tensor
         self.pairs = list(ring.wide_swap.values()) + list(ring.narrow_swap.values())
 
+    def send(self):
+        self.moved = self.ring.move(self.current, self.pairs.pop(0))
+
+    def take(self, *earlier):
+        moved = pass_on([self.moved], *earlier)[0] if earlier else self.moved
+        self.current = self.current + moved
+
     def step(self):
-        self.current = self.current + self.ring.move(self.current, self.pairs.pop(0))
-        return self.current
+        self.send()
+        self.take()
 
     def finish(self):
         while self.pairs:
@@ -703,7 +724,7 @@
             struct((depth, tokens), BF16),
         ],
         us=7,
-        mib=40,
+        mib=56,
         name="enter",
     )(*pooled, *pieces, bias, gain, shift)
 
@@ -1007,32 +1028,68 @@
     )(queries, grads, totals, deltas, *sources, *([] if first else [before]))
 
 
-def feed_kernel(first, cols, x_ref, g_ref, w_ref, *refs):
-    if not first:
-        before_ref, refs = refs[0], refs[1:]
-    y_ref, gx_ref, gb_ref, gw_ref, y_sum, gx_sum = refs
+def feed_parts(w_ref, cols):
     hidden = (w_ref.shape[1] - 16 - cols) // 2
-    step = pl.program_id(0)
-
-    @pl.when(step == 0)
-    def _():
-        y_sum[...] = jnp.zeros_like(y_sum)
-        gx_sum[...] = jnp.zeros_like(gx_sum)
-
     rows_of = lambda start: jnp.concatenate([w_ref[i, start : start + hidden] for i in range(2)], 0)
-    up, down = rows_of(cols), rows_of(cols + hidden)
     bias = []
     for i in range(2):
         rows = w_ref[i, cols + 2 * hidden :, :hidden].astype(F32)
         bias.append(rows[0:1] + (rows[1:2] + rows[2:3]))
+    return rows_of(cols), rows_of(cols + hidden), jnp.concatenate(bias, 1)
+
+
+def gate_of(before):
+    return 0.5 * (1.0 + lax.erf(before * 0.7071067811865476))
+
+
+def feed_kernel(cols, x_ref, w_ref, y_ref, y_sum):
+    step = pl.program_id(0)
+    up, down, bias = feed_parts(w_ref, cols)
+    before = dot(x_ref[...], up, NT) + bias
+    part = dot(low(before * gate_of(before)), down)
+
+    @pl.when(step == 0)
+    def _():
+        y_sum[...] = part
+
+    @pl.when(step > 0)
+    def _():
+        y_sum[...] += part
+
+    @pl.when(step == pl.num_programs(0) - 1)
+    def _():
+        y_ref[...] = low(y_sum[...])
+
+
+def feed_call(cols, rows, staged):
+    whole = fixed(rows.shape)
+    return pallas(
+        lambda *refs: feed_kernel(cols, *refs),
+        grid=(staged.shape[0] // 2,),
+        in_specs=[whole, pl.BlockSpec((2,) + staged.shape[1:], lambda n: (n, 0, 0))],
+        out_specs=whole,
+        out_shape=struct(rows.shape, BF16),
+        scratch_shapes=[pltpu.VMEM(rows.shape, F32)],
+        us=4,
+        mib=40,
+        name="feed",
+    )(rows, staged)
+
+
+def feed_back_kernel(first, cols, x_ref, g_ref, w_ref, *refs):
+    if not first:
+        before_ref, refs = refs[0], refs[1:]
+    gx_ref, gb_ref, gw_ref, gx_sum = refs
+    step = pl.program_id(0)
+    up, down, bias = feed_parts(w_ref, cols)
+    hidden = up.shape[0] // 2
     rows, grads = x_ref[...], g_ref[...]
-    before = dot(rows, up, NT) + jnp.concatenate(bias, 1)
-    bell = 0.5 * (1.0 + lax.erf(before * 0.7071067811865476))
+    before = dot(rows, up, NT) + bias
+    bell = gate_of(before)
     active = low(before * bell)
     slope = bell + before * (0.3989422804014327 * jnp.exp(-0.5 * before * before))
     grad_hidden = low(slope * dot(grads, down, NT))
-    y_sum[...] += dot(active, down)
-    gx_sum[...] += dot(grad_hidden, up)
+    part_sum = dot(grad_hidden, up)
     grad_up = dot(grad_hidden, rows, TN)
     grad_down = dot(active, grads, TN)
     gb_ref[0] = jnp.sum(grad_hidden.astype(F32), 0, keepdims=True)
@@ -1042,35 +1099,40 @@
         made = made if first else made + before_ref[i].astype(F32)
         gw_ref[i] = low(made)
 
+    @pl.when(step == 0)
+    def _():
+        gx_sum[...] = part_sum
+
+    @pl.when(step > 0)
+    def _():
+        gx_sum[...] += part_sum
+
     @pl.when(step == pl.num_programs(0) - 1)
     def _():
-        y_ref[...] = low(y_sum[...])
         gx_ref[...] = low(gx_sum[...])
 
 
-def feed_call(cols, rows, grads, staged, before):
+def feed_back_call(cols, rows, grads, staged, before):
     count, lines, depth = staged.shape
-    tokens = rows.shape[0]
     lines = lines - 16 - cols
-    whole = fixed((tokens, depth))
+    whole = fixed(rows.shape)
     pair = pl.BlockSpec((2, lines, depth), lambda n: (n, 0, 0))
     first = before is None
     return pallas(
-        lambda *refs: feed_kernel(first, cols, *refs),
+        lambda *refs: feed_back_kernel(first, cols, *refs),
         grid=(count // 2,),
         in_specs=[whole, whole, pl.BlockSpec((2,) + staged.shape[1:], lambda n: (n, 0, 0))]
         + ([] if first else [pair]),
-        out_specs=[whole, whole, pl.BlockSpec((1, 1, lines), lambda n: (n, 0, 0)), pair],
+        out_specs=[whole, pl.BlockSpec((1, 1, lines), lambda n: (n, 0, 0)), pair],
         out_shape=[
-            struct((tokens, depth), BF16),
-            struct((tokens, depth), BF16),
+            struct(rows.shape, BF16),
             struct((count // 2, 1, lines), F32),
             struct((count, lines, depth), BF16),
         ],
-        scratch_shapes=[pltpu.VMEM((tokens, depth), F32), pltpu.VMEM((tokens, depth), F32)],
-        us=11,
+        scratch_shapes=[pltpu.VMEM(rows.shape, F32)],
+        us=9,
         mib=40,
-        name="feed",
+        name="feed_back",
     )(rows, grads, staged, *([] if first else [before]))
 
 
@@ -1176,6 +1238,7 @@
         out_specs=[fixed((width, depth)), fixed((VARS, depth))],
         out_shape=[struct((width, depth), F32), struct((VARS, depth), F32)],
         us=9,
+        mib=56,
         name="table_back",
     )(order, terms, values, *products, *pieces)
 
@@ -1309,40 +1372,45 @@
 
     all_rows = ring.gather_wide(normed_two)
     y_all, gx_all, gb_all, grad_feed = [], [], [], None
-    for index in range(wide_size):
-        if grad_feed is not None:
-            wait_for(gx_all[-1])
-        got = feed_call(
+    near = max(1, wide_size // 2)
+    plan = [(False, i) for i in range(near)] + [(True, 0)]
+    plan += [(False, i) for i in range(near, wide_size)]
+    plan += [(True, i) for i in range(1, wide_size)]
+    latest = None
+    for way_back, index in plan:
+        if latest is not None:
+            wait_for(latest)
+        if not way_back:
+            y_all.append(feed_call(local_dim, all_rows[index], feed_all))
+            latest = y_all[-1]
+            if index == wide_size - 1:
+                y_parts = ring.scatter_wide(y_all)
+                block_own = y_parts[0].astype(F32) + y_parts[1].astype(F32)
+                block_own = low(stream_one + down_bias + block_own)
+            continue
+        if index == wide_size - 1:
+            wait_for(block_own)
+        got = feed_back_call(
             local_dim, all_rows[index], all_grads[index], feed_all, grad_feed
         )
-        y_all.append(got[0])
-        gx_all.append(got[1])
-        gb_all.append(got[2])
-        grad_feed = got[3]
+        gx_all.append(got[0])
+        gb_all.append(got[1])
+        grad_feed = got[2]
+        latest = got[0]
+    gather_out = GatherOwn(ring, block_own, BF16)
     scatter_feed = ScatterOwn(ring, grad_feed)
     grad_parts = ring.scatter_wide(gx_all)
-    wait_for(grad_parts[0])
-    for _ in range(narrow_size // 2 - 2):
-        scatter_feed.step()
-    y_parts = ring.scatter_wide(pass_on(y_all, grad_parts[1]))
     grad_up_bias = sum(gb_all).reshape(narrow_size, quarter)
-    wait_for(scatter_feed.ahead)
     grad_stream_one, grad_one, grad_one_t, sums_two = turn_call(
         grad_parts, grads, stream_one, row(second_gain)
     )
-    block_own = low(stream_one + down_bias + (y_parts[0].astype(F32) + y_parts[1].astype(F32)))
-    gather_out = GatherOwn(ring, block_own, BF16)
 
     waiting = {}
     backward = [0] + list(range(groups - 1, 0, -1))
     for turn, g in enumerate(backward):
-        if turn == 1:
-            wait_for(block_own)
-        back = lambda: middle_back_call(
+        grad_attended, deltas, *grad_pair_mixers = middle_back_call(
             grad_one, grad_one_t, attended[g], pair_of(self_pieces, g)
         )
-        got = gather_out.beside(back) if turn in (2, 3) else back()
-        grad_attended, deltas, *grad_pair_mixers = got
         back = lambda chosen, before, last, together: attend_back_call(
             queries[g],
             grad_attended,
@@ -1371,8 +1439,8 @@
             grad_pair = [far]
         waiting[g] = (grad_query, grad_pair, grad_pair_mixers)
         wait_for(far)
-        if turn < 2:
-            wait_for(scatter_feed.step())
+        if turn in (0, 2):
+            wait_for(gather_out.beside(scatter_feed.step))
     grad_normed_one, grad_pieces, sums_triple = None, {}, [None] * groups
     for turn, g in enumerate(backward):
         grad_query, grad_pair, grad_pair_mixers = waiting[g]
@@ -1387,7 +1455,9 @@
             grad_pair_mixers,
             grad_normed_one,
         )
-        made, grad_normed_one, sums = gather_out.beside(back) if turn in (0, 3) else back()
+        if turn == 3:
+            wait_for(gather_out.beside(scatter_feed.step))
+        made, grad_normed_one, sums = back()
         grad_pieces[g], sums_triple[g] = made, sums
     scatter = ScatterShared(ring, *grad_pieces[0])
     grad_zero, grad_zero_t, sums_one = leave_call(
@@ -1411,6 +1481,9 @@
             grad_pixels,
             turn == groups - 1,
         )
+        if turn == 1:
+            wait_for(grad_pixels)
+            wait_for(gather_out.beside(scatter_feed.step))
         made, grad_pixels, terms, shifts = back()
         if turn == 0:
             scatter_last = ScatterShared(ring, *made)
@@ -1441,44 +1514,54 @@
     own_length = own_sums.shape[1]
     shared_sums = jnp.concatenate([sums_one, sums_two], 0)
     all_sums = jnp.concatenate([own_sums.reshape(-1), shared_sums.reshape(-1)]).reshape(-1, 128)
+    adder = AddEverywhere(ring, all_sums)
+    adder.step()
+    adder.step()
     scatter_last.step(made)
-    hand_on(grad_pixels)
+    hand_on(grad_pixels, scatter.current)
     scatter_last.step()
-    gather_pixels = GatherOwn(ring, Gate.handed[0], F32)
+    grad_pixels, scatter.current = Gate.handed
+    gather_pixels = GatherOwn(ring, grad_pixels, F32)
     finish_last = FinishShared(ring, scatter_last.current)
     finish_last.step()
     finish_last.step()
     grad_pool_output, product = finish_last.finish()
     product = low(product[0, : input_width + VARS])
-    gather_product = GatherShared(ring, product)
-    adder = AddEverywhere(ring, *pass_on([all_sums], product))
-    adder.step()
-    block_out = gather_out.finish().reshape(samples, token_count, model_width)
-    gather_pixels.after(product)
-    wait_for(product)
+    products = gather_direct(ring, product)
     scatter.step(grad_pieces[backward[-1]])
-    adder.step()
-    hop = gather_product.step()[0]
-    gather_pixels.after(hop)
-    wait_for(hop)
-    scatter.step()
-    finish = FinishShared(ring, scatter.current)
-    hop = gather_product.step()[0]
-    gather_pixels.after(hop)
-    wait_for(hop)
-    finish.step()
-    finish.step()
-    products = gather_product.finish()
-    grad_feed_pieces = ring.gather_wide(scatter_feed.ahead)
+    passes = narrow_size // 2 - 1
+    for hop in range(passes):
+        gather_pixels.after()
+        if hop:
+            adder.take(gather_pixels.handed[0])
+        if adder.pairs:
+            adder.send()
+        wait_for(gather_pixels.handed[0])
+        if hop == 0:
+            scatter.step()
+            finish = FinishShared(ring, scatter.current)
+            (grad_feed_own,) = pass_on([scatter_feed.ahead], gather_pixels.handed[0])
+            grad_feed_pieces = ring.gather_wide(grad_feed_own)
+        elif finish.bits:
+            finish.step()
+        else:
+            Gate.waits = []
+        if hop == passes - 1:
+            grad_pool_output, late_product, block_out = pass_on(
+                [grad_pool_output, product, gather_out.finish()], gather_pixels.handed[0]
+            )
+    adder.take()
+    while adder.pairs:
+        adder.step()
+    block_out = block_out.reshape(samples, token_count, model_width)
+    grad_first, grad_second = finish.finish()
     grad_feed_up, grad_feed_down = assemble_call(ring.w, grad_feed_pieces)
-    grad_first, grad_second = finish.finish()
-    adder.finish()
     grad_variables = gather_pixels.finish().reshape(samples, token_count, input_width)
     grad_triple = jnp.concatenate([grad_first, grad_second[:1]], 0).transpose(1, 0, 2)
     grad_self_output = grad_second[1].T
     grad_pool_output = grad_pool_output[0].T
-    grad_pool_value = dot(patch_embed, product[:input_width], TN)
-    grad_pool_value = grad_pool_value + dot(variable_embed, product[input_width:], TN)
+    grad_pool_value = dot(patch_embed, late_product[:input_width], TN)
+    grad_pool_value = grad_pool_value + dot(variable_embed, late_product[input_width:], TN)
 
     summed = adder.current.reshape(-1)
     own_all = summed[: narrow_size * own_length].reshape(narrow_size, own_length)
@@ -1503,6 +1586,7 @@
         local_dim
     )
     grad_terms = SCALE * sort_into(places, own_all[:, terms_start:], True)
+    wait_for(finish.other, grad_pool_value, grad_feed_up)
     grad_patch, grad_slot = table_call(
         order,
         grad_terms.reshape(narrow_size * heads, -1),

time: 721 us -> 694 us (0.963)
  waiting for transfers between devices: 240 us -> 195 us
  Pallas kernels: 248 us -> 279 us
  local copies, waits for them, and re-layouts: 76.6 us -> 65.2 us
    ppermute x102, waiting for transfers between devices: 240 us -> 188 us  [move(): return lax.ppermute(tensor, AXES, pairs)]
    pallas_call x83 -> x89, Pallas kernels: 248 us -> 279 us  [call(): pl.pallas_call(body, grid_spec=pltpu.PrefetchScalarGridSpec(num_scalar_pr...]
    all_gather x1, waiting for transfers between devices: 0.01 us -> 7.4 us  [on_device(): feed_all = lax.all_gather(Gate.handed[0], 'narrow')]
    unnamed x425 -> x415, local copies, waits for them, and re-layouts: 48.5 us -> 44.7 us
  transfers between devices with their start and end apart: 103 -> 103, of which waited for: 38 -> 33; matrix products, arithmetic and copies ran while one was open for 8% -> 7% of each run, Pallas kernels for 32% -> 38%
where the time goes in v3:
time: 694 us; the launch traced here: 686 us
  Pallas kernels  279 us (40%)
  waiting for transfers between devices  195 us (28%)
  starting transfers between devices  106 us (15%)
  local copies, waits for them, and re-layouts  65.2 us (9%)
  other arithmetic  19.7 us (3%)
  between operations  16.9 us (2%)
    pallas_call x89, Pallas kernels, call(): pl.pallas_call(body, grid_spec=pltpu.PrefetchScalarGridSpec(num_scalar_pr...  279 us
    ppermute x102, waiting for transfers between devices, move(): return lax.ppermute(tensor, AXES, pairs)  188 us
    ppermute x102, starting transfers between devices, move(): return lax.ppermute(tensor, AXES, pairs)  106 us
    unnamed x415, local copies, waits for them, and re-layouts  44.7 us
  transfers between devices with their start and end apart: 103, of which 33 were waited for; matrix products, arithmetic and copies ran while one was open for 7% of the time, Pallas kernels for 38%

profile of v3, /device:TPU:0, one launch (start us, length us, event | category | flops | bytes accessed | tf_op | source)
XLA Modules:
  0.0 685.8 jit_solution(12857599259918954634)
XLA Ops:
  17.8 14.5 %collective-permute-done.refs_3_.refs_10_.refs_1_.refs_4_.refs_6_.refs_13_ = bf16[5,1024,128]{2,1,0:T(8,128)(2,1)} collective-permute-done((bf16[5,1024,128]{2,1,0:T(8,128)(2,1)S(1)}, bf16[5,1024,128]{2,1,0:T(8,128)(2,1)}, u32[]{:S(2)}, u32[]{:S(2)}) %collective-permute-start) | collective-permute-done | bytes 1310752 | tf_op jit(solution)/shard_map/ppermute | solution.py:156
  41.4 8.9 %collective-permute-done.1.refs_3_.refs_12_.refs_1_.refs_4_.refs_6_.refs_15_ = bf16[5,1024,128]{2,1,0:T(8,128)(2,1)} collective-permute-done((bf16[5,1024,128]{2,1,0:T(8,128)(2,1)}, bf16[5,1024,128]{2,1,0:T(8,128)(2,1)}, u32[]{:S(2)}, u32[]{:S(2)}) %collective-permute-start.1) | collective-permute-done | bytes 1310752 | tf_op jit(solution)/shard_map/ppermute | solution.py:156
  59.0 9.1 %collective-permute-done.2.refs_3_.refs_14_.refs_1_.refs_4_.refs_6_.refs_17_ = bf16[5,1024,128]{2,1,0:T(8,128)(2,1)S(1)} collective-permute-done((bf16[5,1024,128]{2,1,0:T(8,128)(2,1)}, bf16[5,1024,128]{2,1,0:T(8,128)(2,1)S(1)}, u32[]{:S(2)}, u32[]{:S(2)}) %collective-permute-start.2) | collective-permute-done | bytes 1310752 | tf_op jit(solution)/shard_map/ppermute | solution.py:156
  99.7 7.0 %enter.1 = (f32[512,1024]{1,0:T(8,128)}, bf16[512,1024]{1,0:T(8,128)(2,1)}, bf16[1024,512]{1,0:T(8,128)(2,1)}) custom-call(bf16[512,128]{1,0:T(8,128)(2,1)} %copy-done.169, bf16[512,128]{1,0:T(8,128)(2,1)} %copy-done.175, bf16[512,128]{1,0:T(8,128)(2,1)} %copy-done.161, bf16[512,128]{1,0:T(8,128)(2,1)} %copy-done.163, bf16[512,128]{1,0:T(8,128)(2,1)} %copy-done.165, ...), custom_call_target="tpu_custom_call" | custom-call | flops 8049999872 | tf_op jit(solution)/shard_map/enter/pallas_call | solution.py:88
  201.2 7.4 %all-gather.3.cloned.1.call-done = bf16[3200,1024]{1,0:T(8,128)(2,1)} async-done(((bf16[400,1024]{1,0:T(8,128)(2,1)}), bf16[3200,1024]{1,0:T(8,128)(2,1)}) %all-gather.3.cloned.1.call-update) | async-done | bytes 6553616 | tf_op jit(solution)/shard_map/all_gather | solution.py:1326
  211.4 7.3 %feed.4.refs_2_.refs_0_ = bf16[512,1024]{1,0:T(8,128)(2,1)S(1)} custom-call(bf16[512,1024]{1,0:T(8,128)(2,1)} %get-tuple-element.225.refs_0_, bf16[8,400,1024]{2,1,0:T(8,128)(2,1)S(1)} %bitcast.292), custom_call_target="tpu_custom_call" | custom-call | flops 4600000000 | tf_op jit(solution)/shard_map/feed/pallas_call | solution.py:88
  218.7 7.2 %feed.5.refs_3_ = bf16[512,1024]{1,0:T(8,128)(2,1)S(1)} custom-call(bf16[512,1024]{1,0:T(8,128)(2,1)} %collective-permute-done.29.refs_0_, bf16[8,400,1024]{2,1,0:T(8,128)(2,1)S(1)} %bitcast.293, bf16[512,1024]{1,0:T(8,128)(2,1)S(1)} %feed.4.refs_2_.refs_0_), custom_call_target="tpu_custom_call" | custom-call | flops 4600000000 | tf_op jit(solution)/shard_map/feed/pallas_call | solution.py:88
  226.0 9.8 %feed_back.4 = (bf16[512,1024]{1,0:T(8,128)(2,1)S(1)}, f32[4,1,256]{2,1,0:T(1,128)S(1)}, bf16[8,256,1024]{2,1,0:T(8,128)(2,1)S(1)}) custom-call(bf16[512,1024]{1,0:T(8,128)(2,1)} %get-tuple-element.225.refs_0_, bf16[512,1024]{1,0:T(8,128)(2,1)S(1)} %dynamic-slice_bitcast_fusion.refs_6_.refs_1_.refs_2_, bf16[8,400,1024]{2,1,0:T(8,128)(2,1)} %bitcast.287, ...), custom_call_target="tpu_custom_call" | custom-call | flops 10350000128 | tf_op jit(solution)/shard_map/feed_back/pallas_call | solution.py:88
  240.2 7.1 %feed.6.refs_2_ = bf16[512,1024]{1,0:T(8,128)(2,1)S(1)} custom-call(bf16[512,1024]{1,0:T(8,128)(2,1)} %collective-permute-done.31.refs_0_, bf16[8,400,1024]{2,1,0:T(8,128)(2,1)S(1)} %bitcast.294, bf16[512,1024]{1,0:T(8,128)(2,1)S(1)} %get-tuple-element.227.refs_2_.refs_0_), custom_call_target="tpu_custom_call" | custom-call | flops 4600000000 | tf_op jit(solution)/shard_map/feed/pallas_call | solution.py:88
  247.4 7.2 %feed.7.refs_4_ = bf16[512,1024]{1,0:T(8,128)(2,1)S(1)} custom-call(bf16[512,1024]{1,0:T(8,128)(2,1)} %collective-permute-done.30.refs_0_, bf16[8,400,1024]{2,1,0:T(8,128)(2,1)S(1)} %bitcast.295, bf16[512,1024]{1,0:T(8,128)(2,1)S(1)} %feed.6.refs_2_), custom_call_target="tpu_custom_call" | custom-call | flops 4600000000 | tf_op jit(solution)/shard_map/feed/pallas_call | solution.py:88
  259.4 9.8 %feed_back.5 = (bf16[512,1024]{1,0:T(8,128)(2,1)S(1)}, f32[4,1,256]{2,1,0:T(1,128)S(1)}, bf16[8,256,1024]{2,1,0:T(8,128)(2,1)S(1)}) custom-call(bf16[512,1024]{1,0:T(8,128)(2,1)} %collective-permute-done.29.refs_0_, bf16[512,1024]{1,0:T(8,128)(2,1)} %collective-permute-done.7.refs_7_.refs_1_, bf16[8,400,1024]{2,1,0:T(8,128)(2,1)} %bitcast.288, ...), custom_call_target="tpu_custom_call" | custom-call | flops 10350000128 | tf_op jit(solution)/shard_map/feed_back/pallas_call | solution.py:88
  273.5 9.8 %feed_back.6 = (bf16[512,1024]{1,0:T(8,128)(2,1)S(1)}, f32[4,1,256]{2,1,0:T(1,128)S(1)}, bf16[8,256,1024]{2,1,0:T(8,128)(2,1)S(1)}) custom-call(bf16[512,1024]{1,0:T(8,128)(2,1)} %collective-permute-done.31.refs_0_, bf16[512,1024]{1,0:T(8,128)(2,1)} %collective-permute-done.8.refs_8_.refs_1_, bf16[8,400,1024]{2,1,0:T(8,128)(2,1)} %bitcast.289, ...), custom_call_target="tpu_custom_call" | custom-call | flops 10350000128 | tf_op jit(solution)/shard_map/feed_back/pallas_call | solution.py:88
  288.6 9.6 %feed_back.7 = (bf16[512,1024]{1,0:T(8,128)(2,1)S(1)}, f32[4,1,256]{2,1,0:T(1,128)S(1)}, bf16[8,256,1024]{2,1,0:T(8,128)(2,1)S(1)}) custom-call(bf16[512,1024]{1,0:T(8,128)(2,1)} %collective-permute-done.30.refs_0_, bf16[512,1024]{1,0:T(8,128)(2,1)S(1)} %copy-done.42, bf16[8,400,1024]{2,1,0:T(8,128)(2,1)} %bitcast.290, ...), custom_call_target="tpu_custom_call" | custom-call | flops 10350000128 | tf_op jit(solution)/shard_map/feed_back/pallas_call | solution.py:88
  313.8 15.3 %collective-permute-done.37.refs_1_ = bf16[512,1024]{1,0:T(8,128)(2,1)} collective-permute-done((bf16[512,1024]{1,0:T(8,128)(2,1)}, bf16[512,1024]{1,0:T(8,128)(2,1)}, u32[]{:S(2)}, u32[]{:S(2)}) %collective-permute-start.37) | collective-permute-done | bytes 1048608 | tf_op jit(solution)/shard_map/ppermute | solution.py:156
  410.5 21.5 %collective-permute-done.55.refs_4_ = bf16[512,1024]{1,0:T(8,128)(2,1)S(1)} collective-permute-done((bf16[512,1024]{1,0:T(8,128)(2,1)S(1)}, bf16[512,1024]{1,0:T(8,128)(2,1)S(1)}, u32[]{:S(2)}, u32[]{:S(2)}) %collective-permute-start.55) | collective-permute-done | bytes 1048608 | tf_op jit(solution)/shard_map/ppermute | solution.py:156
  461.7 7.2 %pool_back.4 = (bf16[2,1024,128]{2,1,0:T(8,128)(2,1)S(1)}, bf16[2,1024,128]{2,1,0:T(8,128)(2,1)}, f32[768,512]{1,0:T(8,128)S(1)}, f32[2,2,816]{2,1,0:T(2,128)S(1)}, f32[2,1,128]{2,1,0:T(1,128)S(1)}) custom-call(bf16[512,816]{1,0:T(8,128)(2,1)S(1)} %copy-done.141, bf16[768,512]{1,0:T(8,128)(2,1)S(1)} %copy-done.144, ...), custom_call_target="tpu_custom_call" | custom-call | flops 24149999616 | tf_op jit(solution)/shard_map/pool_back/pallas_call | solution.py:88
  491.0 7.4 %pool_back.6 = (bf16[2,1024,128]{2,1,0:T(8,128)(2,1)S(1)}, bf16[2,1024,128]{2,1,0:T(8,128)(2,1)S(1)}, f32[768,512]{1,0:T(8,128)S(1)}, f32[2,2,816]{2,1,0:T(2,128)S(1)}, f32[2,1,128]{2,1,0:T(1,128)S(1)}) custom-call(bf16[512,816]{1,0:T(8,128)(2,1)S(1)} %copy-done.142, bf16[768,512]{1,0:T(8,128)(2,1)S(1)} %copy-done.145, bf16[512,1024]{1,0:T(8,128)(2,1)S(1)} %copy-done.154, ...), custom_call_target="tpu_custom_call" | custom-call | flops 24149999616 | tf_op jit(solution)/shard_map/pool_back/pallas_call | solution.py:88
  509.5 8.1 %pool_back.7 = (bf16[2,1024,128]{2,1,0:T(8,128)(2,1)S(1)}, bf16[2,1024,128]{2,1,0:T(8,128)(2,1)}, bf16[512,768]{1,0:T(8,128)(2,1)S(1)}, f32[2,2,816]{2,1,0:T(2,128)S(1)}, f32[2,1,128]{2,1,0:T(1,128)S(1)}) custom-call(bf16[512,816]{1,0:T(8,128)(2,1)S(1)} %copy-done.142, bf16[768,512]{1,0:T(8,128)(2,1)S(1)} %copy-done.145, bf16[512,1024]{1,0:T(8,128)(2,1)S(1)} %copy-done.154, ...), custom_call_target="tpu_custom_call" | custom-call | flops 24149999616 | tf_op jit(solution)/shard_map/pool_back/pallas_call | solution.py:88
  544.2 9.7 %collective-permute-done.71.refs_0_ = bf16[512,768]{1,0:T(8,128)(2,1)S(1)} collective-permute-done((bf16[512,768]{1,0:T(8,128)(2,1)S(1)}, bf16[512,768]{1,0:T(8,128)(2,1)S(1)}, u32[]{:S(2)}, u32[]{:S(2)}) %collective-permute-start.71) | collective-permute-done | bytes 786464 | tf_op jit(solution)/shard_map/ppermute | solution.py:156
  561.0 12.0 %collective-permute-done.93 = bf16[4,1024,128]{2,1,0:T(8,128)(2,1)S(1)} collective-permute-done((bf16[4,1024,128]{2,1,0:T(8,128)(2,1)S(1)}, bf16[4,1024,128]{2,1,0:T(8,128)(2,1)S(1)}, u32[]{:S(2)}, u32[]{:S(2)}) %collective-permute-start.93) | collective-permute-done | bytes 1048608 | tf_op jit(solution)/shard_map/ppermute | solution.py:156
  588.2 8.9 %collective-permute-done.101.refs_4_ = bf16[256,1024]{1,0:T(8,128)(2,1)S(1)} collective-permute-done((bf16[256,1024]{1,0:T(8,128)(2,1)S(1)}, bf16[256,1024]{1,0:T(8,128)(2,1)S(1)}, u32[]{:S(2)}, u32[]{:S(2)}) %collective-permute-start.101) | collective-permute-done | bytes 524320 | tf_op jit(solution)/shard_map/ppermute | solution.py:156
  604.6 14.5 %collective-permute-done.76.refs_1_ = bf16[512,768]{1,0:T(8,128)(2,1)S(1)} collective-permute-done((bf16[512,768]{1,0:T(8,128)(2,1)S(1)}, bf16[512,768]{1,0:T(8,128)(2,1)S(1)}, u32[]{:S(2)}, u32[]{:S(2)}) %collective-permute-start.76) | collective-permute-done | bytes 786464 | tf_op jit(solution)/shard_map/ppermute | solution.py:156
  640.7 10.9 %collective-permute-done.97 = bf16[2,1024,128]{2,1,0:T(8,128)(2,1)S(1)} collective-permute-done((bf16[2,1024,128]{2,1,0:T(8,128)(2,1)S(1)}, bf16[2,1024,128]{2,1,0:T(8,128)(2,1)S(1)}, u32[]{:S(2)}, u32[]{:S(2)}) %collective-permute-start.97) | collective-permute-done | bytes 524320 | tf_op jit(solution)/shard_map/ppermute | solution.py:156
  667.4 11.4 %table_back.1 = (f32[768,1024]{1,0:T(8,128)}, f32[48,1024]{1,0:T(8,128)}) custom-call(s32[8]{0:T(128)} %stack.359.refs_0_, f32[16,816]{1,0:T(8,128)} %mul.269.refs_1_, bf16[8,400,1024]{2,1,0:T(8,128)(2,1)} %bitcast.291, bf16[816,128]{1,0:T(8,128)(2,1)} %copy-done.191, bf16[816,128]{1,0:T(8,128)(2,1)} %copy-done.202, ...), custom_call_target="tpu_custom_call" | custom-call | flops 10350000128 | tf_op jit(solution)/shard_map/table_back/pallas_call | solution.py:88
  (772 shorter events, 427.3 us)
Async XLA Ops:
  7.2 201.3 %all-gather.3.cloned.1.call-start = ((), (), s32[]{:S(2)}) async-start(), calls=%async_computation | async-start | bytes 7372800 | tf_op jit(solution)/shard_map/all_gather | solution.py:1326
  35.8 41.6 %collective-permute-start.8 = (bf16[512,1024]{1,0:T(8,128)(2,1)S(1)}, bf16[512,1024]{1,0:T(8,128)(2,1)}, u32[]{:S(2)}, u32[]{:S(2)}) collective-permute-start(bf16[512,1024]{1,0:T(8,128)(2,1)S(1)} %dynamic-slice_bitcast_fusion.refs_6_.refs_1_.refs_2_), channel_id=1, source_target_pairs={{0,16},{1,17},{2,18},{3,19},{4,20},{5,21},{6,22},{7,23},{8,24},{9,... | collective-permute-start | bytes 3145736 | tf_op jit(solution)/shard_map/ppermute | solution.py:156
  115.2 41.1 %collective-permute-start.13 = (bf16[2,2,512,128]{3,2,1,0:T(8,128)(2,1)S(1)}, bf16[2,2,512,128]{3,2,1,0:T(8,128)(2,1)S(1)}, u32[]{:S(2)}, u32[]{:S(2)}) collective-permute-start(bf16[2,2,512,128]{3,2,1,0:T(8,128)(2,1)S(1)} %get-tuple-element.212.refs_1_.refs_4_), channel_id=1, source_target_pairs={{0,8},{1,9},{2,10},{3,11},{4,12},{5,13},{6,14},{7,15},{8,0},{9,1},... | collective-permute-start | bytes 1572872 | tf_op jit(solution)/shard_map/ppermute | solution.py:156
  156.8 35.1 %collective-permute-start.26 = (bf16[128,1024]{1,0:T(8,128)(2,1)S(1)}, bf16[128,1024]{1,0:T(8,128)(2,1)S(1)}, u32[]{:S(2)}, u32[]{:S(2)}) collective-permute-start(bf16[128,1024]{1,0:T(8,128)(2,1)S(1)} %get-tuple-element.221.refs_7_.refs_3_), channel_id=1, source_target_pairs={{0,8},{1,9},{2,10},{3,11},{4,12},{5,13},{6,14},{7,15},{8,0},{9,1},... | collective-permute-start | bytes 786440 | tf_op jit(solution)/shard_map/ppermute | solution.py:156
  196.9 38.9 %collective-permute-start.31 = (bf16[512,1024]{1,0:T(8,128)(2,1)}, bf16[512,1024]{1,0:T(8,128)(2,1)}, u32[]{:S(2)}, u32[]{:S(2)}) collective-permute-start(bf16[512,1024]{1,0:T(8,128)(2,1)} %get-tuple-element.225.refs_0_), channel_id=1, source_target_pairs={{0,16},{1,17},{2,18},{3,19},{4,20},{5,21},{6,22},{7,23},{8,24},{9,... | collective-permute-start | bytes 3145736 | tf_op jit(solution)/shard_map/ppermute | solution.py:156
  199.6 47.8 %collective-permute-start.30 = (bf16[512,1024]{1,0:T(8,128)(2,1)}, bf16[512,1024]{1,0:T(8,128)(2,1)}, u32[]{:S(2)}, u32[]{:S(2)}) collective-permute-start(bf16[512,1024]{1,0:T(8,128)(2,1)} %collective-permute-done.29.refs_0_), channel_id=1, source_target_pairs={{0,16},{1,17},{2,18},{3,19},{4,20},{5,21},{6,22},{7,23},{8,24},{9,... | collective-permute-start | bytes 3145736 | tf_op jit(solution)/shard_map/ppermute | solution.py:156
  308.2 39.0 %collective-permute-start.40 = (bf16[512,1024]{1,0:T(8,128)(2,1)S(1)}, bf16[512,1024]{1,0:T(8,128)(2,1)S(1)}, u32[]{:S(2)}, u32[]{:S(2)}) collective-permute-start(bf16[512,1024]{1,0:T(8,128)(2,1)S(1)} %copy-done.9), channel_id=1, source_target_pairs={{0,2},{1,0},{2,4},{3,1},{4,6},{5,3},{6,7},{7,5},{8,10},{9,8},{10,1... | collective-permute-start | bytes 3145736 | tf_op jit(solution)/shard_map/ppermute | solution.py:156
  311.1 36.1 %collective-permute-start.41 = (bf16[512,1024]{1,0:T(8,128)(2,1)S(1)}, bf16[512,1024]{1,0:T(8,128)(2,1)S(1)}, u32[]{:S(2)}, u32[]{:S(2)}) collective-permute-start(bf16[512,1024]{1,0:T(8,128)(2,1)S(1)} %copy-done.9), channel_id=1, source_target_pairs={{0,1},{1,3},{2,0},{3,5},{4,2},{5,7},{6,4},{7,6},{8,9},{9,11},{10,8... | collective-permute-start | bytes 3145736 | tf_op jit(solution)/shard_map/ppermute | solution.py:156
  311.6 35.6 %collective-permute-start.38 = (bf16[256,1024]{1,0:T(8,128)(2,1)S(1)}, bf16[256,1024]{1,0:T(8,128)(2,1)S(1)}, u32[]{:S(2)}, u32[]{:S(2)}) collective-permute-start(bf16[256,1024]{1,0:T(8,128)(2,1)S(1)} %get-tuple-element.445), channel_id=1, source_target_pairs={{0,1},{1,3},{2,0},{3,5},{4,2},{5,7},{6,4},{7,6},{8,9},{9,11},{10,8... | collective-permute-start | bytes 1572872 | tf_op jit(solution)/shard_map/ppermute | solution.py:156
  313.5 69.8 %collective-permute-start.43 = (bf16[256,1024]{1,0:T(8,128)(2,1)S(1)}, bf16[256,1024]{1,0:T(8,128)(2,1)S(1)}, u32[]{:S(2)}, u32[]{:S(2)}) collective-permute-start(bf16[256,1024]{1,0:T(8,128)(2,1)S(1)} %get-tuple-element.442), channel_id=1, source_target_pairs={{0,2},{1,0},{2,4},{3,1},{4,6},{5,3},{6,7},{7,5},{8,10},{9,8},{10,1... | collective-permute-start | bytes 1572872 | tf_op jit(solution)/shard_map/ppermute | solution.py:156
  347.4 36.0 %collective-permute-start.42 = (bf16[256,1024]{1,0:T(8,128)(2,1)S(1)}, bf16[256,1024]{1,0:T(8,128)(2,1)S(1)}, u32[]{:S(2)}, u32[]{:S(2)}) collective-permute-start(bf16[256,1024]{1,0:T(8,128)(2,1)S(1)} %get-tuple-element.248.refs_5_), channel_id=1, source_target_pairs={{0,1},{1,3},{2,0},{3,5},{4,2},{5,7},{6,4},{7,6},{8,9},{9,11},{10,8... | collective-permute-start | bytes 1572872 | tf_op jit(solution)/shard_map/ppermute | solution.py:156
  395.7 36.2 %collective-permute-start.55 = (bf16[512,1024]{1,0:T(8,128)(2,1)S(1)}, bf16[512,1024]{1,0:T(8,128)(2,1)S(1)}, u32[]{:S(2)}, u32[]{:S(2)}) collective-permute-start(bf16[512,1024]{1,0:T(8,128)(2,1)S(1)} %get-tuple-element.290), channel_id=1, source_target_pairs={{0,2},{1,0},{2,4},{3,1},{4,6},{5,3},{6,7},{7,5},{8,10},{9,8},{10,1... | collective-permute-start | bytes 3145736 | tf_op jit(solution)/shard_map/ppermute | solution.py:156
  397.3 35.2 %collective-permute-start.56 = (bf16[512,1024]{1,0:T(8,128)(2,1)S(1)}, bf16[512,1024]{1,0:T(8,128)(2,1)S(1)}, u32[]{:S(2)}, u32[]{:S(2)}) collective-permute-start(bf16[512,1024]{1,0:T(8,128)(2,1)S(1)} %get-tuple-element.291), channel_id=1, source_target_pairs={{0,1},{1,3},{2,0},{3,5},{4,2},{5,7},{6,4},{7,6},{8,9},{9,11},{10,8... | collective-permute-start | bytes 3145736 | tf_op jit(solution)/shard_map/ppermute | solution.py:156
  406.3 33.9 %collective-permute-start.51 = (bf16[2,2,512,128]{3,2,1,0:T(8,128)(2,1)S(1)}, bf16[2,2,512,128]{3,2,1,0:T(8,128)(2,1)S(1)}, u32[]{:S(2)}, u32[]{:S(2)}) collective-permute-start(bf16[2,2,512,128]{3,2,1,0:T(8,128)(2,1)S(1)} %bitcast.317), channel_id=1, source_target_pairs={{0,16},{1,17},{2,18},{3,19},{4,20},{5,21},{6,22},{7,23},{8,24},{9,... | collective-permute-start | bytes 1572872 | tf_op jit(solution)/shard_map/ppermute | solution.py:156
  409.9 36.1 %collective-permute-start.50 = (bf16[2,2,512,128]{3,2,1,0:T(8,128)(2,1)S(1)}, bf16[2,2,512,128]{3,2,1,0:T(8,128)(2,1)S(1)}, u32[]{:S(2)}, u32[]{:S(2)}) collective-permute-start(bf16[2,2,512,128]{3,2,1,0:T(8,128)(2,1)S(1)} %bitcast.319), channel_id=1, source_target_pairs={{0,16},{1,17},{2,18},{3,19},{4,20},{5,21},{6,22},{7,23},{8,24},{9,... | collective-permute-start | bytes 1572872 | tf_op jit(solution)/shard_map/ppermute | solution.py:156
  432.7 36.1 %collective-permute-start.58 = (bf16[256,1024]{1,0:T(8,128)(2,1)S(1)}, bf16[256,1024]{1,0:T(8,128)(2,1)S(1)}, u32[]{:S(2)}, u32[]{:S(2)}) collective-permute-start(bf16[256,1024]{1,0:T(8,128)(2,1)S(1)} %get-tuple-element.292.refs_8_), channel_id=1, source_target_pairs={{0,1},{1,3},{2,0},{3,5},{4,2},{5,7},{6,4},{7,6},{8,9},{9,11},{10,8... | collective-permute-start | bytes 1572872 | tf_op jit(solution)/shard_map/ppermute | solution.py:156
  434.4 34.6 %collective-permute-start.59 = (bf16[256,1024]{1,0:T(8,128)(2,1)S(1)}, bf16[256,1024]{1,0:T(8,128)(2,1)S(1)}, u32[]{:S(2)}, u32[]{:S(2)}) collective-permute-start(bf16[256,1024]{1,0:T(8,128)(2,1)S(1)} %get-tuple-element.303), channel_id=1, source_target_pairs={{0,2},{1,0},{2,4},{3,1},{4,6},{5,3},{6,7},{7,5},{8,10},{9,8},{10,1... | collective-permute-start | bytes 1572872 | tf_op jit(solution)/shard_map/ppermute | solution.py:156
  446.0 35.3 %collective-permute-start.62 = (bf16[4,1024,128]{2,1,0:T(8,128)(2,1)}, bf16[4,1024,128]{2,1,0:T(8,128)(2,1)}, u32[]{:S(2)}, u32[]{:S(2)}) collective-permute-start(bf16[4,1024,128]{2,1,0:T(8,128)(2,1)} %get-tuple-element.308), channel_id=1, source_target_pairs={{2,0},{0,1},{4,2},{1,3},{6,4},{3,5},{7,6},{5,7},{9,8},{11,9},{8,10... | collective-permute-start | bytes 3145736 | tf_op jit(solution)/shard_map/ppermute | solution.py:156
  524.5 35.1 %collective-permute-start.94 = (bf16[4,1024,128]{2,1,0:T(8,128)(2,1)S(1)}, bf16[4,1024,128]{2,1,0:T(8,128)(2,1)S(1)}, u32[]{:S(2)}, u32[]{:S(2)}) collective-permute-start(bf16[4,1024,128]{2,1,0:T(8,128)(2,1)S(1)} %copy-done.44), channel_id=1, source_target_pairs={{0,8},{1,9},{2,10},{3,11},{4,12},{5,13},{6,14},{7,15},{8,0},{9,1},... | collective-permute-start | bytes 3145736 | tf_op jit(solution)/shard_map/ppermute | solution.py:156
  535.5 37.5 %collective-permute-start.93 = (bf16[4,1024,128]{2,1,0:T(8,128)(2,1)S(1)}, bf16[4,1024,128]{2,1,0:T(8,128)(2,1)S(1)}, u32[]{:S(2)}, u32[]{:S(2)}) collective-permute-start(bf16[4,1024,128]{2,1,0:T(8,128)(2,1)S(1)} %get-tuple-element.356), channel_id=1, source_target_pairs={{2,0},{0,1},{4,2},{1,3},{6,4},{3,5},{7,6},{5,7},{9,8},{11,9},{8,10... | collective-permute-start | bytes 3145736 | tf_op jit(solution)/shard_map/ppermute | solution.py:156
  583.9 35.2 %collective-permute-start.76 = (bf16[512,768]{1,0:T(8,128)(2,1)S(1)}, bf16[512,768]{1,0:T(8,128)(2,1)S(1)}, u32[]{:S(2)}, u32[]{:S(2)}) collective-permute-start(bf16[512,768]{1,0:T(8,128)(2,1)S(1)} %get-tuple-element.329), channel_id=1, source_target_pairs={{0,1},{1,3},{2,0},{3,5},{4,2},{5,7},{6,4},{7,6},{8,9},{9,11},{10,8... | collective-permute-start | bytes 2359304 | tf_op jit(solution)/shard_map/ppermute | solution.py:156
  588.2 68.0 %collective-permute-start.87 = (bf16[816,128]{1,0:T(8,128)(2,1)S(1)}, bf16[816,128]{1,0:T(8,128)(2,1)}, u32[]{:S(2)}, u32[]{:S(2)}) collective-permute-start(bf16[816,128]{1,0:T(8,128)(2,1)S(1)} %fusion.1.refs_3_), channel_id=1, source_target_pairs={{0,2},{1,0},{2,4},{3,1},{4,6},{5,3},{6,7},{7,5},{8,9},{9,11},{10,8... | collective-permute-start | bytes 626696 | tf_op jit(solution)/shard_map/ppermute | solution.py:156
  597.1 61.5 %collective-permute-start.89 = (bf16[816,128]{1,0:T(8,128)(2,1)S(1)}, bf16[816,128]{1,0:T(8,128)(2,1)}, u32[]{:S(2)}, u32[]{:S(2)}) collective-permute-start(bf16[816,128]{1,0:T(8,128)(2,1)S(1)} %fusion.1.refs_3_), channel_id=1, source_target_pairs={{0,4},{1,2},{2,6},{3,0},{4,7},{5,1},{6,5},{7,3},{8,11},{9,13},{10,... | collective-permute-start | bytes 626696 | tf_op jit(solution)/shard_map/ppermute | solution.py:156
  601.0 57.9 %collective-permute-start.91 = (bf16[816,128]{1,0:T(8,128)(2,1)S(1)}, bf16[816,128]{1,0:T(8,128)(2,1)}, u32[]{:S(2)}, u32[]{:S(2)}) collective-permute-start(bf16[816,128]{1,0:T(8,128)(2,1)S(1)} %fusion.1.refs_3_), channel_id=1, source_target_pairs={{0,6},{1,4},{2,7},{3,2},{4,5},{5,0},{6,3},{7,1},{8,13},{9,15},{10,... | collective-permute-start | bytes 626696 | tf_op jit(solution)/shard_map/ppermute | solution.py:156
  (283 other events, 3185.4 us)
Sparse Core Ops, SparseCore 0:
  99.8 108.7 all-gather.2

commit v4 on v3

--- a/solution.py
+++ b/solution.py
@@ -325,14 +325,19 @@
 
     def send(self):
         ring, self.hops = self.ring, self.hops + 1
-        ways = [ring.forward, ring.backward] if 2 * self.hops < ring.narrow else [ring.forward]
+        if 2 * self.hops == ring.narrow:
+            half = self.moving[0].shape[0] // 2
+            self.moving = [self.moving[0][:half], self.moving[1][half:]]
+        ways = (ring.forward, ring.backward)
         self.moving = [ring.move(block, way) for block, way in zip(self.moving, ways)]
 
     def place(self):
-        for block, sign in zip(self.moving, (-1, 1)):
+        self.done = 2 * self.hops >= self.ring.narrow
+        for side, (block, sign) in enumerate(zip(self.moving, (-1, 1))):
             index = self.ring.at(sign * self.hops)
-            self.out = put(self.out, block.astype(self.dtype), index)
-        self.done = 2 * self.hops >= self.ring.narrow
+            start = side * block.shape[0] if self.done else 0
+            block = block.astype(self.dtype)[None]
+            self.out = lax.dynamic_update_slice(self.out, block, (index, start, 0))
         if not self.done:
             self.send()
 

time: 694 us -> 711 us (1.024)
  starting transfers between devices: 106 us -> 121 us
    ppermute x102 -> x104, starting transfers between devices: 106 us -> 121 us  [move(): return lax.ppermute(tensor, AXES, pairs)]
    dynamic_update_slice x0 -> x8, other arithmetic: none -> 11.4 us  [place(): self.out = lax.dynamic_update_slice(self.out, block, (index, start, 0))]
    dynamic_update_slice x9 -> x2, other arithmetic: 12.8 us -> 2.86 us  [put(): return lax.dynamic_update_index_in_dim(out, piece, index, 0)]
    ppermute x102 -> x104, waiting for transfers between devices: 188 us -> 185 us  [move(): return lax.ppermute(tensor, AXES, pairs)]
    unnamed x415 -> x399, local copies, waits for them, and re-layouts: 44.7 us -> 43.9 us
  transfers between devices with their start and end apart: 103 -> 105, of which waited for: 33 -> 35; matrix products, arithmetic and copies ran while one was open for 7% -> 7% of each run, Pallas kernels for 38% -> 37%
where the time goes in v4:
time: 711 us; the launch traced here: 703 us
  Pallas kernels  282 us (40%)
  waiting for transfers between devices  192 us (27%)
  starting transfers between devices  121 us (17%)
  local copies, waits for them, and re-layouts  65.8 us (9%)
  other arithmetic  20.6 us (3%)
  between operations  17.1 us (2%)
    pallas_call x89, Pallas kernels, call(): pl.pallas_call(body, grid_spec=pltpu.PrefetchScalarGridSpec(num_scalar_pr...  282 us
    ppermute x104, waiting for transfers between devices, move(): return lax.ppermute(tensor, AXES, pairs)  185 us
    ppermute x104, starting transfers between devices, move(): return lax.ppermute(tensor, AXES, pairs)  121 us
    unnamed x399, local copies, waits for them, and re-layouts  43.9 us
  transfers between devices with their start and end apart: 105, of which 35 were waited for; matrix products, arithmetic and copies ran while one was open for 7% of the time, Pallas kernels for 37%

profile of v4, /device:TPU:0, one launch (start us, length us, event | category | flops | bytes accessed | tf_op | source)
XLA Modules:
  0.0 703.0 jit_solution(1912349359393754605)
XLA Ops:
  22.3 14.5 %collective-permute-done.refs_3_.refs_10_.refs_1_.refs_4_.refs_6_.refs_13_ = bf16[5,1024,128]{2,1,0:T(8,128)(2,1)} collective-permute-done((bf16[5,1024,128]{2,1,0:T(8,128)(2,1)S(1)}, bf16[5,1024,128]{2,1,0:T(8,128)(2,1)}, u32[]{:S(2)}, u32[]{:S(2)}) %collective-permute-start) | collective-permute-done | bytes 1310752 | tf_op jit(solution)/shard_map/ppermute | solution.py:156
  45.9 8.9 %collective-permute-done.1.refs_3_.refs_12_.refs_1_.refs_4_.refs_6_.refs_15_ = bf16[5,1024,128]{2,1,0:T(8,128)(2,1)} collective-permute-done((bf16[5,1024,128]{2,1,0:T(8,128)(2,1)}, bf16[5,1024,128]{2,1,0:T(8,128)(2,1)}, u32[]{:S(2)}, u32[]{:S(2)}) %collective-permute-start.1) | collective-permute-done | bytes 1310752 | tf_op jit(solution)/shard_map/ppermute | solution.py:156
  63.5 9.1 %collective-permute-done.2.refs_3_.refs_14_.refs_1_.refs_4_.refs_6_.refs_17_ = bf16[5,1024,128]{2,1,0:T(8,128)(2,1)S(1)} collective-permute-done((bf16[5,1024,128]{2,1,0:T(8,128)(2,1)}, bf16[5,1024,128]{2,1,0:T(8,128)(2,1)S(1)}, u32[]{:S(2)}, u32[]{:S(2)}) %collective-permute-start.2) | collective-permute-done | bytes 1310752 | tf_op jit(solution)/shard_map/ppermute | solution.py:156
  205.8 7.2 %all-gather.3.cloned.1.call-done = bf16[3200,1024]{1,0:T(8,128)(2,1)} async-done(((bf16[400,1024]{1,0:T(8,128)(2,1)}), bf16[3200,1024]{1,0:T(8,128)(2,1)}) %all-gather.3.cloned.1.call-update) | async-done | bytes 6553616 | tf_op jit(solution)/shard_map/all_gather | solution.py:1331
  215.9 7.3 %feed.4.refs_2_.refs_0_ = bf16[512,1024]{1,0:T(8,128)(2,1)S(1)} custom-call(bf16[512,1024]{1,0:T(8,128)(2,1)} %get-tuple-element.226.refs_0_, bf16[8,400,1024]{2,1,0:T(8,128)(2,1)S(1)} %bitcast.297), custom_call_target="tpu_custom_call" | custom-call | flops 4600000000 | tf_op jit(solution)/shard_map/feed/pallas_call | solution.py:88
  223.2 7.2 %feed.5.refs_3_ = bf16[512,1024]{1,0:T(8,128)(2,1)S(1)} custom-call(bf16[512,1024]{1,0:T(8,128)(2,1)} %collective-permute-done.29.refs_0_, bf16[8,400,1024]{2,1,0:T(8,128)(2,1)S(1)} %bitcast.298, bf16[512,1024]{1,0:T(8,128)(2,1)S(1)} %feed.4.refs_2_.refs_0_), custom_call_target="tpu_custom_call" | custom-call | flops 4600000000 | tf_op jit(solution)/shard_map/feed/pallas_call | solution.py:88
  230.5 9.6 %feed_back.4 = (bf16[512,1024]{1,0:T(8,128)(2,1)S(1)}, f32[4,1,256]{2,1,0:T(1,128)S(1)}, bf16[8,256,1024]{2,1,0:T(8,128)(2,1)S(1)}) custom-call(bf16[512,1024]{1,0:T(8,128)(2,1)} %get-tuple-element.226.refs_0_, bf16[512,1024]{1,0:T(8,128)(2,1)S(1)} %dynamic-slice_bitcast_fusion.refs_6_.refs_1_.refs_2_, bf16[8,400,1024]{2,1,0:T(8,128)(2,1)} %bitcast.292, ...), custom_call_target="tpu_custom_call" | custom-call | flops 10350000128 | tf_op jit(solution)/shard_map/feed_back/pallas_call | solution.py:88
  244.5 7.1 %feed.6.refs_2_ = bf16[512,1024]{1,0:T(8,128)(2,1)S(1)} custom-call(bf16[512,1024]{1,0:T(8,128)(2,1)} %collective-permute-done.31.refs_0_, bf16[8,400,1024]{2,1,0:T(8,128)(2,1)S(1)} %bitcast.299, bf16[512,1024]{1,0:T(8,128)(2,1)S(1)} %get-tuple-element.228.refs_2_.refs_0_), custom_call_target="tpu_custom_call" | custom-call | flops 4600000000 | tf_op jit(solution)/shard_map/feed/pallas_call | solution.py:88
  251.7 7.2 %feed.7.refs_4_ = bf16[512,1024]{1,0:T(8,128)(2,1)S(1)} custom-call(bf16[512,1024]{1,0:T(8,128)(2,1)} %collective-permute-done.30.refs_0_, bf16[8,400,1024]{2,1,0:T(8,128)(2,1)S(1)} %bitcast.300, bf16[512,1024]{1,0:T(8,128)(2,1)S(1)} %feed.6.refs_2_), custom_call_target="tpu_custom_call" | custom-call | flops 4600000000 | tf_op jit(solution)/shard_map/feed/pallas_call | solution.py:88
  263.7 9.8 %feed_back.5 = (bf16[512,1024]{1,0:T(8,128)(2,1)S(1)}, f32[4,1,256]{2,1,0:T(1,128)S(1)}, bf16[8,256,1024]{2,1,0:T(8,128)(2,1)S(1)}) custom-call(bf16[512,1024]{1,0:T(8,128)(2,1)} %collective-permute-done.29.refs_0_, bf16[512,1024]{1,0:T(8,128)(2,1)} %collective-permute-done.7.refs_7_.refs_1_, bf16[8,400,1024]{2,1,0:T(8,128)(2,1)} %bitcast.293, ...), custom_call_target="tpu_custom_call" | custom-call | flops 10350000128 | tf_op jit(solution)/shard_map/feed_back/pallas_call | solution.py:88
  277.8 9.8 %feed_back.6 = (bf16[512,1024]{1,0:T(8,128)(2,1)S(1)}, f32[4,1,256]{2,1,0:T(1,128)S(1)}, bf16[8,256,1024]{2,1,0:T(8,128)(2,1)S(1)}) custom-call(bf16[512,1024]{1,0:T(8,128)(2,1)} %collective-permute-done.31.refs_0_, bf16[512,1024]{1,0:T(8,128)(2,1)} %collective-permute-done.8.refs_8_.refs_1_, bf16[8,400,1024]{2,1,0:T(8,128)(2,1)} %bitcast.294, ...), custom_call_target="tpu_custom_call" | custom-call | flops 10350000128 | tf_op jit(solution)/shard_map/feed_back/pallas_call | solution.py:88
  292.9 9.8 %feed_back.7 = (bf16[512,1024]{1,0:T(8,128)(2,1)S(1)}, f32[4,1,256]{2,1,0:T(1,128)S(1)}, bf16[8,256,1024]{2,1,0:T(8,128)(2,1)S(1)}) custom-call(bf16[512,1024]{1,0:T(8,128)(2,1)} %collective-permute-done.30.refs_0_, bf16[512,1024]{1,0:T(8,128)(2,1)S(1)} %copy-done.40, bf16[8,400,1024]{2,1,0:T(8,128)(2,1)} %bitcast.295, ...), custom_call_target="tpu_custom_call" | custom-call | flops 10350000128 | tf_op jit(solution)/shard_map/feed_back/pallas_call | solution.py:88
  320.2 15.3 %collective-permute-done.37.refs_1_ = bf16[512,1024]{1,0:T(8,128)(2,1)} collective-permute-done((bf16[512,1024]{1,0:T(8,128)(2,1)}, bf16[512,1024]{1,0:T(8,128)(2,1)}, u32[]{:S(2)}, u32[]{:S(2)}) %collective-permute-start.37) | collective-permute-done | bytes 1048608 | tf_op jit(solution)/shard_map/ppermute | solution.py:156
  417.2 21.5 %collective-permute-done.55.refs_4_ = bf16[512,1024]{1,0:T(8,128)(2,1)S(1)} collective-permute-done((bf16[512,1024]{1,0:T(8,128)(2,1)S(1)}, bf16[512,1024]{1,0:T(8,128)(2,1)S(1)}, u32[]{:S(2)}, u32[]{:S(2)}) %collective-permute-start.55) | collective-permute-done | bytes 1048608 | tf_op jit(solution)/shard_map/ppermute | solution.py:156
  476.5 7.3 %pool_back.5 = (bf16[2,1024,128]{2,1,0:T(8,128)(2,1)S(1)}, bf16[2,1024,128]{2,1,0:T(8,128)(2,1)}, f32[768,512]{1,0:T(8,128)S(1)}, f32[2,2,816]{2,1,0:T(2,128)S(1)}, f32[2,1,128]{2,1,0:T(1,128)S(1)}) custom-call(bf16[512,816]{1,0:T(8,128)(2,1)S(1)} %copy-done.137, bf16[768,512]{1,0:T(8,128)(2,1)S(1)} %copy-done.140, ...), custom_call_target="tpu_custom_call" | custom-call | flops 24149999616 | tf_op jit(solution)/shard_map/pool_back/pallas_call | solution.py:88
  494.0 7.4 %pool_back.6 = (bf16[2,1024,128]{2,1,0:T(8,128)(2,1)S(1)}, bf16[2,1024,128]{2,1,0:T(8,128)(2,1)S(1)}, f32[768,512]{1,0:T(8,128)S(1)}, f32[2,2,816]{2,1,0:T(2,128)S(1)}, f32[2,1,128]{2,1,0:T(1,128)S(1)}) custom-call(bf16[512,816]{1,0:T(8,128)(2,1)S(1)} %copy-done.138, bf16[768,512]{1,0:T(8,128)(2,1)S(1)} %copy-done.141, bf16[512,1024]{1,0:T(8,128)(2,1)S(1)} %copy-done.150, ...), custom_call_target="tpu_custom_call" | custom-call | flops 24149999616 | tf_op jit(solution)/shard_map/pool_back/pallas_call | solution.py:88
  513.5 8.1 %pool_back.7 = (bf16[2,1024,128]{2,1,0:T(8,128)(2,1)S(1)}, bf16[2,1024,128]{2,1,0:T(8,128)(2,1)}, bf16[512,768]{1,0:T(8,128)(2,1)S(1)}, f32[2,2,816]{2,1,0:T(2,128)S(1)}, f32[2,1,128]{2,1,0:T(1,128)S(1)}) custom-call(bf16[512,816]{1,0:T(8,128)(2,1)S(1)} %copy-done.138, bf16[768,512]{1,0:T(8,128)(2,1)S(1)} %copy-done.141, bf16[512,1024]{1,0:T(8,128)(2,1)S(1)} %copy-done.150, ...), custom_call_target="tpu_custom_call" | custom-call | flops 24149999616 | tf_op jit(solution)/shard_map/pool_back/pallas_call | solution.py:88
  549.2 9.7 %collective-permute-done.72.refs_0_ = bf16[512,768]{1,0:T(8,128)(2,1)S(1)} collective-permute-done((bf16[512,768]{1,0:T(8,128)(2,1)S(1)}, bf16[512,768]{1,0:T(8,128)(2,1)S(1)}, u32[]{:S(2)}, u32[]{:S(2)}) %collective-permute-start.72) | collective-permute-done | bytes 786464 | tf_op jit(solution)/shard_map/ppermute | solution.py:156
  566.0 11.8 %collective-permute-done.95 = bf16[4,1024,128]{2,1,0:T(8,128)(2,1)S(1)} collective-permute-done((bf16[4,1024,128]{2,1,0:T(8,128)(2,1)S(1)}, bf16[4,1024,128]{2,1,0:T(8,128)(2,1)S(1)}, u32[]{:S(2)}, u32[]{:S(2)}) %collective-permute-start.95) | collective-permute-done | bytes 1048608 | tf_op jit(solution)/shard_map/ppermute | solution.py:156
  596.2 7.1 %collective-permute-done.103.refs_4_ = bf16[256,1024]{1,0:T(8,128)(2,1)S(1)} collective-permute-done((bf16[256,1024]{1,0:T(8,128)(2,1)S(1)}, bf16[256,1024]{1,0:T(8,128)(2,1)S(1)}, u32[]{:S(2)}, u32[]{:S(2)}) %collective-permute-start.103) | collective-permute-done | bytes 524320 | tf_op jit(solution)/shard_map/ppermute | solution.py:156
  608.5 13.1 %collective-permute-start.98 = (bf16[2,1024,128]{2,1,0:T(8,128)(2,1)}, bf16[2,1024,128]{2,1,0:T(8,128)(2,1)S(1)}, u32[]{:S(2)}, u32[]{:S(2)}) collective-permute-start(bf16[2,1024,128]{2,1,0:T(8,128)(2,1)} %get-tuple-element.452), channel_id=1, source_target_pairs={{0,8},{1,9},{2,10},{3,11},{4,12},{5,13},{6,14},{7,15},{8,0},{9,1},... | collective-permute-start | bytes 1572872 | tf_op jit(solution)/shard_map/ppermute | solution.py:156
  648.1 11.1 %collective-permute-done.99 = bf16[2,1024,128]{2,1,0:T(8,128)(2,1)S(1)} collective-permute-done((bf16[2,1024,128]{2,1,0:T(8,128)(2,1)S(1)}, bf16[2,1024,128]{2,1,0:T(8,128)(2,1)S(1)}, u32[]{:S(2)}, u32[]{:S(2)}) %collective-permute-start.99) | collective-permute-done | bytes 524320 | tf_op jit(solution)/shard_map/ppermute | solution.py:156
  668.0 11.6 %collective-permute-done.93.refs_9_ = bf16[816,128]{1,0:T(8,128)(2,1)S(1)} collective-permute-done((bf16[816,128]{1,0:T(8,128)(2,1)S(1)}, bf16[816,128]{1,0:T(8,128)(2,1)S(1)}, u32[]{:S(2)}, u32[]{:S(2)}) %collective-permute-start.93) | collective-permute-done | bytes 208928 | tf_op jit(solution)/shard_map/ppermute | solution.py:156
  684.5 11.4 %table_back.1 = (f32[768,1024]{1,0:T(8,128)}, f32[48,1024]{1,0:T(8,128)}) custom-call(s32[8]{0:T(128)} %stack.359.refs_0_, f32[16,816]{1,0:T(8,128)} %mul.135.refs_1_, bf16[8,400,1024]{2,1,0:T(8,128)(2,1)} %bitcast.296, bf16[816,128]{1,0:T(8,128)(2,1)} %copy-done.187, bf16[816,128]{1,0:T(8,128)(2,1)} %collective-permute-done.88.refs_4_, ...), custom_call_target="tpu_custom_call" | custom-call | flops 10350000128 | tf_op jit(solution)/shard_map/table_back/pallas_call | solution.py:88
  (766 shorter events, 442.9 us)
Async XLA Ops:
  7.2 205.8 %all-gather.3.cloned.1.call-start = ((), (), s32[]{:S(2)}) async-start(), calls=%async_computation | async-start | bytes 7372800 | tf_op jit(solution)/shard_map/all_gather | solution.py:1331
  40.3 41.3 %collective-permute-start.8 = (bf16[512,1024]{1,0:T(8,128)(2,1)S(1)}, bf16[512,1024]{1,0:T(8,128)(2,1)}, u32[]{:S(2)}, u32[]{:S(2)}) collective-permute-start(bf16[512,1024]{1,0:T(8,128)(2,1)S(1)} %dynamic-slice_bitcast_fusion.refs_6_.refs_1_.refs_2_), channel_id=1, source_target_pairs={{0,16},{1,17},{2,18},{3,19},{4,20},{5,21},{6,22},{7,23},{8,24},{9,... | collective-permute-start | bytes 3145736 | tf_op jit(solution)/shard_map/ppermute | solution.py:156
  119.7 41.1 %collective-permute-start.13 = (bf16[2,2,512,128]{3,2,1,0:T(8,128)(2,1)S(1)}, bf16[2,2,512,128]{3,2,1,0:T(8,128)(2,1)S(1)}, u32[]{:S(2)}, u32[]{:S(2)}) collective-permute-start(bf16[2,2,512,128]{3,2,1,0:T(8,128)(2,1)S(1)} %get-tuple-element.213.refs_1_.refs_4_), channel_id=1, source_target_pairs={{0,8},{1,9},{2,10},{3,11},{4,12},{5,13},{6,14},{7,15},{8,0},{9,1},... | collective-permute-start | bytes 1572872 | tf_op jit(solution)/shard_map/ppermute | solution.py:156
  161.3 35.3 %collective-permute-start.26 = (bf16[128,1024]{1,0:T(8,128)(2,1)S(1)}, bf16[128,1024]{1,0:T(8,128)(2,1)S(1)}, u32[]{:S(2)}, u32[]{:S(2)}) collective-permute-start(bf16[128,1024]{1,0:T(8,128)(2,1)S(1)} %get-tuple-element.222.refs_7_.refs_3_), channel_id=1, source_target_pairs={{0,8},{1,9},{2,10},{3,11},{4,12},{5,13},{6,14},{7,15},{8,0},{9,1},... | collective-permute-start | bytes 786440 | tf_op jit(solution)/shard_map/ppermute | solution.py:156
  201.6 38.5 %collective-permute-start.31 = (bf16[512,1024]{1,0:T(8,128)(2,1)}, bf16[512,1024]{1,0:T(8,128)(2,1)}, u32[]{:S(2)}, u32[]{:S(2)}) collective-permute-start(bf16[512,1024]{1,0:T(8,128)(2,1)} %get-tuple-element.226.refs_0_), channel_id=1, source_target_pairs={{0,16},{1,17},{2,18},{3,19},{4,20},{5,21},{6,22},{7,23},{8,24},{9,... | collective-permute-start | bytes 3145736 | tf_op jit(solution)/shard_map/ppermute | solution.py:156
  204.2 47.4 %collective-permute-start.30 = (bf16[512,1024]{1,0:T(8,128)(2,1)}, bf16[512,1024]{1,0:T(8,128)(2,1)}, u32[]{:S(2)}, u32[]{:S(2)}) collective-permute-start(bf16[512,1024]{1,0:T(8,128)(2,1)} %collective-permute-done.29.refs_0_), channel_id=1, source_target_pairs={{0,16},{1,17},{2,18},{3,19},{4,20},{5,21},{6,22},{7,23},{8,24},{9,... | collective-permute-start | bytes 3145736 | tf_op jit(solution)/shard_map/ppermute | solution.py:156
  314.6 39.0 %collective-permute-start.40 = (bf16[512,1024]{1,0:T(8,128)(2,1)S(1)}, bf16[512,1024]{1,0:T(8,128)(2,1)S(1)}, u32[]{:S(2)}, u32[]{:S(2)}) collective-permute-start(bf16[512,1024]{1,0:T(8,128)(2,1)S(1)} %copy-done.7), channel_id=1, source_target_pairs={{0,2},{1,0},{2,4},{3,1},{4,6},{5,3},{6,7},{7,5},{8,10},{9,8},{10,1... | collective-permute-start | bytes 3145736 | tf_op jit(solution)/shard_map/ppermute | solution.py:156
  317.5 36.1 %collective-permute-start.41 = (bf16[512,1024]{1,0:T(8,128)(2,1)S(1)}, bf16[512,1024]{1,0:T(8,128)(2,1)S(1)}, u32[]{:S(2)}, u32[]{:S(2)}) collective-permute-start(bf16[512,1024]{1,0:T(8,128)(2,1)S(1)} %copy-done.7), channel_id=1, source_target_pairs={{0,1},{1,3},{2,0},{3,5},{4,2},{5,7},{6,4},{7,6},{8,9},{9,11},{10,8... | collective-permute-start | bytes 3145736 | tf_op jit(solution)/shard_map/ppermute | solution.py:156
  318.0 35.6 %collective-permute-start.38 = (bf16[256,1024]{1,0:T(8,128)(2,1)S(1)}, bf16[256,1024]{1,0:T(8,128)(2,1)S(1)}, u32[]{:S(2)}, u32[]{:S(2)}) collective-permute-start(bf16[256,1024]{1,0:T(8,128)(2,1)S(1)} %get-tuple-element.447), channel_id=1, source_target_pairs={{0,1},{1,3},{2,0},{3,5},{4,2},{5,7},{6,4},{7,6},{8,9},{9,11},{10,8... | collective-permute-start | bytes 1572872 | tf_op jit(solution)/shard_map/ppermute | solution.py:156
  319.9 69.8 %collective-permute-start.43 = (bf16[256,1024]{1,0:T(8,128)(2,1)S(1)}, bf16[256,1024]{1,0:T(8,128)(2,1)S(1)}, u32[]{:S(2)}, u32[]{:S(2)}) collective-permute-start(bf16[256,1024]{1,0:T(8,128)(2,1)S(1)} %get-tuple-element.444), channel_id=1, source_target_pairs={{0,2},{1,0},{2,4},{3,1},{4,6},{5,3},{6,7},{7,5},{8,10},{9,8},{10,1... | collective-permute-start | bytes 1572872 | tf_op jit(solution)/shard_map/ppermute | solution.py:156
  353.7 35.9 %collective-permute-start.42 = (bf16[256,1024]{1,0:T(8,128)(2,1)S(1)}, bf16[256,1024]{1,0:T(8,128)(2,1)S(1)}, u32[]{:S(2)}, u32[]{:S(2)}) collective-permute-start(bf16[256,1024]{1,0:T(8,128)(2,1)S(1)} %get-tuple-element.249.refs_5_), channel_id=1, source_target_pairs={{0,1},{1,3},{2,0},{3,5},{4,2},{5,7},{6,4},{7,6},{8,9},{9,11},{10,8... | collective-permute-start | bytes 1572872 | tf_op jit(solution)/shard_map/ppermute | solution.py:156
  402.4 36.3 %collective-permute-start.55 = (bf16[512,1024]{1,0:T(8,128)(2,1)S(1)}, bf16[512,1024]{1,0:T(8,128)(2,1)S(1)}, u32[]{:S(2)}, u32[]{:S(2)}) collective-permute-start(bf16[512,1024]{1,0:T(8,128)(2,1)S(1)} %get-tuple-element.291), channel_id=1, source_target_pairs={{0,2},{1,0},{2,4},{3,1},{4,6},{5,3},{6,7},{7,5},{8,10},{9,8},{10,1... | collective-permute-start | bytes 3145736 | tf_op jit(solution)/shard_map/ppermute | solution.py:156
  404.1 35.1 %collective-permute-start.56 = (bf16[512,1024]{1,0:T(8,128)(2,1)S(1)}, bf16[512,1024]{1,0:T(8,128)(2,1)S(1)}, u32[]{:S(2)}, u32[]{:S(2)}) collective-permute-start(bf16[512,1024]{1,0:T(8,128)(2,1)S(1)} %get-tuple-element.292), channel_id=1, source_target_pairs={{0,1},{1,3},{2,0},{3,5},{4,2},{5,7},{6,4},{7,6},{8,9},{9,11},{10,8... | collective-permute-start | bytes 3145736 | tf_op jit(solution)/shard_map/ppermute | solution.py:156
  416.7 34.3 %collective-permute-start.50 = (bf16[2,2,512,128]{3,2,1,0:T(8,128)(2,1)S(1)}, bf16[2,2,512,128]{3,2,1,0:T(8,128)(2,1)S(1)}, u32[]{:S(2)}, u32[]{:S(2)}) collective-permute-start(bf16[2,2,512,128]{3,2,1,0:T(8,128)(2,1)S(1)} %bitcast.323), channel_id=1, source_target_pairs={{0,16},{1,17},{2,18},{3,19},{4,20},{5,21},{6,22},{7,23},{8,24},{9,... | collective-permute-start | bytes 1572872 | tf_op jit(solution)/shard_map/ppermute | solution.py:156
  439.5 34.4 %collective-permute-start.58 = (bf16[256,1024]{1,0:T(8,128)(2,1)S(1)}, bf16[256,1024]{1,0:T(8,128)(2,1)S(1)}, u32[]{:S(2)}, u32[]{:S(2)}) collective-permute-start(bf16[256,1024]{1,0:T(8,128)(2,1)S(1)} %get-tuple-element.293.refs_8_), channel_id=1, source_target_pairs={{0,1},{1,3},{2,0},{3,5},{4,2},{5,7},{6,4},{7,6},{8,9},{9,11},{10,8... | collective-permute-start | bytes 1572872 | tf_op jit(solution)/shard_map/ppermute | solution.py:156
  441.2 32.8 %collective-permute-start.59 = (bf16[256,1024]{1,0:T(8,128)(2,1)S(1)}, bf16[256,1024]{1,0:T(8,128)(2,1)S(1)}, u32[]{:S(2)}, u32[]{:S(2)}) collective-permute-start(bf16[256,1024]{1,0:T(8,128)(2,1)S(1)} %get-tuple-element.304), channel_id=1, source_target_pairs={{0,2},{1,0},{2,4},{3,1},{4,6},{5,3},{6,7},{7,5},{8,10},{9,8},{10,1... | collective-permute-start | bytes 1572872 | tf_op jit(solution)/shard_map/ppermute | solution.py:156
  501.6 63.1 %collective-permute-start.96 = (bf16[4,1024,128]{2,1,0:T(8,128)(2,1)}, bf16[4,1024,128]{2,1,0:T(8,128)(2,1)}, u32[]{:S(2)}, u32[]{:S(2)}) collective-permute-start(bf16[4,1024,128]{2,1,0:T(8,128)(2,1)} %get-tuple-element.360), channel_id=1, source_target_pairs={{0,8},{1,9},{2,10},{3,11},{4,12},{5,13},{6,14},{7,15},{8,0},{9,1},... | collective-permute-start | bytes 3145736 | tf_op jit(solution)/shard_map/ppermute | solution.py:156
  540.6 37.3 %collective-permute-start.95 = (bf16[4,1024,128]{2,1,0:T(8,128)(2,1)S(1)}, bf16[4,1024,128]{2,1,0:T(8,128)(2,1)S(1)}, u32[]{:S(2)}, u32[]{:S(2)}) collective-permute-start(bf16[4,1024,128]{2,1,0:T(8,128)(2,1)S(1)} %get-tuple-element.358), channel_id=1, source_target_pairs={{2,0},{0,1},{4,2},{1,3},{6,4},{3,5},{7,6},{5,7},{9,8},{11,9},{8,10... | collective-permute-start | bytes 3145736 | tf_op jit(solution)/shard_map/ppermute | solution.py:156
  589.3 32.9 %collective-permute-start.77 = (bf16[512,768]{1,0:T(8,128)(2,1)S(1)}, bf16[512,768]{1,0:T(8,128)(2,1)S(1)}, u32[]{:S(2)}, u32[]{:S(2)}) collective-permute-start(bf16[512,768]{1,0:T(8,128)(2,1)S(1)} %get-tuple-element.331), channel_id=1, source_target_pairs={{0,1},{1,3},{2,0},{3,5},{4,2},{5,7},{6,4},{7,6},{8,9},{9,11},{10,8... | collective-permute-start | bytes 2359304 | tf_op jit(solution)/shard_map/ppermute | solution.py:156
  593.6 72.0 %collective-permute-start.89 = (bf16[816,128]{1,0:T(8,128)(2,1)S(1)}, bf16[816,128]{1,0:T(8,128)(2,1)}, u32[]{:S(2)}, u32[]{:S(2)}) collective-permute-start(bf16[816,128]{1,0:T(8,128)(2,1)S(1)} %fusion.1.refs_3_), channel_id=1, source_target_pairs={{0,2},{1,0},{2,4},{3,1},{4,6},{5,3},{6,7},{7,5},{8,9},{9,11},{10,8... | collective-permute-start | bytes 626696 | tf_op jit(solution)/shard_map/ppermute | solution.py:156
  603.3 64.7 %collective-permute-start.91 = (bf16[816,128]{1,0:T(8,128)(2,1)S(1)}, bf16[816,128]{1,0:T(8,128)(2,1)}, u32[]{:S(2)}, u32[]{:S(2)}) collective-permute-start(bf16[816,128]{1,0:T(8,128)(2,1)S(1)} %fusion.1.refs_3_), channel_id=1, source_target_pairs={{0,4},{1,2},{2,6},{3,0},{4,7},{5,1},{6,5},{7,3},{8,11},{9,13},{10,... | collective-permute-start | bytes 626696 | tf_op jit(solution)/shard_map/ppermute | solution.py:156
  608.5 37.8 %collective-permute-start.98 = (bf16[2,1024,128]{2,1,0:T(8,128)(2,1)}, bf16[2,1024,128]{2,1,0:T(8,128)(2,1)S(1)}, u32[]{:S(2)}, u32[]{:S(2)}) collective-permute-start(bf16[2,1024,128]{2,1,0:T(8,128)(2,1)} %get-tuple-element.452), channel_id=1, source_target_pairs={{0,8},{1,9},{2,10},{3,11},{4,12},{5,13},{6,14},{7,15},{8,0},{9,1},... | collective-permute-start | bytes 1572872 | tf_op jit(solution)/shard_map/ppermute | solution.py:156
  624.8 37.7 %collective-permute-start.81 = (bf16[256,768]{1,0:T(8,128)(2,1)}, bf16[256,768]{1,0:T(8,128)(2,1)}, u32[]{:S(2)}, u32[]{:S(2)}) collective-permute-start(bf16[256,768]{1,0:T(8,128)(2,1)} %slice.90), channel_id=1, source_target_pairs={{0,2},{1,0},{2,4},{3,1},{4,6},{5,3},{6,7},{7,5},{8,10},{9,8},{10,1... | collective-permute-start | bytes 1179656 | tf_op jit(solution)/shard_map/ppermute | solution.py:156
  636.0 43.6 %collective-permute-start.82 = (bf16[256,768]{1,0:T(8,128)(2,1)}, bf16[256,768]{1,0:T(8,128)(2,1)}, u32[]{:S(2)}, u32[]{:S(2)}) collective-permute-start(bf16[256,768]{1,0:T(8,128)(2,1)} %slice.91), channel_id=1, source_target_pairs={{0,1},{1,3},{2,0},{3,5},{4,2},{5,7},{6,4},{7,6},{8,9},{9,11},{10,8... | collective-permute-start | bytes 1179656 | tf_op jit(solution)/shard_map/ppermute | solution.py:156
  (277 other events, 3362.2 us)
Sparse Core Ops, SparseCore 0:
  104.3 108.7 all-gather.2
